TPU v7x, 32 devices: a whole 2x2x4 slice. The times are simulated.
32 devices in a mesh: occ: 2 (over x), vir: 16 (over z, y, core).
Axes of the slice: x: 2, y: 2, z: 4, core: 2. Of those that a mesh axis runs over, the one named last changes fastest.
Arguments:
- amplitudes: bfloat16 [1536, 2048], P('occ', 'vir'), may hold values from -6 to 6
- integrals: bfloat16 [2048, 40960], P('occ', 'vir'), may hold values from -0.375 to 0.375
- occ_sym: int32 [12], P('occ'), may hold values from 0 to 7, as said below
- vir_sym: int32 [320], P('vir'), may hold values from 0 to 7, as said below
- k_sym: int32 [16], replicated, may hold values from 0 to 7
Outputs:
- ladder: bfloat16 [1536, 40960], P('occ', 'vir')
Inputs may be any that keep to these rules, and one draw needn't show every extreme that they name: `occ_sym`: among the 6 blocks of one index of occ no irrep occurs more than 2 times, and one occurs exactly 2 times. `vir_sym`: among the 20 blocks of one index of vir no irrep occurs more than 5 times, and one occurs exactly 5 times.
All inputs are finite; a program needn't handle non-finite values.
Results may differ from a plain program's by a relative error of at most 0.001.
Values may be sent and summed in bfloat16 or wider, within the bound.
No kernel may reach another device: no remote copies, remote signals or barrier semaphores. Data moves between devices by JAX's collectives and lax.ppermute only.
A program may use at most 64 MiB of HBM per device.

v0:
```python
import jax
import jax.numpy as jnp
from jax import lax
from jax.sharding import PartitionSpec as P

BLK = 128


def per_device(amplitudes, integrals, occ_sym, vir_sym, k_sym):
    occ_rows = amplitudes.shape[0]
    occ_blocks = occ_rows // BLK
    kblocks = k_sym.shape[0]
    window = kblocks * BLK
    vir_blocks = vir_sym.shape[0]
    col_width = vir_blocks * BLK
    block_ids = jnp.arange(kblocks, dtype=jnp.int32)
    gathered = lax.all_gather(amplitudes, "vir", axis=1, tiled=True)
    allowed = (occ_sym[:, None] == k_sym[None, :]).astype(jnp.bfloat16)
    amp_masked = (
        gathered.reshape(occ_blocks, BLK, kblocks, BLK) * allowed[:, None, :, None]
    ).reshape(occ_rows, window)
    shard_rows = integrals.shape[0]
    own_count = shard_rows // BLK
    first_block = lax.axis_index("occ") * own_count
    own_ids = first_block + jnp.arange(own_count, dtype=jnp.int32)
    own_syms = jnp.sum(jnp.where(own_ids[:, None] == block_ids[None, :], k_sym[None, :], 0), axis=1)
    allowed_v = (own_syms[:, None] == vir_sym[None, :]).astype(jnp.bfloat16)
    masked_v = (
        integrals.reshape(own_count, BLK, vir_blocks, BLK) * allowed_v[:, None, :, None]
    ).reshape(shard_rows, col_width)
    product = jnp.dot(
        amp_masked,
        lax.all_gather(masked_v, "occ", axis=0, tiled=True),
        preferred_element_type=jnp.float32,
    )
    summed = product.reshape(occ_rows, vir_blocks, BLK)
    return summed.reshape(occ_rows, col_width).astype(jnp.bfloat16)


def solution(mesh):
    return jax.shard_map(
        per_device,
        mesh=mesh,
        in_specs=(P("occ", "vir"), P("occ", "vir"), P("occ"), P("vir"), P()),
        out_specs=P("occ", "vir"),
        check_vma=False,
    )
```

profile of v0, /device:TPU:0, one launch (start us, length us, event | category | flops | bytes accessed | tf_op | source)
XLA Modules:
  0.0 209.5 jit_solution(2373978537652658381)
XLA Ops:
  6.5 0.0 all-gather.3.cloned.1.call-start
  6.5 0.7 all-gather.3.cloned.1.call-update
  7.3 0.0 all-gather.5.cloned.1.call-start
  7.3 0.0 copy-start.2
  7.3 0.0 copy-start.1
  7.3 8.0 %copy.7 = bf16[1024,2560]{0,1:T(8,128)(2,1)} copy(bf16[1024,2560]{1,0:T(8,128)(2,1)} %param.6) | data formatting | bytes 10485760 | tf_op args[1]
  15.3 0.0 copy-start
  15.3 0.0 copy-done.2
  15.3 0.2 select_reduce_fusion
  15.5 0.0 copy-done.1
  15.5 0.1 compare_convert_fusion
  15.5 0.7 mul.29
  16.3 1.5 copy-done
  17.8 3.0 %bitcast_multiply_fusion = bf16[1024,2560]{0,1:T(8,128)(2,1)} fusion(bf16[1024,2560]{0,1:T(8,128)(2,1)S(1)} %copy-done, bf16[320,8,8,128]{3,2,1,0:T(8,128)(2,1)S(1)} %bitcast.12), kind=kLoop, calls=%fused_computation | loop fusion | flops 2621440 | bytes 15728640 | tf_op jit(solution)/shard_map/mul | solution.py:29
  20.8 0.0 copy-start.3
  20.8 0.0 all-gather.5.cloned.1.call-update
  20.8 0.6 copy-done.3
  21.5 0.1 compare_convert_fusion.1
  21.5 37.9 %all-gather.3.cloned.1.call-done = bf16[768,2048]{1,0:T(8,128)(2,1)} async-done(((bf16[768,128]{1,0:T(8,128)(2,1)}), bf16[768,2048]{1,0:T(8,128)(2,1)}) %all-gather.3.cloned.1.call-update) | async-done | bytes 3145744 | tf_op jit(solution)/shard_map/all_gather | solution.py:17
  59.5 129.3 %all-gather.5.cloned.1.call-done = bf16[2048,2560]{0,1:T(8,128)(2,1)} async-done(((bf16[1024,2560]{0,1:T(8,128)(2,1)}), bf16[2048,2560]{0,1:T(8,128)(2,1)}) %all-gather.5.cloned.1.call-update) | async-done | bytes 10485776 | tf_op jit(solution)/shard_map/all_gather | solution.py:33
  188.7 0.5 mul.25
  189.2 13.4 %convolution_convert_fusion = bf16[768,2560]{1,0:T(8,128)(2,1)} fusion(bf16[2048,2560]{0,1:T(8,128)(2,1)} %all-gather.5.cloned.1.call-done, bf16[768,2048]{1,0:T(8,128)(2,1)} %all-gather.3.cloned.1.call-done, bf16[96,8,16,128]{3,2,1,0:T(8,128)(2,1)S(1)} %bitcast.13), kind=kOutput, calls=%fused_computation.1 | convolution fusion | flops 8056602624 | bytes 20709376 | tf_op jit(solution)/shard_map/dot_general | solution.py:31
  (1 shorter events, 0.0 us)
Async XLA Ops:
  6.5 52.9 %all-gather.3.cloned.1.call-start = ((), (), s32[]{:S(2)}) async-start(), calls=%async_computation | async-start | bytes 3342336 | tf_op jit(solution)/shard_map/all_gather | solution.py:17
  7.3 181.5 %all-gather.5.cloned.1.call-start = ((), (), s32[]{:S(2)}) async-start(), calls=%async_computation.1 | async-start | bytes 15728640 | tf_op jit(solution)/shard_map/all_gather | solution.py:33
  7.3 8.0 %copy-start.2 = (s32[16]{0:T(128)S(1)}, s32[16]{0:T(128)}, u32[]{:S(2)}) copy-start(s32[16]{0:T(128)} %param.9) | copy-start | bytes 196
  7.3 8.2 %copy-start.1 = (s32[20]{0:T(128)S(1)}, s32[20]{0:T(128)}, u32[]{:S(2)}) copy-start(s32[20]{0:T(128)} %param.8) | copy-start | bytes 244
  15.3 2.5 %copy-start = (bf16[1024,2560]{0,1:T(8,128)(2,1)S(1)}, bf16[1024,2560]{0,1:T(8,128)(2,1)}, u32[]{:S(2)}) copy-start(bf16[1024,2560]{0,1:T(8,128)(2,1)} %copy.7) | copy-start | bytes 15728644
  20.8 0.7 copy-start.3
Sparse Core Ops, SparseCore 0:
  9.5 49.8 all-gather.2
  61.0 127.6 all-gather.4
where the time goes:
time: 210 us; the launch traced here: 209 us
  waiting for transfers between devices  168 us (80%)
  matrix products  13.4 us (6%)
  between operations  13.4 us (6%)
  local copies, waits for them, and re-layouts  11.3 us (5%)
  other arithmetic  3.38 us (2%)
    all_gather x1, waiting for transfers between devices, per_device(): lax.all_gather(masked_v, 'occ', axis=0, tiled=True)  129 us
    all_gather x1, waiting for transfers between devices, per_device(): gathered = lax.all_gather(amplitudes, 'vir', axis=1, tiled=True)  37.9 us
    dot_general x1, matrix products, per_device(): jnp.dot(amp_masked, lax.all_gather(masked_v, 'occ', axis=0, tiled=True),...  13.4 us
    unnamed x9, local copies, waits for them, and re-layouts  10.1 us
  transfers between devices with their start and end apart: 2, of which 2 were waited for; matrix products, arithmetic and copies ran while one was open for 6% of the time, Pallas kernels for 0%

commit v1 on v0

v1 whole, which is shorter than its diff:
```python
import functools

import jax
import jax.numpy as jnp
from jax import lax
from jax.experimental import pallas as pl
from jax.experimental.pallas import tpu as pltpu
from jax.sharding import PartitionSpec as P

BLK = 128
IRREPS = 8
MAXO = 2
MAXB = 5
INFO = 16

CNT = 0
VBL = CNT + IRREPS
SLOT = VBL + IRREPS * MAXB
OFF = SLOT + IRREPS * MAXO

SMEM = pl.BlockSpec(memory_space=pltpu.SMEM)
VMEM = pl.BlockSpec(memory_space=pltpu.VMEM)
ANY = pl.BlockSpec(memory_space=pl.ANY)
HBM = pl.BlockSpec(memory_space=pltpu.HBM)


def prep_kernel(
    n_occ, first_cap, ksym, vsym, osym, v_ref, a_ref, head, rest, pay, tab, sems
):
    kblocks, vblocks, oblocks = ksym.shape[0], vsym.shape[0], osym.shape[0]
    own = kblocks // n_occ
    first = lax.axis_index("occ") * own
    width = a_ref.shape[1]

    for s in range(IRREPS):
        tab[CNT + s] = 0
        for slot in range(MAXO):
            tab[SLOT + s * MAXO + slot] = -1

    @pl.loop(0, vblocks)
    def _(vb):
        s = vsym[vb]
        rank = tab[CNT + s]
        tab[VBL + s * MAXB + rank] = vb
        tab[CNT + s] = rank + 1

    most = jnp.int32(0)
    for half in range(n_occ):
        total = jnp.int32(0)
        for kb in range(half * own, (half + 1) * own):
            tab[OFF + kb] = total
            total = total + tab[CNT + ksym[kb]]
        most = jnp.maximum(most, total)

    def pieces(act):
        @pl.loop(0, own)
        def _(kb):
            s = ksym[first + kb]
            place0 = tab[OFF + first + kb]
            for j in range(MAXB):
                @pl.when(j < tab[CNT + s])
                def _():
                    place = place0 + j
                    src = v_ref.at[
                        pl.ds(pl.multiple_of(kb * BLK, BLK), BLK),
                        pl.ds(pl.multiple_of(tab[VBL + s * MAXB + j] * BLK, BLK), BLK),
                    ]

                    @pl.when(place < first_cap)
                    def _():
                        act(pltpu.make_async_copy(src, head.at[place], sems.at[place]))

                    @pl.when(place >= first_cap)
                    def _():
                        act(
                            pltpu.make_async_copy(
                                src, rest.at[place - first_cap], sems.at[place]
                            )
                        )

    pieces(lambda copy: copy.start())

    for ob in range(oblocks):
        s = osym[ob]
        used = (tab[SLOT + s * MAXO] >= 0).astype(jnp.int32)
        tab[SLOT + s * MAXO + used] = ob
    vir = lax.axis_index("vir")
    step = min(width, BLK)
    for q in range(width // step):
        s = ksym[(vir * width + q * step) // BLK]
        cols = slice(q * step, (q + 1) * step)
        for slot in range(MAXO):
            ob = tab[SLOT + s * MAXO + slot]
            rows = pl.ds(pl.multiple_of(jnp.maximum(ob, 0) * BLK, BLK), BLK)
            block = a_ref[rows, cols]
            pay[slot * BLK : (slot + 1) * BLK, cols] = jnp.where(
                ob >= 0, block, jnp.zeros_like(block)
            )
    pay[MAXO * BLK :, :] = jnp.full(
        (INFO, width), most.astype(jnp.float32), jnp.float32
    ).astype(jnp.bfloat16)

    pieces(lambda copy: copy.wait())


def add_half(first, own, ksym, tab, amp, read, acc, spare):
    @pl.loop(0, own)
    def _(i):
        kb = first + i
        s = ksym[kb]
        count = tab[CNT + s]
        place = tab[OFF + kb]

        @pl.when((tab[SLOT + s * MAXO] >= 0) & (count > 0))
        def _():
            left = amp[kb, : MAXO * BLK, :]
            for j in range(MAXB):
                there = j < count
                right = read(jnp.where(there, place + j, place))
                vb = jnp.where(there, tab[VBL + s * MAXB + j], spare)
                acc[vb] += jnp.dot(left, right, preferred_element_type=jnp.float32)


def own_kernel(masks, n_occ, first_cap, ksym, tab, *refs):
    n = len(masks) if masks else 1
    parts, (head, rest, acc, amp, zero_out, most, zeros, sems, zsems) = refs[:n], refs[n:]
    kblocks = ksym.shape[0]
    own = kblocks // n_occ
    vblocks = acc.shape[0] - 1
    me = lax.axis_index("vir")

    def gather(act):
        if not masks:
            act(pltpu.make_async_copy(parts[0], amp, sems.at[0]))
            return
        for i, (mask, part) in enumerate(zip(masks, parts)):
            act(pltpu.make_async_copy(part, amp.at[me ^ mask], sems.at[i]))

    gather(lambda copy: copy.start())
    zeros[...] = jnp.zeros_like(zeros)
    strips = zero_out.shape[0] // BLK

    def fill(act):
        for i in range(strips):
            act(
                pltpu.make_async_copy(
                    zeros, zero_out.at[pl.ds(i * BLK, BLK)], zsems.at[i]
                )
            )

    fill(lambda copy: copy.start())

    @pl.loop(0, vblocks)
    def _(vb):
        acc[vb] = jnp.zeros_like(acc[vb])

    gather(lambda copy: copy.wait())
    info = amp[:, MAXO * BLK : MAXO * BLK + INFO, :].astype(jnp.float32)
    most[0] = jnp.max(info).astype(jnp.int32)

    def read(place):
        return lax.cond(
            place < first_cap,
            lambda: head[jnp.minimum(place, first_cap - 1)],
            lambda: rest[jnp.maximum(place - first_cap, 0)],
        )

    add_half(
        lax.axis_index("occ") * own, own, ksym, tab, amp, read, acc, vblocks
    )
    fill(lambda copy: copy.wait())


def last_kernel(shifts, n_occ, first_cap, ksym, tab, amp, start, *refs):
    n = len(shifts)
    heads = refs[:n]
    rests = refs[n : 2 * n]
    _, out, acc, stage, sems = refs[-5:]
    kblocks = ksym.shape[0]
    own = kblocks // n_occ
    vblocks = acc.shape[0] - 1
    me = lax.axis_index("occ")

    @pl.loop(0, vblocks)
    def _(vb):
        acc[vb] = start[vb]

    for shift, head, rest in zip(shifts, heads, rests):
        source = lax.rem(me - shift + n_occ, n_occ)

        def read(place):
            return lax.cond(
                place < first_cap,
                lambda: head[jnp.minimum(place, first_cap - 1)],
                lambda: rest[jnp.maximum(place - first_cap, 0)],
            )

        add_half(source * own, own, ksym, tab, amp, read, acc, vblocks)

    def blocks(act):
        @pl.loop(0, IRREPS)
        def _(s):
            for slot in range(MAXO):
                ob = tab[SLOT + s * MAXO + slot]
                for j in range(MAXB):
                    @pl.when((ob >= 0) & (j < tab[CNT + s]))
                    def _():
                        act(ob, slot, tab[VBL + s * MAXB + j])

    def send(ob, slot, vb):
        return pltpu.make_async_copy(
            stage.at[vb, pl.ds(slot * BLK, BLK)],
            out.at[
                pl.ds(pl.multiple_of(ob * BLK, BLK), BLK),
                pl.ds(pl.multiple_of(vb * BLK, BLK), BLK),
            ],
            sems.at[vb, slot],
        )

    def store(ob, slot, vb):
        rows = slice(slot * BLK, (slot + 1) * BLK)
        stage[vb, rows, :] = acc[vb, rows, :].astype(jnp.bfloat16)
        send(ob, slot, vb).start()

    blocks(store)
    blocks(lambda ob, slot, vb: send(ob, slot, vb).wait())


def per_device(n_occ, n_vir, amplitudes, integrals, occ_sym, vir_sym, k_sym):
    occ_rows, width = amplitudes.shape
    kblocks = k_sym.shape[0]
    own = kblocks // n_occ
    vblocks = vir_sym.shape[0]
    cols = vblocks * BLK
    cap = own * MAXB
    first_cap = (cap * 3 + 3) // 4
    rows = MAXO * BLK + INFO
    bf16, f32, i32 = jnp.bfloat16, jnp.float32, jnp.int32

    head, rest, pay, tab = pl.pallas_call(
        functools.partial(prep_kernel, n_occ, first_cap),
        out_shape=(
            jax.ShapeDtypeStruct((first_cap, BLK, BLK), bf16),
            jax.ShapeDtypeStruct((cap - first_cap, BLK, BLK), bf16),
            jax.ShapeDtypeStruct((rows, width), bf16),
            jax.ShapeDtypeStruct((OFF + kblocks,), i32),
        ),
        in_specs=[SMEM, SMEM, SMEM, ANY, VMEM],
        out_specs=(VMEM, VMEM, VMEM, SMEM),
        scratch_shapes=[pltpu.SemaphoreType.DMA((cap,))],
        name="pack",
    )(k_sym, vir_sym, occ_sym, integrals, amplitudes)

    shifts = tuple(range(1, n_occ))

    def across(x, shift):
        return lax.ppermute(x, "occ", [(i, (i + shift) % n_occ) for i in range(n_occ)])

    heads = [across(head, shift) for shift in shifts]

    bits = [1 << b for b in range(n_vir.bit_length() - 1)]
    bits = bits[::-1]
    if width == BLK:
        parts, masks = [pay], [0]
        for bit in bits:
            pairs = [(i, i ^ bit) for i in range(n_vir)]
            parts = parts + [lax.ppermute(p, "vir", pairs) for p in parts]
            masks = masks + [m ^ bit for m in masks]
    else:
        whole, masks = pay[None], [0]
        for bit in bits:
            pairs = [(i, i ^ bit) for i in range(n_vir)]
            whole = jnp.concatenate([whole, lax.ppermute(whole, "vir", pairs)])
            masks = masks + [m ^ bit for m in masks]
        place = [masks.index(m) for m in range(n_vir)]
        order = jnp.asarray(place, i32)[
            jnp.arange(n_vir, dtype=i32) ^ lax.axis_index("vir").astype(i32)
        ]
        whole = whole[order].transpose(1, 0, 2).reshape(rows, kblocks, BLK)
        whole = whole.transpose(1, 0, 2)
        parts, masks = [whole], []
    acc, amp, zero_out, most = own_call(
        parts, masks, n_occ, first_cap, k_sym, tab, head, rest, kblocks, rows, vblocks,
        occ_rows, cols,
    )

    rests = lax.cond(
        most[0] > first_cap,
        lambda x: [across(x, shift) for shift in shifts],
        lambda x: [x for _ in shifts],
        rest,
    )
    return pl.pallas_call(
        functools.partial(last_kernel, shifts, n_occ, first_cap),
        out_shape=jax.ShapeDtypeStruct((occ_rows, cols), bf16),
        in_specs=[SMEM, SMEM] + [VMEM] * (2 + 2 * len(shifts)) + [HBM],
        out_specs=HBM,
        scratch_shapes=[
            pltpu.VMEM((vblocks + 1, MAXO * BLK, BLK), f32),
            pltpu.VMEM((vblocks, MAXO * BLK, BLK), bf16),
            pltpu.SemaphoreType.DMA((vblocks, MAXO)),
        ],
        input_output_aliases={4 + 2 * len(shifts): 0},
        compiler_params=pltpu.CompilerParams(vmem_limit_bytes=24 * 2**20),
        name="finish",
    )(k_sym, tab, amp, acc, *heads, *rests, zero_out)


def own_call(
    parts, masks, n_occ, first_cap, k_sym, tab, head, rest, kblocks, rows, vblocks,
    occ_rows, cols,
):
    bf16, f32, i32 = jnp.bfloat16, jnp.float32, jnp.int32
    return pl.pallas_call(
        functools.partial(own_kernel, tuple(masks), n_occ, first_cap),
        out_shape=(
            jax.ShapeDtypeStruct((vblocks + 1, MAXO * BLK, BLK), f32),
            jax.ShapeDtypeStruct((kblocks, rows, BLK), bf16),
            jax.ShapeDtypeStruct((occ_rows, cols), bf16),
            jax.ShapeDtypeStruct((1,), i32),
        ),
        in_specs=[SMEM, SMEM] + [ANY] * len(parts) + [VMEM, VMEM],
        out_specs=(VMEM, VMEM, HBM, SMEM),
        scratch_shapes=[
            pltpu.VMEM((BLK, cols), bf16),
            pltpu.SemaphoreType.DMA((len(parts),)),
            pltpu.SemaphoreType.DMA((occ_rows // BLK,)),
        ],
        compiler_params=pltpu.CompilerParams(vmem_limit_bytes=24 * 2**20),
        name="own_half",
    )(k_sym, tab, *parts, head, rest)


def solution(mesh):
    return jax.shard_map(
        functools.partial(per_device, mesh.shape["occ"], mesh.shape["vir"]),
        mesh=mesh,
        in_specs=(P("occ", "vir"), P("occ", "vir"), P("occ"), P("vir"), P()),
        out_specs=P("occ", "vir"),
        check_vma=False,
    )
```

time: 210 us -> 42.9 us (0.20)
  waiting for transfers between devices: 168 us -> 9.57 us
  Pallas kernels: 0 us -> 14.2 us
  matrix products: 13.4 us -> 0 us
  between operations: 13.4 us -> 0.66 us
  starting transfers between devices: 0.04 us -> 12.5 us
  local copies, waits for them, and re-layouts: 11.3 us -> 5.58 us
  other arithmetic: 3.38 us -> 0 us
    all_gather x2 -> x0, waiting for transfers between devices: 167 us -> none  [the longest x1 129 us: per_device(): lax.all_gather(masked_v, 'occ', axis=0, tiled=True)]
    pallas_call x0 -> x3, Pallas kernels: none -> 14.2 us  [the longest x1 5.55 us: per_device(): pl.pallas_call(functools.partial(last_kernel, shifts, n_occ, first_cap),...]
    dot_general x1 -> x0, matrix products: 13.4 us -> none  [per_device(): jnp.dot(amp_masked, lax.all_gather(masked_v, 'occ', axis=0, tiled=True),...]
    ppermute x0 -> x16, starting transfers between devices: none -> 12.5 us  [the longest x15 9.51 us: per_device(): parts = parts + [lax.ppermute(p, 'vir', pairs) for p in parts]]
    ppermute x0 -> x16, waiting for transfers between devices: none -> 9.57 us  [the longest x15 9.56 us: per_device(): parts = parts + [lax.ppermute(p, 'vir', pairs) for p in parts]]
    unnamed x9 -> x14, local copies, waits for them, and re-layouts: 10.1 us -> 5.58 us
    mul x1 -> x0, other arithmetic: 3.04 us -> none  [per_device(): integrals.reshape(own_count, BLK, vir_blocks, BLK)]
  transfers between devices with their start and end apart: 2 -> 16, of which waited for: 2 -> 7; matrix products, arithmetic and copies ran while one was open for 6% -> 0% of each run, Pallas kernels for 0% -> 11%
where the time goes in v1:
time: 42.9 us; the launch traced here: 42.5 us
  Pallas kernels  14.2 us (33%)
  starting transfers between devices  12.5 us (29%)
  waiting for transfers between devices  9.57 us (22%)
  local copies, waits for them, and re-layouts  5.58 us (13%)
  between operations  0.66 us (2%)
    ppermute x15, waiting for transfers between devices, per_device(): parts = parts + [lax.ppermute(p, 'vir', pairs) for p in parts]  9.56 us
    ppermute x15, starting transfers between devices, per_device(): parts = parts + [lax.ppermute(p, 'vir', pairs) for p in parts]  9.51 us
    unnamed x14, local copies, waits for them, and re-layouts  5.58 us
    pallas_call x1, Pallas kernels, per_device(): pl.pallas_call(functools.partial(last_kernel, shifts, n_occ, first_cap),...  5.55 us
    pallas_call x1, Pallas kernels, own_call(): pl.pallas_call(functools.partial(own_kernel, tuple(masks), n_occ, first_c...  4.77 us
    pallas_call x1, Pallas kernels, per_device(): pl.pallas_call(functools.partial(prep_kernel, n_occ, first_cap), out_shap...  3.88 us
    ppermute x1, starting transfers between devices, across(): lax.ppermute(x, 'occ', [(i, (i + shift) % n_occ) for i in range(n_occ)])  2.99 us
  transfers between devices with their start and end apart: 16, of which 7 were waited for; matrix products, arithmetic and copies ran while one was open for 0% of the time, Pallas kernels for 11%

profile of v1, /device:TPU:0, one launch (start us, length us, event | category | flops | bytes accessed | tf_op | source)
XLA Modules:
  0.0 42.5 jit_solution(10332205775762601736)
XLA Ops:
  0.0 3.9 %pack.1 = (bf16[30,128,128]{2,1,0:T(8,128)(2,1)}, bf16[10,128,128]{2,1,0:T(8,128)(2,1)S(1)}, bf16[272,128]{1,0:T(8,128)(2,1)}, s32[80]{0:T(128)}) custom-call(s32[16]{0:T(128)} %ksym.5, s32[20]{0:T(128)} %vsym.1, s32[6]{0:T(128)} %osym.1, bf16[1024,2560]{1,0:T(8,128)(2,1)} %v_ref.1, bf16[768,128]{1,0:T(8,128)(2,1)} %a_ref.1), custom_call_target="tpu_custom_call" | custom-call | tf_op jit(solution)/shard_map/pack/pallas_call | solution.py:240
  3.9 3.0 %collective-permute-start.16 = (bf16[30,128,128]{2,1,0:T(8,128)(2,1)}, bf16[30,128,128]{2,1,0:T(8,128)(2,1)}, u32[]{:S(2)}, u32[]{:S(2)}) collective-permute-start(bf16[30,128,128]{2,1,0:T(8,128)(2,1)} %get-tuple-element.20.refs_16_), channel_id=1, source_target_pairs={{0,16},{16,0},{1,17},{17,1},{2,18},{18,2},{3,19},{19,3},{4,20},{20... | collective-permute-start | bytes 2949128 | tf_op jit(solution)/shard_map/ppermute | solution.py:257
  6.9 1.5 %collective-permute-start.4 = (bf16[272,128]{1,0:T(8,128)(2,1)}, bf16[272,128]{1,0:T(8,128)(2,1)S(1)}, u32[]{:S(2)}, u32[]{:S(2)}) collective-permute-start(bf16[272,128]{1,0:T(8,128)(2,1)} %get-tuple-element.19.refs_0_), channel_id=1, source_target_pairs={{0,2},{1,3},{2,0},{3,1},{4,6},{5,7},{6,4},{7,5},{8,10},{9,11},{10,... | collective-permute-start | bytes 208904 | tf_op jit(solution)/shard_map/ppermute | solution.py:267
  8.3 1.6 %collective-permute-start.2 = (bf16[272,128]{1,0:T(8,128)(2,1)}, bf16[272,128]{1,0:T(8,128)(2,1)S(1)}, u32[]{:S(2)}, u32[]{:S(2)}) collective-permute-start(bf16[272,128]{1,0:T(8,128)(2,1)} %get-tuple-element.19.refs_0_), channel_id=1, source_target_pairs={{0,4},{1,5},{2,6},{3,7},{4,0},{5,1},{6,2},{7,3},{8,12},{9,13},{10,... | collective-permute-start | bytes 208904 | tf_op jit(solution)/shard_map/ppermute | solution.py:267
  9.9 2.6 %collective-permute-start.1 = (bf16[272,128]{1,0:T(8,128)(2,1)}, bf16[272,128]{1,0:T(8,128)(2,1)S(1)}, u32[]{:S(2)}, u32[]{:S(2)}) collective-permute-start(bf16[272,128]{1,0:T(8,128)(2,1)} %get-tuple-element.19.refs_0_), channel_id=1, source_target_pairs={{0,8},{1,9},{2,10},{3,11},{4,12},{5,13},{6,14},{7,15},{8,0},{9,1},... | collective-permute-start | bytes 208904 | tf_op jit(solution)/shard_map/ppermute | solution.py:267
  12.6 0.5 %collective-permute-start.12 = (bf16[272,128]{1,0:T(8,128)(2,1)S(1)}, bf16[272,128]{1,0:T(8,128)(2,1)S(1)}, u32[]{:S(2)}, u32[]{:S(2)}) collective-permute-start(bf16[272,128]{1,0:T(8,128)(2,1)S(1)} %collective-permute-done.4.refs_4_), channel_id=1, source_target_pairs={{0,1},{1,0},{2,3},{3,2},{4,5},{5,4},{6,7},{7,6},{8,9},{9,8},{10,11... | collective-permute-start | bytes 208904 | tf_op jit(solution)/shard_map/ppermute | solution.py:267
  13.1 0.5 %collective-permute-done.2.refs_2_ = bf16[272,128]{1,0:T(8,128)(2,1)S(1)} collective-permute-done((bf16[272,128]{1,0:T(8,128)(2,1)}, bf16[272,128]{1,0:T(8,128)(2,1)S(1)}, u32[]{:S(2)}, u32[]{:S(2)}) %collective-permute-start.2) | collective-permute-done | bytes 69664 | tf_op jit(solution)/shard_map/ppermute | solution.py:267
  13.6 0.0 collective-permute-start.10
  13.6 2.5 %collective-permute-done.1.refs_1_ = bf16[272,128]{1,0:T(8,128)(2,1)S(1)} collective-permute-done((bf16[272,128]{1,0:T(8,128)(2,1)}, bf16[272,128]{1,0:T(8,128)(2,1)S(1)}, u32[]{:S(2)}, u32[]{:S(2)}) %collective-permute-start.1) | collective-permute-done | bytes 69664 | tf_op jit(solution)/shard_map/ppermute | solution.py:267
  16.1 0.2 collective-permute-start.3
  16.3 0.0 collective-permute-done.8.refs_8_
  16.3 0.5 %collective-permute-start.6 = (bf16[272,128]{1,0:T(8,128)(2,1)S(1)}, bf16[272,128]{1,0:T(8,128)(2,1)S(1)}, u32[]{:S(2)}, u32[]{:S(2)}) collective-permute-start(bf16[272,128]{1,0:T(8,128)(2,1)S(1)} %collective-permute-done.2.refs_2_), channel_id=1, source_target_pairs={{0,2},{1,3},{2,0},{3,1},{4,6},{5,7},{6,4},{7,5},{8,10},{9,11},{10,... | collective-permute-start | bytes 208904 | tf_op jit(solution)/shard_map/ppermute | solution.py:267
  16.8 0.0 collective-permute-done.12.refs_12_
  16.8 0.0 collective-permute-start.9
  16.8 1.6 %collective-permute-start.5 = (bf16[272,128]{1,0:T(8,128)(2,1)S(1)}, bf16[272,128]{1,0:T(8,128)(2,1)S(1)}, u32[]{:S(2)}, u32[]{:S(2)}) collective-permute-start(bf16[272,128]{1,0:T(8,128)(2,1)S(1)} %collective-permute-done.1.refs_1_), channel_id=1, source_target_pairs={{0,2},{1,3},{2,0},{3,1},{4,6},{5,7},{6,4},{7,5},{8,10},{9,11},{10,... | collective-permute-start | bytes 208904 | tf_op jit(solution)/shard_map/ppermute | solution.py:267
  18.4 2.0 %collective-permute-done.3.refs_3_ = bf16[272,128]{1,0:T(8,128)(2,1)S(1)} collective-permute-done((bf16[272,128]{1,0:T(8,128)(2,1)S(1)}, bf16[272,128]{1,0:T(8,128)(2,1)S(1)}, u32[]{:S(2)}, u32[]{:S(2)}) %collective-permute-start.3) | collective-permute-done | bytes 69664 | tf_op jit(solution)/shard_map/ppermute | solution.py:267
  20.4 0.5 %collective-permute-start.7 = (bf16[272,128]{1,0:T(8,128)(2,1)S(1)}, bf16[272,128]{1,0:T(8,128)(2,1)S(1)}, u32[]{:S(2)}, u32[]{:S(2)}) collective-permute-start(bf16[272,128]{1,0:T(8,128)(2,1)S(1)} %collective-permute-done.3.refs_3_), channel_id=1, source_target_pairs={{0,2},{1,3},{2,0},{3,1},{4,6},{5,7},{6,4},{7,5},{8,10},{9,11},{10,... | collective-permute-start | bytes 208904 | tf_op jit(solution)/shard_map/ppermute | solution.py:267
  20.9 0.4 %collective-permute-done.6.refs_6_ = bf16[272,128]{1,0:T(8,128)(2,1)S(1)} collective-permute-done((bf16[272,128]{1,0:T(8,128)(2,1)S(1)}, bf16[272,128]{1,0:T(8,128)(2,1)S(1)}, u32[]{:S(2)}, u32[]{:S(2)}) %collective-permute-start.6) | collective-permute-done | bytes 69664 | tf_op jit(solution)/shard_map/ppermute | solution.py:267
  21.3 0.0 collective-permute-start.11
  21.3 0.0 collective-permute-done.9.refs_9_
  21.3 0.5 %collective-permute-start.14 = (bf16[272,128]{1,0:T(8,128)(2,1)S(1)}, bf16[272,128]{1,0:T(8,128)(2,1)S(1)}, u32[]{:S(2)}, u32[]{:S(2)}) collective-permute-start(bf16[272,128]{1,0:T(8,128)(2,1)S(1)} %collective-permute-done.6.refs_6_), channel_id=1, source_target_pairs={{0,1},{1,0},{2,3},{3,2},{4,5},{5,4},{6,7},{7,6},{8,9},{9,8},{10,11... | collective-permute-start | bytes 208904 | tf_op jit(solution)/shard_map/ppermute | solution.py:267
  21.9 1.0 %collective-permute-done.5.refs_5_ = bf16[272,128]{1,0:T(8,128)(2,1)S(1)} collective-permute-done((bf16[272,128]{1,0:T(8,128)(2,1)S(1)}, bf16[272,128]{1,0:T(8,128)(2,1)S(1)}, u32[]{:S(2)}, u32[]{:S(2)}) %collective-permute-start.5) | collective-permute-done | bytes 69664 | tf_op jit(solution)/shard_map/ppermute | solution.py:267
  22.8 1.9 %collective-permute-done.7.refs_7_ = bf16[272,128]{1,0:T(8,128)(2,1)S(1)} collective-permute-done((bf16[272,128]{1,0:T(8,128)(2,1)S(1)}, bf16[272,128]{1,0:T(8,128)(2,1)S(1)}, u32[]{:S(2)}, u32[]{:S(2)}) %collective-permute-start.7) | collective-permute-done | bytes 69664 | tf_op jit(solution)/shard_map/ppermute | solution.py:267
  24.7 1.2 %collective-permute-done.15.refs_15_ = bf16[272,128]{1,0:T(8,128)(2,1)S(1)} collective-permute-done((bf16[272,128]{1,0:T(8,128)(2,1)S(1)}, bf16[272,128]{1,0:T(8,128)(2,1)S(1)}, u32[]{:S(2)}, u32[]{:S(2)}) %collective-permute-start.15) | collective-permute-done | bytes 69664 | tf_op jit(solution)/shard_map/ppermute | solution.py:267
  26.0 1.2 %copy-done.2 = bf16[30,128,128]{2,1,0:T(8,128)(2,1)S(1)} copy-done((bf16[30,128,128]{2,1,0:T(8,128)(2,1)S(1)}, bf16[30,128,128]{2,1,0:T(8,128)(2,1)}, u32[]{:S(2)}) %copy-start.2) | copy-done | bytes 983064
  27.2 0.9 %copy-done.3 = bf16[272,128]{1,0:T(8,128)(2,1)S(1)} copy-done((bf16[272,128]{1,0:T(8,128)(2,1)S(1)}, bf16[272,128]{1,0:T(8,128)(2,1)}, u32[]{:S(2)}) %copy-start.3) | copy-done | bytes 69656
  28.1 0.6 %copy-done.5 = s32[80]{0:T(128)S(1)} copy-done((s32[80]{0:T(128)S(1)}, s32[80]{0:T(128)}, u32[]{:S(2)}) %copy-start.5) | copy-done | bytes 344
  28.7 4.8 %own_half.1 = (f32[21,256,128]{2,1,0:T(8,128)S(1)}, bf16[16,272,128]{2,1,0:T(8,128)(2,1)S(1)}, bf16[768,2560]{1,0:T(8,128)(2,1)}, s32[1]{0:T(128)}) custom-call(s32[16]{0:T(128)S(1)} %copy-done.4, s32[80]{0:T(128)S(1)} %copy-done.5, bf16[272,128]{1,0:T(8,128)(2,1)S(1)} %copy-done.3, bf16[272,128]{1,0:T(8,128)(2,1)S(1)} %collective-permute-done.1.refs_1_, ...), custom_call_target="tpu_custom_call" | custom-call | tf_op jit(solution)/shard_map/own_half/pallas_call | solution.py:314
  33.5 1.0 %copy-done = bf16[16,272,128]{2,1,0:T(8,128)(2,1)} copy-done((bf16[16,272,128]{2,1,0:T(8,128)(2,1)}, bf16[16,272,128]{2,1,0:T(8,128)(2,1)S(1)}, u32[]{:S(2)}) %copy-start) | copy-done | bytes 1114136
  35.1 1.2 %copy-done.1 = bf16[16,272,128]{2,1,0:T(8,128)(2,1)S(1)} copy-done((bf16[16,272,128]{2,1,0:T(8,128)(2,1)S(1)}, bf16[16,272,128]{2,1,0:T(8,128)(2,1)}, u32[]{:S(2)}) %copy-start.1) | copy-done | bytes 1114136
  36.3 0.6 %copy-done.6 = s32[80]{0:T(128)S(1)} copy-done((s32[80]{0:T(128)S(1)}, s32[80]{0:T(128)}, u32[]{:S(2)}) %copy-start.6) | copy-done | bytes 344
  37.0 5.5 %finish.1 = bf16[768,2560]{1,0:T(8,128)(2,1)} custom-call(s32[16]{0:T(128)S(1)} %copy-done.4, s32[80]{0:T(128)S(1)} %copy-done.6, bf16[16,272,128]{2,1,0:T(8,128)(2,1)S(1)} %copy-done.1, f32[21,256,128]{2,1,0:T(8,128)S(1)} %get-tuple-element.23.start, bf16[30,128,128]{2,1,0:T(8,128)(2,1)} %collective-permute-done.16.refs_0_, ...), custom_call_target="tpu_custom_call", output_to_operand_aliasing={{}: (6, {})} | custom-call | tf_op jit(solution)/shard_map/finish/pallas_call | solution.py:293
  (18 shorter events, 0.0 us)
Async XLA Ops:
  0.0 26.0 %copy-start.4 = (s32[16]{0:T(128)S(1)}, s32[16]{0:T(128)}, u32[]{:S(2)}) copy-start(s32[16]{0:T(128)} %ksym.5) | copy-start | bytes 196
  3.9 31.2 %collective-permute-start.16 = (bf16[30,128,128]{2,1,0:T(8,128)(2,1)}, bf16[30,128,128]{2,1,0:T(8,128)(2,1)}, u32[]{:S(2)}, u32[]{:S(2)}) collective-permute-start(bf16[30,128,128]{2,1,0:T(8,128)(2,1)} %get-tuple-element.20.refs_16_), channel_id=1, source_target_pairs={{0,16},{16,0},{1,17},{17,1},{2,18},{18,2},{3,19},{19,3},{4,20},{20... | collective-permute-start | bytes 2949128 | tf_op jit(solution)/shard_map/ppermute | solution.py:257
  6.9 5.7 %collective-permute-start.4 = (bf16[272,128]{1,0:T(8,128)(2,1)}, bf16[272,128]{1,0:T(8,128)(2,1)S(1)}, u32[]{:S(2)}, u32[]{:S(2)}) collective-permute-start(bf16[272,128]{1,0:T(8,128)(2,1)} %get-tuple-element.19.refs_0_), channel_id=1, source_target_pairs={{0,2},{1,3},{2,0},{3,1},{4,6},{5,7},{6,4},{7,5},{8,10},{9,11},{10,... | collective-permute-start | bytes 208904 | tf_op jit(solution)/shard_map/ppermute | solution.py:267
  8.3 5.2 %collective-permute-start.2 = (bf16[272,128]{1,0:T(8,128)(2,1)}, bf16[272,128]{1,0:T(8,128)(2,1)S(1)}, u32[]{:S(2)}, u32[]{:S(2)}) collective-permute-start(bf16[272,128]{1,0:T(8,128)(2,1)} %get-tuple-element.19.refs_0_), channel_id=1, source_target_pairs={{0,4},{1,5},{2,6},{3,7},{4,0},{5,1},{6,2},{7,3},{8,12},{9,13},{10,... | collective-permute-start | bytes 208904 | tf_op jit(solution)/shard_map/ppermute | solution.py:267
  9.9 6.2 %collective-permute-start.1 = (bf16[272,128]{1,0:T(8,128)(2,1)}, bf16[272,128]{1,0:T(8,128)(2,1)S(1)}, u32[]{:S(2)}, u32[]{:S(2)}) collective-permute-start(bf16[272,128]{1,0:T(8,128)(2,1)} %get-tuple-element.19.refs_0_), channel_id=1, source_target_pairs={{0,8},{1,9},{2,10},{3,11},{4,12},{5,13},{6,14},{7,15},{8,0},{9,1},... | collective-permute-start | bytes 208904 | tf_op jit(solution)/shard_map/ppermute | solution.py:267
  12.6 3.7 %collective-permute-start.8 = (bf16[272,128]{1,0:T(8,128)(2,1)}, bf16[272,128]{1,0:T(8,128)(2,1)S(1)}, u32[]{:S(2)}, u32[]{:S(2)}) collective-permute-start(bf16[272,128]{1,0:T(8,128)(2,1)} %get-tuple-element.19.refs_0_), channel_id=1, source_target_pairs={{0,1},{1,0},{2,3},{3,2},{4,5},{5,4},{6,7},{7,6},{8,9},{9,8},{10,11... | collective-permute-start | bytes 208904 | tf_op jit(solution)/shard_map/ppermute | solution.py:267
  12.6 4.2 %collective-permute-start.12 = (bf16[272,128]{1,0:T(8,128)(2,1)S(1)}, bf16[272,128]{1,0:T(8,128)(2,1)S(1)}, u32[]{:S(2)}, u32[]{:S(2)}) collective-permute-start(bf16[272,128]{1,0:T(8,128)(2,1)S(1)} %collective-permute-done.4.refs_4_), channel_id=1, source_target_pairs={{0,1},{1,0},{2,3},{3,2},{4,5},{5,4},{6,7},{7,6},{8,9},{9,8},{10,11... | collective-permute-start | bytes 208904 | tf_op jit(solution)/shard_map/ppermute | solution.py:267
  13.6 3.2 %collective-permute-start.10 = (bf16[272,128]{1,0:T(8,128)(2,1)S(1)}, bf16[272,128]{1,0:T(8,128)(2,1)S(1)}, u32[]{:S(2)}, u32[]{:S(2)}) collective-permute-start(bf16[272,128]{1,0:T(8,128)(2,1)S(1)} %collective-permute-done.2.refs_2_), channel_id=1, source_target_pairs={{0,1},{1,0},{2,3},{3,2},{4,5},{5,4},{6,7},{7,6},{8,9},{9,8},{10,11... | collective-permute-start | bytes 208904 | tf_op jit(solution)/shard_map/ppermute | solution.py:267
  16.1 4.3 %collective-permute-start.3 = (bf16[272,128]{1,0:T(8,128)(2,1)S(1)}, bf16[272,128]{1,0:T(8,128)(2,1)S(1)}, u32[]{:S(2)}, u32[]{:S(2)}) collective-permute-start(bf16[272,128]{1,0:T(8,128)(2,1)S(1)} %collective-permute-done.1.refs_1_), channel_id=1, source_target_pairs={{0,4},{1,5},{2,6},{3,7},{4,0},{5,1},{6,2},{7,3},{8,12},{9,13},{10,... | collective-permute-start | bytes 208904 | tf_op jit(solution)/shard_map/ppermute | solution.py:267
  16.3 5.0 %collective-permute-start.6 = (bf16[272,128]{1,0:T(8,128)(2,1)S(1)}, bf16[272,128]{1,0:T(8,128)(2,1)S(1)}, u32[]{:S(2)}, u32[]{:S(2)}) collective-permute-start(bf16[272,128]{1,0:T(8,128)(2,1)S(1)} %collective-permute-done.2.refs_2_), channel_id=1, source_target_pairs={{0,2},{1,3},{2,0},{3,1},{4,6},{5,7},{6,4},{7,5},{8,10},{9,11},{10,... | collective-permute-start | bytes 208904 | tf_op jit(solution)/shard_map/ppermute | solution.py:267
  16.8 4.5 %collective-permute-start.9 = (bf16[272,128]{1,0:T(8,128)(2,1)S(1)}, bf16[272,128]{1,0:T(8,128)(2,1)S(1)}, u32[]{:S(2)}, u32[]{:S(2)}) collective-permute-start(bf16[272,128]{1,0:T(8,128)(2,1)S(1)} %collective-permute-done.1.refs_1_), channel_id=1, source_target_pairs={{0,1},{1,0},{2,3},{3,2},{4,5},{5,4},{6,7},{7,6},{8,9},{9,8},{10,11... | collective-permute-start | bytes 208904 | tf_op jit(solution)/shard_map/ppermute | solution.py:267
  16.8 6.0 %collective-permute-start.5 = (bf16[272,128]{1,0:T(8,128)(2,1)S(1)}, bf16[272,128]{1,0:T(8,128)(2,1)S(1)}, u32[]{:S(2)}, u32[]{:S(2)}) collective-permute-start(bf16[272,128]{1,0:T(8,128)(2,1)S(1)} %collective-permute-done.1.refs_1_), channel_id=1, source_target_pairs={{0,2},{1,3},{2,0},{3,1},{4,6},{5,7},{6,4},{7,5},{8,10},{9,11},{10,... | collective-permute-start | bytes 208904 | tf_op jit(solution)/shard_map/ppermute | solution.py:267
  20.4 4.3 %collective-permute-start.7 = (bf16[272,128]{1,0:T(8,128)(2,1)S(1)}, bf16[272,128]{1,0:T(8,128)(2,1)S(1)}, u32[]{:S(2)}, u32[]{:S(2)}) collective-permute-start(bf16[272,128]{1,0:T(8,128)(2,1)S(1)} %collective-permute-done.3.refs_3_), channel_id=1, source_target_pairs={{0,2},{1,3},{2,0},{3,1},{4,6},{5,7},{6,4},{7,5},{8,10},{9,11},{10,... | collective-permute-start | bytes 208904 | tf_op jit(solution)/shard_map/ppermute | solution.py:267
  21.3 3.4 %collective-permute-start.11 = (bf16[272,128]{1,0:T(8,128)(2,1)S(1)}, bf16[272,128]{1,0:T(8,128)(2,1)S(1)}, u32[]{:S(2)}, u32[]{:S(2)}) collective-permute-start(bf16[272,128]{1,0:T(8,128)(2,1)S(1)} %collective-permute-done.3.refs_3_), channel_id=1, source_target_pairs={{0,1},{1,0},{2,3},{3,2},{4,5},{5,4},{6,7},{7,6},{8,9},{9,8},{10,11... | collective-permute-start | bytes 208904 | tf_op jit(solution)/shard_map/ppermute | solution.py:267
  21.3 3.4 %collective-permute-start.14 = (bf16[272,128]{1,0:T(8,128)(2,1)S(1)}, bf16[272,128]{1,0:T(8,128)(2,1)S(1)}, u32[]{:S(2)}, u32[]{:S(2)}) collective-permute-start(bf16[272,128]{1,0:T(8,128)(2,1)S(1)} %collective-permute-done.6.refs_6_), channel_id=1, source_target_pairs={{0,1},{1,0},{2,3},{3,2},{4,5},{5,4},{6,7},{7,6},{8,9},{9,8},{10,11... | collective-permute-start | bytes 208904 | tf_op jit(solution)/shard_map/ppermute | solution.py:267
  22.8 1.9 %collective-permute-start.13 = (bf16[272,128]{1,0:T(8,128)(2,1)S(1)}, bf16[272,128]{1,0:T(8,128)(2,1)S(1)}, u32[]{:S(2)}, u32[]{:S(2)}) collective-permute-start(bf16[272,128]{1,0:T(8,128)(2,1)S(1)} %collective-permute-done.5.refs_5_), channel_id=1, source_target_pairs={{0,1},{1,0},{2,3},{3,2},{4,5},{5,4},{6,7},{7,6},{8,9},{9,8},{10,11... | collective-permute-start | bytes 208904 | tf_op jit(solution)/shard_map/ppermute | solution.py:267
  24.7 1.3 %collective-permute-start.15 = (bf16[272,128]{1,0:T(8,128)(2,1)S(1)}, bf16[272,128]{1,0:T(8,128)(2,1)S(1)}, u32[]{:S(2)}, u32[]{:S(2)}) collective-permute-start(bf16[272,128]{1,0:T(8,128)(2,1)S(1)} %collective-permute-done.7.refs_7_), channel_id=1, source_target_pairs={{0,1},{1,0},{2,3},{3,2},{4,5},{5,4},{6,7},{7,6},{8,9},{9,8},{10,11... | collective-permute-start | bytes 208904 | tf_op jit(solution)/shard_map/ppermute | solution.py:267
  26.0 1.2 %copy-start.2 = (bf16[30,128,128]{2,1,0:T(8,128)(2,1)S(1)}, bf16[30,128,128]{2,1,0:T(8,128)(2,1)}, u32[]{:S(2)}) copy-start(bf16[30,128,128]{2,1,0:T(8,128)(2,1)} %get-tuple-element.20.refs_16_) | copy-start | bytes 2949124
  27.2 0.9 %copy-start.3 = (bf16[272,128]{1,0:T(8,128)(2,1)S(1)}, bf16[272,128]{1,0:T(8,128)(2,1)}, u32[]{:S(2)}) copy-start(bf16[272,128]{1,0:T(8,128)(2,1)} %get-tuple-element.19.refs_0_) | copy-start | bytes 208900
  28.1 0.6 %copy-start.5 = (s32[80]{0:T(128)S(1)}, s32[80]{0:T(128)}, u32[]{:S(2)}) copy-start(s32[80]{0:T(128)} %get-tuple-element.18.tab) | copy-start | bytes 964
  33.5 1.0 %copy-start = (bf16[16,272,128]{2,1,0:T(8,128)(2,1)}, bf16[16,272,128]{2,1,0:T(8,128)(2,1)S(1)}, u32[]{:S(2)}) copy-start(bf16[16,272,128]{2,1,0:T(8,128)(2,1)S(1)} %get-tuple-element.22.amp) | copy-start | bytes 3342340
  35.1 1.2 %copy-start.1 = (bf16[16,272,128]{2,1,0:T(8,128)(2,1)S(1)}, bf16[16,272,128]{2,1,0:T(8,128)(2,1)}, u32[]{:S(2)}) copy-start(bf16[16,272,128]{2,1,0:T(8,128)(2,1)} %copy-done) | copy-start | bytes 3342340
  36.3 0.6 %copy-start.6 = (s32[80]{0:T(128)S(1)}, s32[80]{0:T(128)}, u32[]{:S(2)}) copy-start(s32[80]{0:T(128)} %get-tuple-element.18.tab) | copy-start | bytes 964

commit v2 on v0

v2 whole, which is shorter than its diff:
```python
import functools

import jax
import jax.numpy as jnp
from jax import lax
from jax.experimental import pallas as pl
from jax.experimental.pallas import tpu as pltpu
from jax.sharding import PartitionSpec as P

BLK = 128
IRREPS = 8
MAXO = 2
MAXB = 5
INFO = 16

SMEM = pl.BlockSpec(memory_space=pltpu.SMEM)
VMEM = pl.BlockSpec(memory_space=pltpu.VMEM)
ANY = pl.BlockSpec(memory_space=pl.ANY)
HBM = pl.BlockSpec(memory_space=pltpu.HBM)


def here(x):
    return pltpu.with_memory_space_constraint(x, pltpu.VMEM)


def away(x):
    return pltpu.with_memory_space_constraint(x, pltpu.HBM)


class Table:
    def __init__(self, n_occ, kblocks, vblocks):
        self.n_occ, self.own, self.vblocks = n_occ, kblocks // n_occ, vblocks
        self.nk = 0
        self.kbl = self.nk + n_occ * IRREPS
        self.cnt = self.kbl + n_occ * IRREPS * self.own
        self.vbl = self.cnt + IRREPS
        self.slot = self.vbl + IRREPS * MAXB
        self.off = self.slot + IRREPS * MAXO
        self.total = self.off + n_occ * vblocks
        self.size = self.total + n_occ


def contraction_lists(t, ksym, tab):
    for i in range(t.n_occ * IRREPS):
        tab[t.nk + i] = 0
    for half in range(t.n_occ):
        for i in range(t.own):
            kb = half * t.own + i
            row = half * IRREPS + ksym[kb]
            rank = tab[t.nk + row]
            tab[t.kbl + row * t.own + rank] = kb
            tab[t.nk + row] = rank + 1


def pack_kernel(
    t, first_cap, ksym, vsym, osym, v_ref, a_ref, head, rest, pay, tab, sems
):
    own, vblocks, oblocks = t.own, t.vblocks, osym.shape[0]
    width = a_ref.shape[1]
    me = lax.axis_index("occ")
    others = tuple(lax.rem(me + d, t.n_occ) for d in range(1, t.n_occ))
    contraction_lists(t, ksym, tab)

    def block(row, rank, vb):
        kb = tab[t.kbl + row * own + rank] - me * own
        return v_ref.at[
            pl.ds(pl.multiple_of(kb * BLK, BLK), BLK),
            pl.ds(pl.multiple_of(vb * BLK, BLK), BLK),
        ]

    def send(vb, places):
        place0 = places[0]
        s = vsym[vb]
        row = me * IRREPS + s
        n = tab[t.nk + row]

        @pl.loop(0, n)
        def _(rank):
            place = place0 + rank

            @pl.when(place < first_cap)
            def _():
                pltpu.make_async_copy(
                    block(row, rank, vb), head.at[place], sems.at[place]
                ).start()

            @pl.when(place >= first_cap)
            def _():
                pltpu.make_async_copy(
                    block(row, rank, vb), rest.at[place - first_cap], sems.at[place]
                ).start()

        return (place0 + n,) + tuple(
            place + tab[t.nk + half * IRREPS + s]
            for half, place in zip(others, places[1:])
        )

    totals = lax.fori_loop(0, vblocks, send, (jnp.int32(0),) * t.n_occ)
    most = totals[0]
    for other in totals[1:]:
        most = jnp.maximum(most, other)

    vir = lax.axis_index("vir")
    step = min(width, BLK)
    for q in range(width // step):
        s = ksym[(vir * width + q * step) // BLK]
        cols = slice(q * step, (q + 1) * step)
        found = jnp.int32(0)
        slots = [jnp.int32(-1)] * MAXO
        for ob in range(oblocks):
            match = osym[ob] == s
            slots = [
                jnp.where(match & (found == i), ob, slot) for i, slot in enumerate(slots)
            ]
            found = found + match.astype(jnp.int32)
        for i, ob in enumerate(slots):
            rows = pl.ds(pl.multiple_of(jnp.maximum(ob, 0) * BLK, BLK), BLK)
            part = a_ref[rows, cols]
            pay[i * BLK : (i + 1) * BLK, cols] = jnp.where(
                ob >= 0, part, jnp.zeros_like(part)
            )
    pay[MAXO * BLK :, :] = jnp.full(
        (INFO, width), most.astype(jnp.float32), jnp.float32
    ).astype(jnp.bfloat16)

    @pl.loop(0, totals[0])
    def _(place):
        pltpu.make_async_copy(
            v_ref.at[pl.ds(0, BLK), pl.ds(0, BLK)], head.at[0], sems.at[place]
        ).wait()


def plan_kernel(t, ksym, vsym, osym, after, out, tab, *refs):
    del after
    zeros, sems = refs[-2:]
    zeros[...] = jnp.zeros_like(zeros)
    fills = [
        pltpu.make_async_copy(zeros, out.at[pl.ds(i * BLK, BLK)], sems.at[i])
        for i in range(out.shape[0] // BLK)
    ]
    for fill in fills:
        fill.start()

    contraction_lists(t, ksym, tab)
    for s in range(IRREPS):
        tab[t.cnt + s] = 0
        for slot in range(MAXO):
            tab[t.slot + s * MAXO + slot] = -1
    for ob in range(osym.shape[0]):
        s = osym[ob]
        used = (tab[t.slot + s * MAXO] >= 0).astype(jnp.int32)
        tab[t.slot + s * MAXO + used] = ob

    def count(vb, places):
        s = vsym[vb]
        rank = tab[t.cnt + s]
        tab[t.vbl + s * MAXB + rank] = vb
        tab[t.cnt + s] = rank + 1
        new = []
        for half, place in enumerate(places):
            tab[t.off + half * t.vblocks + vb] = place
            new.append(place + tab[t.nk + half * IRREPS + s])
        return tuple(new)

    totals = lax.fori_loop(0, t.vblocks, count, (jnp.int32(0),) * t.n_occ)
    for half, total in enumerate(totals):
        tab[t.total + half] = total
    for fill in fills:
        fill.wait()


def each_irrep(t, tab, spare, act):
    @pl.loop(0, IRREPS)
    def _(s):
        count = tab[t.cnt + s]
        vbs = [
            jnp.where(j < count, tab[t.vbl + s * MAXB + j], spare) for j in range(MAXB)
        ]
        one = tab[t.slot + s * MAXO] >= 0
        more = tab[t.slot + s * MAXO + 1] >= 0

        @pl.when((count > 0) & one & jnp.logical_not(more))
        def _():
            act(s, BLK, vbs)

        @pl.when((count > 0) & more)
        def _():
            act(s, MAXO * BLK, vbs)


def multiply(t, tab, half, s, rows, vbs, amp, blocks, acc, places):
    row = half * IRREPS + s
    offs = [
        jnp.where(
            vb < t.vblocks,
            tab[t.off + half * t.vblocks + jnp.minimum(vb, t.vblocks - 1)],
            0,
        )
        for vb in vbs
    ]

    @pl.loop(0, tab[t.nk + row])
    def _(rank):
        left = amp[tab[t.kbl + row * t.own + rank], :rows, :]
        for off, place in zip(offs, places):
            acc[place, :rows, :] += jnp.dot(
                left, blocks[off + rank], preferred_element_type=jnp.float32
            )


def sort_kernel(masks, *refs):
    parts, (amp, most) = refs[:-2], refs[-2:]
    peak = parts[0][..., MAXO * BLK :, :].astype(jnp.float32)
    if masks:
        me = lax.axis_index("vir")
        for mask, part in zip(masks, parts):
            amp[me ^ mask] = part[: MAXO * BLK, :]
            peak = jnp.maximum(peak, part[MAXO * BLK :, :].astype(jnp.float32))
    else:
        amp[...] = parts[0][:, : MAXO * BLK, :]
    most[0] = jnp.max(peak).astype(jnp.int32)


def finish_kernel(t, first_cap, tab, amp, *refs):
    n = t.n_occ
    heads, rests = refs[:n], refs[n : 2 * n]
    _, out, acc, stage, blocks, sems = refs[2 * n :]
    me = lax.axis_index("occ")
    halves = [lax.rem(me - shift + n, n) for shift in range(n)]

    def send(s, slot, vb):
        ob = tab[t.slot + s * MAXO + slot]
        return pltpu.make_async_copy(
            stage.at[vb, pl.ds(slot * BLK, BLK)],
            out.at[
                pl.ds(pl.multiple_of(ob * BLK, BLK), BLK),
                pl.ds(pl.multiple_of(vb * BLK, BLK), BLK),
            ],
            sems.at[vb, slot],
        )

    def products(sources):
        def act(s, rows, vbs):
            acc[:, :rows, :] = jnp.zeros((MAXB, rows, BLK), jnp.float32)
            for half, source in zip(halves, sources):
                multiply(t, tab, half, s, rows, vbs, amp, source, acc, range(MAXB))
            for j, vb in enumerate(vbs):

                @pl.when(vb < t.vblocks)
                def _():
                    stage[vb, :rows, :] = acc[j, :rows, :].astype(jnp.bfloat16)
                    for slot in range(rows // BLK):
                        send(s, slot, vb).start()

        each_irrep(t, tab, t.vblocks, act)

    most = tab[t.total]
    for half in range(1, n):
        most = jnp.maximum(most, tab[t.total + half])

    @pl.when(most <= first_cap)
    def _():
        products(heads)

    @pl.when(most > first_cap)
    def _():
        for i in range(n):
            blocks[i, :first_cap] = heads[i][...]
            pltpu.sync_copy(rests[i], blocks.at[i, pl.ds(first_cap, blocks.shape[1] - first_cap)])
        products([blocks.at[i] for i in range(n)])

    def settle(s, rows, vbs):
        for vb in vbs:

            @pl.when(vb < t.vblocks)
            def _():
                for slot in range(rows // BLK):
                    send(s, slot, vb).wait()

    each_irrep(t, tab, t.vblocks, settle)


def per_device(n_occ, n_vir, amplitudes, integrals, occ_sym, vir_sym, k_sym):
    occ_rows, width = amplitudes.shape
    kblocks = k_sym.shape[0]
    vblocks = vir_sym.shape[0]
    cols = vblocks * BLK
    t = Table(n_occ, kblocks, vblocks)
    cap = t.own * MAXB
    first_cap = (cap * 3 + 3) // 4
    rows = MAXO * BLK + INFO
    bf16, f32, i32 = jnp.bfloat16, jnp.float32, jnp.int32

    head, rest, pay = pl.pallas_call(
        functools.partial(pack_kernel, t, first_cap),
        out_shape=(
            pltpu.VMEM((first_cap, BLK, BLK), bf16),
            pltpu.VMEM((cap - first_cap, BLK, BLK), bf16),
            pltpu.VMEM((rows, width), bf16),
        ),
        in_specs=[SMEM, SMEM, SMEM, HBM, VMEM],
        out_specs=(VMEM, VMEM, VMEM),
        scratch_shapes=[
            pltpu.SMEM((t.size,), i32),
            pltpu.SemaphoreType.DMA((cap,)),
        ],
        compiler_params=pltpu.CompilerParams(vmem_limit_bytes=8 * 2**20),
        name="pack",
    )(*[away(x) for x in (k_sym, vir_sym, occ_sym, integrals, amplitudes)])
    zero_out, tab, *spares = pl.pallas_call(
        functools.partial(plan_kernel, t),
        out_shape=(pltpu.HBM((occ_rows, cols), bf16), pltpu.SMEM((t.size,), i32))
        + (pltpu.HBM((cap - first_cap, BLK, BLK), bf16),) * (n_occ - 1),
        in_specs=[SMEM, SMEM, SMEM, ANY],
        out_specs=(HBM, SMEM) + (HBM,) * (n_occ - 1),
        scratch_shapes=[
            pltpu.VMEM((BLK, cols), bf16),
            pltpu.SemaphoreType.DMA((occ_rows // BLK,)),
        ],
        compiler_params=pltpu.CompilerParams(vmem_limit_bytes=4 * 2**20),
        name="plan",
    )(*[away(x) for x in (k_sym, vir_sym, occ_sym)], pay)

    shifts = tuple(range(1, n_occ))

    def across(x, shift):
        return lax.ppermute(x, "occ", [(i, (i + shift) % n_occ) for i in range(n_occ)])

    heads = [across(head, shift) for shift in shifts]

    bits = [1 << b for b in range(n_vir.bit_length() - 1)][::-1]
    masks = [0]
    for bit in bits:
        masks = masks + [m ^ bit for m in masks]
    if width == BLK:
        parts = [pay]
        for bit in bits:
            pairs = [(i, i ^ bit) for i in range(n_vir)]
            parts = parts + [lax.ppermute(p, "vir", pairs) for p in parts]
            if len(parts) == 2:
                parts[1], zero_out = lax.optimization_barrier((parts[1], zero_out))
    else:
        whole = pay[None]
        for bit in bits:
            pairs = [(i, i ^ bit) for i in range(n_vir)]
            whole = jnp.concatenate([whole, lax.ppermute(whole, "vir", pairs)])
        place = [masks.index(m) for m in range(n_vir)]
        order = jnp.asarray(place, i32)[
            jnp.arange(n_vir, dtype=i32) ^ lax.axis_index("vir").astype(i32)
        ]
        whole = whole[order].transpose(1, 0, 2).reshape(rows, kblocks, BLK)
        parts, masks = [whole.transpose(1, 0, 2)], []

    amp, most = pl.pallas_call(
        functools.partial(sort_kernel, tuple(masks)),
        out_shape=(
            pltpu.VMEM((kblocks, MAXO * BLK, BLK), bf16),
            jax.ShapeDtypeStruct((1,), i32),
        ),
        in_specs=[VMEM] * len(parts),
        out_specs=(VMEM, SMEM),
        compiler_params=pltpu.CompilerParams(vmem_limit_bytes=8 * 2**20),
        name="sort",
    )(*parts)

    rests = lax.cond(
        most[0] > first_cap,
        lambda x, spares: [across(x, shift) for shift in shifts],
        lambda x, spares: spares,
        rest,
        spares,
    )
    heads, rests = [head] + heads, [rest] + rests
    return pl.pallas_call(
        functools.partial(finish_kernel, t, first_cap),
        out_shape=jax.ShapeDtypeStruct((occ_rows, cols), bf16),
        in_specs=[SMEM] + [VMEM] * (1 + n_occ) + [ANY] * n_occ + [HBM],
        out_specs=HBM,
        scratch_shapes=[
            pltpu.VMEM((MAXB, MAXO * BLK, BLK), f32),
            pltpu.VMEM((vblocks, MAXO * BLK, BLK), bf16),
            pltpu.VMEM((n_occ, cap, BLK, BLK), bf16),
            pltpu.SemaphoreType.DMA((vblocks, MAXO)),
        ],
        input_output_aliases={2 + 2 * n_occ: 0},
        compiler_params=pltpu.CompilerParams(vmem_limit_bytes=24 * 2**20),
        name="finish",
    )(tab, *[here(x) for x in (amp, *heads)], *rests, zero_out)


def solution(mesh):
    return jax.shard_map(
        functools.partial(per_device, mesh.shape["occ"], mesh.shape["vir"]),
        mesh=mesh,
        in_specs=(P("occ", "vir"), P("occ", "vir"), P("occ"), P("vir"), P()),
        out_specs=P("occ", "vir"),
        check_vma=False,
    )
```

time: 210 us -> 31.8 us (0.15)
  waiting for transfers between devices: 168 us -> 7.26 us
  matrix products: 13.4 us -> 0 us
  starting transfers between devices: 0.04 us -> 13.4 us
  between operations: 13.4 us -> 0.7 us
  local copies, waits for them, and re-layouts: 11.3 us -> 0 us
  Pallas kernels: 0 us -> 10.2 us
  other arithmetic: 3.38 us -> 0 us
    all_gather x2 -> x0, waiting for transfers between devices: 167 us -> none  [the longest x1 129 us: per_device(): lax.all_gather(masked_v, 'occ', axis=0, tiled=True)]
    dot_general x1 -> x0, matrix products: 13.4 us -> none  [per_device(): jnp.dot(amp_masked, lax.all_gather(masked_v, 'occ', axis=0, tiled=True),...]
    ppermute x0 -> x16, starting transfers between devices: none -> 13.4 us  [the longest x15 10.3 us: per_device(): parts = parts + [lax.ppermute(p, 'vir', pairs) for p in parts]]
    pallas_call x0 -> x4, Pallas kernels: none -> 10.2 us  [the longest x1 3.79 us: per_device(): pl.pallas_call(functools.partial(finish_kernel, t, first_cap), out_shape=...]
    unnamed x9 -> x0, local copies, waits for them, and re-layouts: 10.1 us -> none
    ppermute x0 -> x16, waiting for transfers between devices: none -> 7.26 us  [the longest x15 6.05 us: per_device(): parts = parts + [lax.ppermute(p, 'vir', pairs) for p in parts]]
    mul x1 -> x0, other arithmetic: 3.04 us -> none  [per_device(): integrals.reshape(own_count, BLK, vir_blocks, BLK)]
  transfers between devices with their start and end apart: 2 -> 16, of which waited for: 2 -> 6; matrix products, arithmetic and copies ran while one was open for 6% -> 0% of each run, Pallas kernels for 0% -> 11%
where the time goes in v2:
time: 31.8 us; the launch traced here: 31.5 us
  starting transfers between devices  13.4 us (42%)
  Pallas kernels  10.2 us (32%)
  waiting for transfers between devices  7.26 us (23%)
  between operations  0.7 us (2%)
    ppermute x15, starting transfers between devices, per_device(): parts = parts + [lax.ppermute(p, 'vir', pairs) for p in parts]  10.3 us
    ppermute x15, waiting for transfers between devices, per_device(): parts = parts + [lax.ppermute(p, 'vir', pairs) for p in parts]  6.05 us
    pallas_call x1, Pallas kernels, per_device(): pl.pallas_call(functools.partial(finish_kernel, t, first_cap), out_shape=...  3.79 us
    ppermute x1, starting transfers between devices, across(): lax.ppermute(x, 'occ', [(i, (i + shift) % n_occ) for i in range(n_occ)])  3.07 us
    pallas_call x1, Pallas kernels, per_device(): pl.pallas_call(functools.partial(pack_kernel, t, first_cap), out_shape=(p...  2.93 us
    pallas_call x1, Pallas kernels, per_device(): pl.pallas_call(functools.partial(plan_kernel, t), out_shape=(pltpu.HBM((o...  2.73 us
    ppermute x1, waiting for transfers between devices, across(): lax.ppermute(x, 'occ', [(i, (i + shift) % n_occ) for i in range(n_occ)])  1.21 us
    pallas_call x1, Pallas kernels, per_device(): pl.pallas_call(functools.partial(sort_kernel, tuple(masks)), out_shape=(p...  0.71 us
  transfers between devices with their start and end apart: 16, of which 6 were waited for; matrix products, arithmetic and copies ran while one was open for 0% of the time, Pallas kernels for 11%

profile of v2, /device:TPU:0, one launch (start us, length us, event | category | flops | bytes accessed | tf_op | source)
XLA Modules:
  0.0 31.5 jit_solution(5191162222330569360)
XLA Ops:
  0.0 2.9 %pack.1 = (bf16[30,128,128]{2,1,0:T(8,128)(2,1)S(1)}, bf16[10,128,128]{2,1,0:T(8,128)(2,1)S(1)}, bf16[272,128]{1,0:T(8,128)(2,1)S(1)}) custom-call(s32[16]{0:T(128)} %ksym.3, s32[20]{0:T(128)} %vsym.3, s32[6]{0:T(128)} %osym.3, bf16[1024,2560]{1,0:T(8,128)(2,1)} %v_ref.1, bf16[768,128]{1,0:T(8,128)(2,1)} %a_ref.1), custom_call_target="tpu_custom_call" | custom-call | tf_op jit(solution)/shard_map/pack/pallas_call | solution.py:294
  2.9 3.1 %collective-permute-start.16 = (bf16[30,128,128]{2,1,0:T(8,128)(2,1)S(1)}, bf16[30,128,128]{2,1,0:T(8,128)(2,1)S(1)}, u32[]{:S(2)}, u32[]{:S(2)}) collective-permute-start(bf16[30,128,128]{2,1,0:T(8,128)(2,1)S(1)} %get-tuple-element.25.refs_0_), channel_id=1, source_target_pairs={{0,16},{16,0},{1,17},{17,1},{2,18},{18,2},{3,19},{19,3},{4,20},{20... | collective-permute-start | bytes 2949128 | tf_op jit(solution)/shard_map/ppermute | solution.py:327
  6.0 2.6 %collective-permute-start.1 = (bf16[272,128]{1,0:T(8,128)(2,1)S(1)}, bf16[272,128]{1,0:T(8,128)(2,1)S(1)}, u32[]{:S(2)}, u32[]{:S(2)}) collective-permute-start(bf16[272,128]{1,0:T(8,128)(2,1)S(1)} %get-tuple-element.20.after.refs_0_), channel_id=1, source_target_pairs={{0,8},{1,9},{2,10},{3,11},{4,12},{5,13},{6,14},{7,15},{8,0},{9,1},... | collective-permute-start | bytes 208904 | tf_op jit(solution)/shard_map/ppermute | solution.py:339
  8.6 1.5 %collective-permute-start.4 = (bf16[272,128]{1,0:T(8,128)(2,1)S(1)}, bf16[272,128]{1,0:T(8,128)(2,1)S(1)}, u32[]{:S(2)}, u32[]{:S(2)}) collective-permute-start(bf16[272,128]{1,0:T(8,128)(2,1)S(1)} %get-tuple-element.20.after.refs_0_), channel_id=1, source_target_pairs={{0,2},{1,3},{2,0},{3,1},{4,6},{5,7},{6,4},{7,5},{8,10},{9,11},{10,... | collective-permute-start | bytes 208904 | tf_op jit(solution)/shard_map/ppermute | solution.py:339
  10.1 1.5 %collective-permute-start.2 = (bf16[272,128]{1,0:T(8,128)(2,1)S(1)}, bf16[272,128]{1,0:T(8,128)(2,1)S(1)}, u32[]{:S(2)}, u32[]{:S(2)}) collective-permute-start(bf16[272,128]{1,0:T(8,128)(2,1)S(1)} %get-tuple-element.20.after.refs_0_), channel_id=1, source_target_pairs={{0,4},{1,5},{2,6},{3,7},{4,0},{5,1},{6,2},{7,3},{8,12},{9,13},{10,... | collective-permute-start | bytes 208904 | tf_op jit(solution)/shard_map/ppermute | solution.py:339
  11.6 0.0 collective-permute-start.8
  11.6 2.7 %plan.1 = (bf16[768,2560]{1,0:T(8,128)(2,1)}, s32[250]{0:T(256)S(4)}, bf16[10,128,128]{2,1,0:T(8,128)(2,1)}) custom-call(s32[16]{0:T(128)} %ksym.3, s32[20]{0:T(128)} %vsym.3, s32[6]{0:T(128)} %osym.3, bf16[272,128]{1,0:T(8,128)(2,1)S(1)} %get-tuple-element.20.after.refs_0_), custom_call_target="tpu_custom_call" | custom-call | tf_op jit(solution)/shard_map/plan/pallas_call | solution.py:310
  14.4 0.0 collective-permute-done.1.refs_1_
  14.4 0.0 collective-permute-done.4.refs_4_
  14.4 0.6 %collective-permute-start.12 = (bf16[272,128]{1,0:T(8,128)(2,1)S(1)}, bf16[272,128]{1,0:T(8,128)(2,1)S(1)}, u32[]{:S(2)}, u32[]{:S(2)}) collective-permute-start(bf16[272,128]{1,0:T(8,128)(2,1)S(1)} %collective-permute-done.4.refs_4_), channel_id=1, source_target_pairs={{0,1},{1,0},{2,3},{3,2},{4,5},{5,4},{6,7},{7,6},{8,9},{9,8},{10,11... | collective-permute-start | bytes 208904 | tf_op jit(solution)/shard_map/ppermute | solution.py:339
  15.0 0.0 collective-permute-done.2.refs_2_
  15.0 0.1 collective-permute-start.10
  15.0 0.9 %collective-permute-start.3 = (bf16[272,128]{1,0:T(8,128)(2,1)S(1)}, bf16[272,128]{1,0:T(8,128)(2,1)S(1)}, u32[]{:S(2)}, u32[]{:S(2)}) collective-permute-start(bf16[272,128]{1,0:T(8,128)(2,1)S(1)} %collective-permute-done.1.refs_1_), channel_id=1, source_target_pairs={{0,4},{1,5},{2,6},{3,7},{4,0},{5,1},{6,2},{7,3},{8,12},{9,13},{10,... | collective-permute-start | bytes 208904 | tf_op jit(solution)/shard_map/ppermute | solution.py:339
  15.9 0.5 %collective-permute-start.6 = (bf16[272,128]{1,0:T(8,128)(2,1)S(1)}, bf16[272,128]{1,0:T(8,128)(2,1)S(1)}, u32[]{:S(2)}, u32[]{:S(2)}) collective-permute-start(bf16[272,128]{1,0:T(8,128)(2,1)S(1)} %collective-permute-done.2.refs_2_), channel_id=1, source_target_pairs={{0,2},{1,3},{2,0},{3,1},{4,6},{5,7},{6,4},{7,5},{8,10},{9,11},{10,... | collective-permute-start | bytes 208904 | tf_op jit(solution)/shard_map/ppermute | solution.py:339
  16.5 0.0 collective-permute-done.10.refs_10_
  16.5 1.6 %collective-permute-start.5 = (bf16[272,128]{1,0:T(8,128)(2,1)S(1)}, bf16[272,128]{1,0:T(8,128)(2,1)S(1)}, u32[]{:S(2)}, u32[]{:S(2)}) collective-permute-start(bf16[272,128]{1,0:T(8,128)(2,1)S(1)} %collective-permute-done.1.refs_1_), channel_id=1, source_target_pairs={{0,2},{1,3},{2,0},{3,1},{4,6},{5,7},{6,4},{7,5},{8,10},{9,11},{10,... | collective-permute-start | bytes 208904 | tf_op jit(solution)/shard_map/ppermute | solution.py:339
  18.0 1.5 %collective-permute-done.3.refs_3_ = bf16[272,128]{1,0:T(8,128)(2,1)S(1)} collective-permute-done((bf16[272,128]{1,0:T(8,128)(2,1)S(1)}, bf16[272,128]{1,0:T(8,128)(2,1)S(1)}, u32[]{:S(2)}, u32[]{:S(2)}) %collective-permute-start.3) | collective-permute-done | bytes 69664 | tf_op jit(solution)/shard_map/ppermute | solution.py:339
  19.6 0.5 %collective-permute-start.7 = (bf16[272,128]{1,0:T(8,128)(2,1)S(1)}, bf16[272,128]{1,0:T(8,128)(2,1)S(1)}, u32[]{:S(2)}, u32[]{:S(2)}) collective-permute-start(bf16[272,128]{1,0:T(8,128)(2,1)S(1)} %collective-permute-done.3.refs_3_), channel_id=1, source_target_pairs={{0,2},{1,3},{2,0},{3,1},{4,6},{5,7},{6,4},{7,5},{8,10},{9,11},{10,... | collective-permute-start | bytes 208904 | tf_op jit(solution)/shard_map/ppermute | solution.py:339
  20.1 0.8 %collective-permute-done.6.refs_6_ = bf16[272,128]{1,0:T(8,128)(2,1)S(1)} collective-permute-done((bf16[272,128]{1,0:T(8,128)(2,1)S(1)}, bf16[272,128]{1,0:T(8,128)(2,1)S(1)}, u32[]{:S(2)}, u32[]{:S(2)}) %collective-permute-start.6) | collective-permute-done | bytes 69664 | tf_op jit(solution)/shard_map/ppermute | solution.py:339
  20.9 0.0 collective-permute-start.11
  20.9 0.0 collective-permute-done.9.refs_9_
  20.9 0.5 %collective-permute-start.14 = (bf16[272,128]{1,0:T(8,128)(2,1)S(1)}, bf16[272,128]{1,0:T(8,128)(2,1)S(1)}, u32[]{:S(2)}, u32[]{:S(2)}) collective-permute-start(bf16[272,128]{1,0:T(8,128)(2,1)S(1)} %collective-permute-done.6.refs_6_), channel_id=1, source_target_pairs={{0,1},{1,0},{2,3},{3,2},{4,5},{5,4},{6,7},{7,6},{8,9},{9,8},{10,11... | collective-permute-start | bytes 208904 | tf_op jit(solution)/shard_map/ppermute | solution.py:339
  21.4 0.3 collective-permute-done.5.refs_5_
  21.7 0.0 collective-permute-start.13
  21.7 2.1 %collective-permute-done.7.refs_7_ = bf16[272,128]{1,0:T(8,128)(2,1)S(1)} collective-permute-done((bf16[272,128]{1,0:T(8,128)(2,1)S(1)}, bf16[272,128]{1,0:T(8,128)(2,1)S(1)}, u32[]{:S(2)}, u32[]{:S(2)}) %collective-permute-start.7) | collective-permute-done | bytes 69664 | tf_op jit(solution)/shard_map/ppermute | solution.py:339
  23.9 0.0 collective-permute-start.15
  23.9 0.0 collective-permute-done.14.refs_14_
  23.9 0.0 collective-permute-done.13.refs_13_
  23.9 1.2 %collective-permute-done.15.refs_15_ = bf16[272,128]{1,0:T(8,128)(2,1)S(1)} collective-permute-done((bf16[272,128]{1,0:T(8,128)(2,1)S(1)}, bf16[272,128]{1,0:T(8,128)(2,1)S(1)}, u32[]{:S(2)}, u32[]{:S(2)}) %collective-permute-start.15) | collective-permute-done | bytes 69664 | tf_op jit(solution)/shard_map/ppermute | solution.py:339
  25.1 0.7 %sort.1 = (bf16[16,256,128]{2,1,0:T(8,128)(2,1)S(1)}, s32[1]{0:T(128)}) custom-call(bf16[272,128]{1,0:T(8,128)(2,1)S(1)} %get-tuple-element.20.after.refs_0_, bf16[272,128]{1,0:T(8,128)(2,1)S(1)} %collective-permute-done.1.refs_1_, bf16[272,128]{1,0:T(8,128)(2,1)S(1)} %collective-permute-done.2.refs_2_, bf16[272,128]{1,0:T(8,128)(2,1)S(1)} %collective-permute-done.3.refs_3_, ...), custom_call_target="tpu_custom_call" | custom-call | tf_op jit(solution)/shard_map/sort/pallas_call | solution.py:354
  26.5 1.2 %collective-permute-done.16.refs_1_ = bf16[30,128,128]{2,1,0:T(8,128)(2,1)S(1)} collective-permute-done((bf16[30,128,128]{2,1,0:T(8,128)(2,1)S(1)}, bf16[30,128,128]{2,1,0:T(8,128)(2,1)S(1)}, u32[]{:S(2)}, u32[]{:S(2)}) %collective-permute-start.16) | collective-permute-done | bytes 983072 | tf_op jit(solution)/shard_map/ppermute | solution.py:327
  27.7 3.8 %finish.1 = bf16[768,2560]{1,0:T(8,128)(2,1)} custom-call(s32[250]{0:T(256)S(4)} %get-tuple-element.21.tab, bf16[16,256,128]{2,1,0:T(8,128)(2,1)S(1)} %get-tuple-element.24.amp, bf16[30,128,128]{2,1,0:T(8,128)(2,1)S(1)} %get-tuple-element.25.refs_0_, bf16[30,128,128]{2,1,0:T(8,128)(2,1)S(1)} %collective-permute-done.16.refs_1_, ...), custom_call_target="tpu_custom_call", output_to_operand_aliasing={{}: (6, {})} | custom-call | tf_op jit(solution)/shard_map/finish/pallas_call | solution.py:374
  (5 shorter events, 0.0 us)
Async XLA Ops:
  2.9 24.8 %collective-permute-start.16 = (bf16[30,128,128]{2,1,0:T(8,128)(2,1)S(1)}, bf16[30,128,128]{2,1,0:T(8,128)(2,1)S(1)}, u32[]{:S(2)}, u32[]{:S(2)}) collective-permute-start(bf16[30,128,128]{2,1,0:T(8,128)(2,1)S(1)} %get-tuple-element.25.refs_0_), channel_id=1, source_target_pairs={{0,16},{16,0},{1,17},{17,1},{2,18},{18,2},{3,19},{19,3},{4,20},{20... | collective-permute-start | bytes 2949128 | tf_op jit(solution)/shard_map/ppermute | solution.py:327
  6.0 8.4 %collective-permute-start.1 = (bf16[272,128]{1,0:T(8,128)(2,1)S(1)}, bf16[272,128]{1,0:T(8,128)(2,1)S(1)}, u32[]{:S(2)}, u32[]{:S(2)}) collective-permute-start(bf16[272,128]{1,0:T(8,128)(2,1)S(1)} %get-tuple-element.20.after.refs_0_), channel_id=1, source_target_pairs={{0,8},{1,9},{2,10},{3,11},{4,12},{5,13},{6,14},{7,15},{8,0},{9,1},... | collective-permute-start | bytes 208904 | tf_op jit(solution)/shard_map/ppermute | solution.py:339
  8.6 5.8 %collective-permute-start.4 = (bf16[272,128]{1,0:T(8,128)(2,1)S(1)}, bf16[272,128]{1,0:T(8,128)(2,1)S(1)}, u32[]{:S(2)}, u32[]{:S(2)}) collective-permute-start(bf16[272,128]{1,0:T(8,128)(2,1)S(1)} %get-tuple-element.20.after.refs_0_), channel_id=1, source_target_pairs={{0,2},{1,3},{2,0},{3,1},{4,6},{5,7},{6,4},{7,5},{8,10},{9,11},{10,... | collective-permute-start | bytes 208904 | tf_op jit(solution)/shard_map/ppermute | solution.py:339
  10.1 4.9 %collective-permute-start.2 = (bf16[272,128]{1,0:T(8,128)(2,1)S(1)}, bf16[272,128]{1,0:T(8,128)(2,1)S(1)}, u32[]{:S(2)}, u32[]{:S(2)}) collective-permute-start(bf16[272,128]{1,0:T(8,128)(2,1)S(1)} %get-tuple-element.20.after.refs_0_), channel_id=1, source_target_pairs={{0,4},{1,5},{2,6},{3,7},{4,0},{5,1},{6,2},{7,3},{8,12},{9,13},{10,... | collective-permute-start | bytes 208904 | tf_op jit(solution)/shard_map/ppermute | solution.py:339
  11.6 4.3 %collective-permute-start.8 = (bf16[272,128]{1,0:T(8,128)(2,1)S(1)}, bf16[272,128]{1,0:T(8,128)(2,1)S(1)}, u32[]{:S(2)}, u32[]{:S(2)}) collective-permute-start(bf16[272,128]{1,0:T(8,128)(2,1)S(1)} %get-tuple-element.20.after.refs_0_), channel_id=1, source_target_pairs={{0,1},{1,0},{2,3},{3,2},{4,5},{5,4},{6,7},{7,6},{8,9},{9,8},{10,11... | collective-permute-start | bytes 208904 | tf_op jit(solution)/shard_map/ppermute | solution.py:339
  14.4 2.1 %collective-permute-start.12 = (bf16[272,128]{1,0:T(8,128)(2,1)S(1)}, bf16[272,128]{1,0:T(8,128)(2,1)S(1)}, u32[]{:S(2)}, u32[]{:S(2)}) collective-permute-start(bf16[272,128]{1,0:T(8,128)(2,1)S(1)} %collective-permute-done.4.refs_4_), channel_id=1, source_target_pairs={{0,1},{1,0},{2,3},{3,2},{4,5},{5,4},{6,7},{7,6},{8,9},{9,8},{10,11... | collective-permute-start | bytes 208904 | tf_op jit(solution)/shard_map/ppermute | solution.py:339
  15.0 1.5 %collective-permute-start.10 = (bf16[272,128]{1,0:T(8,128)(2,1)S(1)}, bf16[272,128]{1,0:T(8,128)(2,1)S(1)}, u32[]{:S(2)}, u32[]{:S(2)}) collective-permute-start(bf16[272,128]{1,0:T(8,128)(2,1)S(1)} %collective-permute-done.2.refs_2_), channel_id=1, source_target_pairs={{0,1},{1,0},{2,3},{3,2},{4,5},{5,4},{6,7},{7,6},{8,9},{9,8},{10,11... | collective-permute-start | bytes 208904 | tf_op jit(solution)/shard_map/ppermute | solution.py:339
  15.0 4.5 %collective-permute-start.3 = (bf16[272,128]{1,0:T(8,128)(2,1)S(1)}, bf16[272,128]{1,0:T(8,128)(2,1)S(1)}, u32[]{:S(2)}, u32[]{:S(2)}) collective-permute-start(bf16[272,128]{1,0:T(8,128)(2,1)S(1)} %collective-permute-done.1.refs_1_), channel_id=1, source_target_pairs={{0,4},{1,5},{2,6},{3,7},{4,0},{5,1},{6,2},{7,3},{8,12},{9,13},{10,... | collective-permute-start | bytes 208904 | tf_op jit(solution)/shard_map/ppermute | solution.py:339
  15.9 5.0 %collective-permute-start.6 = (bf16[272,128]{1,0:T(8,128)(2,1)S(1)}, bf16[272,128]{1,0:T(8,128)(2,1)S(1)}, u32[]{:S(2)}, u32[]{:S(2)}) collective-permute-start(bf16[272,128]{1,0:T(8,128)(2,1)S(1)} %collective-permute-done.2.refs_2_), channel_id=1, source_target_pairs={{0,2},{1,3},{2,0},{3,1},{4,6},{5,7},{6,4},{7,5},{8,10},{9,11},{10,... | collective-permute-start | bytes 208904 | tf_op jit(solution)/shard_map/ppermute | solution.py:339
  16.5 4.5 %collective-permute-start.9 = (bf16[272,128]{1,0:T(8,128)(2,1)S(1)}, bf16[272,128]{1,0:T(8,128)(2,1)S(1)}, u32[]{:S(2)}, u32[]{:S(2)}) collective-permute-start(bf16[272,128]{1,0:T(8,128)(2,1)S(1)} %collective-permute-done.1.refs_1_), channel_id=1, source_target_pairs={{0,1},{1,0},{2,3},{3,2},{4,5},{5,4},{6,7},{7,6},{8,9},{9,8},{10,11... | collective-permute-start | bytes 208904 | tf_op jit(solution)/shard_map/ppermute | solution.py:339
  16.5 5.3 %collective-permute-start.5 = (bf16[272,128]{1,0:T(8,128)(2,1)S(1)}, bf16[272,128]{1,0:T(8,128)(2,1)S(1)}, u32[]{:S(2)}, u32[]{:S(2)}) collective-permute-start(bf16[272,128]{1,0:T(8,128)(2,1)S(1)} %collective-permute-done.1.refs_1_), channel_id=1, source_target_pairs={{0,2},{1,3},{2,0},{3,1},{4,6},{5,7},{6,4},{7,5},{8,10},{9,11},{10,... | collective-permute-start | bytes 208904 | tf_op jit(solution)/shard_map/ppermute | solution.py:339
  19.6 4.3 %collective-permute-start.7 = (bf16[272,128]{1,0:T(8,128)(2,1)S(1)}, bf16[272,128]{1,0:T(8,128)(2,1)S(1)}, u32[]{:S(2)}, u32[]{:S(2)}) collective-permute-start(bf16[272,128]{1,0:T(8,128)(2,1)S(1)} %collective-permute-done.3.refs_3_), channel_id=1, source_target_pairs={{0,2},{1,3},{2,0},{3,1},{4,6},{5,7},{6,4},{7,5},{8,10},{9,11},{10,... | collective-permute-start | bytes 208904 | tf_op jit(solution)/shard_map/ppermute | solution.py:339
  20.9 3.0 %collective-permute-start.11 = (bf16[272,128]{1,0:T(8,128)(2,1)S(1)}, bf16[272,128]{1,0:T(8,128)(2,1)S(1)}, u32[]{:S(2)}, u32[]{:S(2)}) collective-permute-start(bf16[272,128]{1,0:T(8,128)(2,1)S(1)} %collective-permute-done.3.refs_3_), channel_id=1, source_target_pairs={{0,1},{1,0},{2,3},{3,2},{4,5},{5,4},{6,7},{7,6},{8,9},{9,8},{10,11... | collective-permute-start | bytes 208904 | tf_op jit(solution)/shard_map/ppermute | solution.py:339
  20.9 3.0 %collective-permute-start.14 = (bf16[272,128]{1,0:T(8,128)(2,1)S(1)}, bf16[272,128]{1,0:T(8,128)(2,1)S(1)}, u32[]{:S(2)}, u32[]{:S(2)}) collective-permute-start(bf16[272,128]{1,0:T(8,128)(2,1)S(1)} %collective-permute-done.6.refs_6_), channel_id=1, source_target_pairs={{0,1},{1,0},{2,3},{3,2},{4,5},{5,4},{6,7},{7,6},{8,9},{9,8},{10,11... | collective-permute-start | bytes 208904 | tf_op jit(solution)/shard_map/ppermute | solution.py:339
  21.7 2.1 %collective-permute-start.13 = (bf16[272,128]{1,0:T(8,128)(2,1)S(1)}, bf16[272,128]{1,0:T(8,128)(2,1)S(1)}, u32[]{:S(2)}, u32[]{:S(2)}) collective-permute-start(bf16[272,128]{1,0:T(8,128)(2,1)S(1)} %collective-permute-done.5.refs_5_), channel_id=1, source_target_pairs={{0,1},{1,0},{2,3},{3,2},{4,5},{5,4},{6,7},{7,6},{8,9},{9,8},{10,11... | collective-permute-start | bytes 208904 | tf_op jit(solution)/shard_map/ppermute | solution.py:339
  23.9 1.3 %collective-permute-start.15 = (bf16[272,128]{1,0:T(8,128)(2,1)S(1)}, bf16[272,128]{1,0:T(8,128)(2,1)S(1)}, u32[]{:S(2)}, u32[]{:S(2)}) collective-permute-start(bf16[272,128]{1,0:T(8,128)(2,1)S(1)} %collective-permute-done.7.refs_7_), channel_id=1, source_target_pairs={{0,1},{1,0},{2,3},{3,2},{4,5},{5,4},{6,7},{7,6},{8,9},{9,8},{10,11... | collective-permute-start | bytes 208904 | tf_op jit(solution)/shard_map/ppermute | solution.py:339

commit v3 on v2

--- a/solution.py
+++ b/solution.py
@@ -40,10 +40,10 @@
         self.size = self.total + n_occ
 
 
-def contraction_lists(t, ksym, tab):
-    for i in range(t.n_occ * IRREPS):
-        tab[t.nk + i] = 0
-    for half in range(t.n_occ):
+def contraction_lists(t, ksym, tab, halves):
+    for half in halves:
+        for s in range(IRREPS):
+            tab[t.nk + half * IRREPS + s] = 0
         for i in range(t.own):
             kb = half * t.own + i
             row = half * IRREPS + ksym[kb]
@@ -59,7 +59,7 @@
     width = a_ref.shape[1]
     me = lax.axis_index("occ")
     others = tuple(lax.rem(me + d, t.n_occ) for d in range(1, t.n_occ))
-    contraction_lists(t, ksym, tab)
+    contraction_lists(t, ksym, tab, [me])
 
     def block(row, rank, vb):
         kb = tab[t.kbl + row * own + rank] - me * own
@@ -68,14 +68,13 @@
             pl.ds(pl.multiple_of(vb * BLK, BLK), BLK),
         ]
 
-    def send(vb, places):
-        place0 = places[0]
-        s = vsym[vb]
-        row = me * IRREPS + s
+    total = jnp.int32(0)
+    for vb in range(vblocks):
+        row = me * IRREPS + vsym[vb]
         n = tab[t.nk + row]
 
         @pl.loop(0, n)
-        def _(rank):
+        def _(rank, vb=vb, row=row, place0=total):
             place = place0 + rank
 
             @pl.when(place < first_cap)
@@ -90,14 +89,14 @@
                     block(row, rank, vb), rest.at[place - first_cap], sems.at[place]
                 ).start()
 
-        return (place0 + n,) + tuple(
-            place + tab[t.nk + half * IRREPS + s]
-            for half, place in zip(others, places[1:])
-        )
-
-    totals = lax.fori_loop(0, vblocks, send, (jnp.int32(0),) * t.n_occ)
-    most = totals[0]
-    for other in totals[1:]:
+        total = total + n
+
+    contraction_lists(t, ksym, tab, others)
+    most = total
+    for half in others:
+        other = jnp.int32(0)
+        for vb in range(vblocks):
+            other = other + tab[t.nk + half * IRREPS + vsym[vb]]
         most = jnp.maximum(most, other)
 
     vir = lax.axis_index("vir")
@@ -123,7 +122,7 @@
         (INFO, width), most.astype(jnp.float32), jnp.float32
     ).astype(jnp.bfloat16)
 
-    @pl.loop(0, totals[0])
+    @pl.loop(0, total)
     def _(place):
         pltpu.make_async_copy(
             v_ref.at[pl.ds(0, BLK), pl.ds(0, BLK)], head.at[0], sems.at[place]
@@ -141,7 +140,7 @@
     for fill in fills:
         fill.start()
 
-    contraction_lists(t, ksym, tab)
+    contraction_lists(t, ksym, tab, range(t.n_occ))
     for s in range(IRREPS):
         tab[t.cnt + s] = 0
         for slot in range(MAXO):
@@ -169,43 +168,67 @@
         fill.wait()
 
 
-def each_irrep(t, tab, spare, act):
+def each_irrep(t, tab, act, variants):
     @pl.loop(0, IRREPS)
     def _(s):
         count = tab[t.cnt + s]
-        vbs = [
-            jnp.where(j < count, tab[t.vbl + s * MAXB + j], spare) for j in range(MAXB)
-        ]
-        one = tab[t.slot + s * MAXO] >= 0
-        more = tab[t.slot + s * MAXO + 1] >= 0
-
-        @pl.when((count > 0) & one & jnp.logical_not(more))
-        def _():
-            act(s, BLK, vbs)
-
-        @pl.when((count > 0) & more)
-        def _():
-            act(s, MAXO * BLK, vbs)
-
-
-def multiply(t, tab, half, s, rows, vbs, amp, blocks, acc, places):
-    row = half * IRREPS + s
+        rows = jnp.where(tab[t.slot + s * MAXO] >= 0, BLK, 0)
+        for slot in range(1, MAXO):
+            more = tab[t.slot + s * MAXO + slot] >= 0
+            rows = jnp.where(more, (slot + 1) * BLK, rows)
+        todo = (count > 0) & (rows > 0)
+        for have, width in variants:
+            fits = todo & (rows <= have) & (count <= width)
+
+            @pl.when(fits)
+            def _():
+                act(
+                    s,
+                    have,
+                    [
+                        jnp.where(j < count, tab[t.vbl + s * MAXB + j], -1)
+                        for j in range(width)
+                    ],
+                )
+
+            todo = todo & jnp.logical_not(fits)
+
+
+def multiply(t, tab, halves, s, rows, vbs, amp, sources, acc):
+    bases = [half * IRREPS + s for half in halves]
+    counts = [tab[t.nk + row] for row in bases]
     offs = [
-        jnp.where(
-            vb < t.vblocks,
-            tab[t.off + half * t.vblocks + jnp.minimum(vb, t.vblocks - 1)],
-            0,
-        )
-        for vb in vbs
+        [jnp.where(vb >= 0, tab[t.off + half * t.vblocks + jnp.maximum(vb, 0)], 0) for vb in vbs]
+        for half in halves
     ]
-
-    @pl.loop(0, tab[t.nk + row])
+    steps = counts[0]
+    for count in counts[1:]:
+        steps = jnp.maximum(steps, count)
+
+    def terms(rank):
+        sums = [None] * len(vbs)
+        for row, count, places, source in zip(bases, counts, offs, sources):
+            there = rank < count
+            here = jnp.where(there, rank, 0)
+            kb = jnp.where(there, tab[t.kbl + row * t.own + here], 0)
+            left = amp[kb, :rows, :]
+            for j, place in enumerate(places):
+                part = jnp.dot(
+                    left,
+                    source[jnp.where(there, place + here, 0)],
+                    preferred_element_type=jnp.float32,
+                )
+                part = jnp.where(there, part, 0.0)
+                sums[j] = part if sums[j] is None else sums[j] + part
+        return sums
+
+    for j, part in enumerate(terms(jnp.int32(0))):
+        acc[j, :rows, :] = part
+
+    @pl.loop(1, steps)
     def _(rank):
-        left = amp[tab[t.kbl + row * t.own + rank], :rows, :]
-        for off, place in zip(offs, places):
-            acc[place, :rows, :] += jnp.dot(
-                left, blocks[off + rank], preferred_element_type=jnp.float32
-            )
+        for j, part in enumerate(terms(rank)):
+            acc[j, :rows, :] += part
 
 
 def sort_kernel(masks, *refs):
@@ -224,11 +247,13 @@
 def finish_kernel(t, first_cap, tab, amp, *refs):
     n = t.n_occ
     heads, rests = refs[:n], refs[n : 2 * n]
-    _, out, acc, stage, blocks, sems = refs[2 * n :]
+    _, out, acc, stage, blocks, sent, sems = refs[2 * n :]
     me = lax.axis_index("occ")
     halves = [lax.rem(me - shift + n, n) for shift in range(n)]
 
-    def send(s, slot, vb):
+    sent[0] = 0
+
+    def send(s, slot, vb, index):
         ob = tab[t.slot + s * MAXO + slot]
         return pltpu.make_async_copy(
             stage.at[vb, pl.ds(slot * BLK, BLK)],
@@ -236,23 +261,30 @@
                 pl.ds(pl.multiple_of(ob * BLK, BLK), BLK),
                 pl.ds(pl.multiple_of(vb * BLK, BLK), BLK),
             ],
-            sems.at[vb, slot],
+            sems.at[index],
         )
 
-    def products(sources):
+    def store(s, slot, j, vb):
+        rows = slice(slot * BLK, (slot + 1) * BLK)
+        stage[vb, rows, :] = acc[j, rows, :].astype(jnp.bfloat16)
+        index = sent[0]
+        send(s, slot, vb, index).start()
+        sent[0] = index + 1
+
+    def products(sources, variants):
         def act(s, rows, vbs):
-            acc[:, :rows, :] = jnp.zeros((MAXB, rows, BLK), jnp.float32)
-            for half, source in zip(halves, sources):
-                multiply(t, tab, half, s, rows, vbs, amp, source, acc, range(MAXB))
+            multiply(t, tab, halves, s, rows, vbs, amp, sources, acc)
             for j, vb in enumerate(vbs):
-
-                @pl.when(vb < t.vblocks)
-                def _():
-                    stage[vb, :rows, :] = acc[j, :rows, :].astype(jnp.bfloat16)
-                    for slot in range(rows // BLK):
-                        send(s, slot, vb).start()
-
-        each_irrep(t, tab, t.vblocks, act)
+                for slot in range(rows // BLK):
+
+                    @pl.when((vb >= 0) & (tab[t.slot + s * MAXO + slot] >= 0))
+                    def _():
+                        store(s, slot, j, vb)
+
+        each_irrep(t, tab, act, variants)
+
+    whole = ((MAXO * BLK, MAXB),)
+    usual = ((BLK, 2), (BLK, 3), (BLK, MAXB), (MAXO * BLK, 3)) + whole
 
     most = tab[t.total]
     for half in range(1, n):
@@ -260,24 +292,22 @@
 
     @pl.when(most <= first_cap)
     def _():
-        products(heads)
+        products(heads, usual)
 
     @pl.when(most > first_cap)
     def _():
         for i in range(n):
             blocks[i, :first_cap] = heads[i][...]
             pltpu.sync_copy(rests[i], blocks.at[i, pl.ds(first_cap, blocks.shape[1] - first_cap)])
-        products([blocks.at[i] for i in range(n)])
-
-    def settle(s, rows, vbs):
-        for vb in vbs:
-
-            @pl.when(vb < t.vblocks)
-            def _():
-                for slot in range(rows // BLK):
-                    send(s, slot, vb).wait()
-
-    each_irrep(t, tab, t.vblocks, settle)
+        products([blocks.at[i] for i in range(n)], whole)
+
+    @pl.loop(0, sent[0])
+    def _(index):
+        pltpu.make_async_copy(
+            stage.at[0, pl.ds(0, BLK)],
+            out.at[pl.ds(0, BLK), pl.ds(0, BLK)],
+            sems.at[index],
+        ).wait()
 
 
 def per_device(n_occ, n_vir, amplitudes, integrals, occ_sym, vir_sym, k_sym):
@@ -380,7 +410,8 @@
             pltpu.VMEM((MAXB, MAXO * BLK, BLK), f32),
             pltpu.VMEM((vblocks, MAXO * BLK, BLK), bf16),
             pltpu.VMEM((n_occ, cap, BLK, BLK), bf16),
-            pltpu.SemaphoreType.DMA((vblocks, MAXO)),
+            pltpu.SMEM((1,), i32),
+            pltpu.SemaphoreType.DMA((vblocks * MAXO,)),
         ],
         input_output_aliases={2 + 2 * n_occ: 0},
         compiler_params=pltpu.CompilerParams(vmem_limit_bytes=24 * 2**20),

time: 31.8 us -> 31 us (0.975)
  Pallas kernels: 10.2 us -> 9.69 us
where the time goes in v3:
time: 31 us; the launch traced here: 30.9 us
  starting transfers between devices  13.3 us (43%)
  Pallas kernels  9.69 us (31%)
  waiting for transfers between devices  7.2 us (23%)
  between operations  0.7 us (2%)
    ppermute x15, starting transfers between devices, per_device(): parts = parts + [lax.ppermute(p, 'vir', pairs) for p in parts]  10.4 us
    ppermute x15, waiting for transfers between devices, per_device(): parts = parts + [lax.ppermute(p, 'vir', pairs) for p in parts]  6.06 us
    pallas_call x1, Pallas kernels, per_device(): pl.pallas_call(functools.partial(finish_kernel, t, first_cap), out_shape=...  3.49 us
    ppermute x1, starting transfers between devices, across(): lax.ppermute(x, 'occ', [(i, (i + shift) % n_occ) for i in range(n_occ)])  2.87 us
    pallas_call x1, Pallas kernels, per_device(): pl.pallas_call(functools.partial(pack_kernel, t, first_cap), out_shape=(p...  2.76 us
    pallas_call x1, Pallas kernels, per_device(): pl.pallas_call(functools.partial(plan_kernel, t), out_shape=(pltpu.HBM((o...  2.73 us
    ppermute x1, waiting for transfers between devices, across(): lax.ppermute(x, 'occ', [(i, (i + shift) % n_occ) for i in range(n_occ)])  1.13 us
    pallas_call x1, Pallas kernels, per_device(): pl.pallas_call(functools.partial(sort_kernel, tuple(masks)), out_shape=(p...  0.71 us
  transfers between devices with their start and end apart: 16, of which 6 were waited for; matrix products, arithmetic and copies ran while one was open for 0% of the time, Pallas kernels for 11%

profile of v3, /device:TPU:0, one launch (start us, length us, event | category | flops | bytes accessed | tf_op | source)
XLA Modules:
  0.0 30.9 jit_solution(14877879465288396496)
XLA Ops:
  0.0 2.8 %pack.1 = (bf16[30,128,128]{2,1,0:T(8,128)(2,1)S(1)}, bf16[10,128,128]{2,1,0:T(8,128)(2,1)S(1)}, bf16[272,128]{1,0:T(8,128)(2,1)S(1)}) custom-call(s32[16]{0:T(128)} %ksym.3, s32[20]{0:T(128)} %vsym.3, s32[6]{0:T(128)} %osym.3, bf16[1024,2560]{1,0:T(8,128)(2,1)} %v_ref.1, bf16[768,128]{1,0:T(8,128)(2,1)} %a_ref.1), custom_call_target="tpu_custom_call" | custom-call | tf_op jit(solution)/shard_map/pack/pallas_call | solution.py:324
  2.8 2.9 %collective-permute-start.16 = (bf16[30,128,128]{2,1,0:T(8,128)(2,1)S(1)}, bf16[30,128,128]{2,1,0:T(8,128)(2,1)S(1)}, u32[]{:S(2)}, u32[]{:S(2)}) collective-permute-start(bf16[30,128,128]{2,1,0:T(8,128)(2,1)S(1)} %get-tuple-element.25.refs_0_), channel_id=1, source_target_pairs={{0,16},{16,0},{1,17},{17,1},{2,18},{18,2},{3,19},{19,3},{4,20},{20... | collective-permute-start | bytes 2949128 | tf_op jit(solution)/shard_map/ppermute | solution.py:357
  5.6 2.7 %collective-permute-start.1 = (bf16[272,128]{1,0:T(8,128)(2,1)S(1)}, bf16[272,128]{1,0:T(8,128)(2,1)S(1)}, u32[]{:S(2)}, u32[]{:S(2)}) collective-permute-start(bf16[272,128]{1,0:T(8,128)(2,1)S(1)} %get-tuple-element.20.after.refs_0_), channel_id=1, source_target_pairs={{0,8},{1,9},{2,10},{3,11},{4,12},{5,13},{6,14},{7,15},{8,0},{9,1},... | collective-permute-start | bytes 208904 | tf_op jit(solution)/shard_map/ppermute | solution.py:369
  8.3 1.4 %collective-permute-start.4 = (bf16[272,128]{1,0:T(8,128)(2,1)S(1)}, bf16[272,128]{1,0:T(8,128)(2,1)S(1)}, u32[]{:S(2)}, u32[]{:S(2)}) collective-permute-start(bf16[272,128]{1,0:T(8,128)(2,1)S(1)} %get-tuple-element.20.after.refs_0_), channel_id=1, source_target_pairs={{0,2},{1,3},{2,0},{3,1},{4,6},{5,7},{6,4},{7,5},{8,10},{9,11},{10,... | collective-permute-start | bytes 208904 | tf_op jit(solution)/shard_map/ppermute | solution.py:369
  9.8 1.6 %collective-permute-start.2 = (bf16[272,128]{1,0:T(8,128)(2,1)S(1)}, bf16[272,128]{1,0:T(8,128)(2,1)S(1)}, u32[]{:S(2)}, u32[]{:S(2)}) collective-permute-start(bf16[272,128]{1,0:T(8,128)(2,1)S(1)} %get-tuple-element.20.after.refs_0_), channel_id=1, source_target_pairs={{0,4},{1,5},{2,6},{3,7},{4,0},{5,1},{6,2},{7,3},{8,12},{9,13},{10,... | collective-permute-start | bytes 208904 | tf_op jit(solution)/shard_map/ppermute | solution.py:369
  11.4 0.0 collective-permute-start.8
  11.4 2.7 %plan.1 = (bf16[768,2560]{1,0:T(8,128)(2,1)}, s32[250]{0:T(256)S(4)}, bf16[10,128,128]{2,1,0:T(8,128)(2,1)}) custom-call(s32[16]{0:T(128)} %ksym.3, s32[20]{0:T(128)} %vsym.3, s32[6]{0:T(128)} %osym.3, bf16[272,128]{1,0:T(8,128)(2,1)S(1)} %get-tuple-element.20.after.refs_0_), custom_call_target="tpu_custom_call" | custom-call | tf_op jit(solution)/shard_map/plan/pallas_call | solution.py:340
  14.1 0.0 collective-permute-done.1.refs_1_
  14.1 0.6 %collective-permute-start.12 = (bf16[272,128]{1,0:T(8,128)(2,1)S(1)}, bf16[272,128]{1,0:T(8,128)(2,1)S(1)}, u32[]{:S(2)}, u32[]{:S(2)}) collective-permute-start(bf16[272,128]{1,0:T(8,128)(2,1)S(1)} %collective-permute-done.4.refs_4_), channel_id=1, source_target_pairs={{0,1},{1,0},{2,3},{3,2},{4,5},{5,4},{6,7},{7,6},{8,9},{9,8},{10,11... | collective-permute-start | bytes 208904 | tf_op jit(solution)/shard_map/ppermute | solution.py:369
  14.7 0.0 collective-permute-done.2.refs_2_
  14.7 0.1 collective-permute-start.10
  14.8 0.9 %collective-permute-start.3 = (bf16[272,128]{1,0:T(8,128)(2,1)S(1)}, bf16[272,128]{1,0:T(8,128)(2,1)S(1)}, u32[]{:S(2)}, u32[]{:S(2)}) collective-permute-start(bf16[272,128]{1,0:T(8,128)(2,1)S(1)} %collective-permute-done.1.refs_1_), channel_id=1, source_target_pairs={{0,4},{1,5},{2,6},{3,7},{4,0},{5,1},{6,2},{7,3},{8,12},{9,13},{10,... | collective-permute-start | bytes 208904 | tf_op jit(solution)/shard_map/ppermute | solution.py:369
  15.7 0.5 %collective-permute-start.6 = (bf16[272,128]{1,0:T(8,128)(2,1)S(1)}, bf16[272,128]{1,0:T(8,128)(2,1)S(1)}, u32[]{:S(2)}, u32[]{:S(2)}) collective-permute-start(bf16[272,128]{1,0:T(8,128)(2,1)S(1)} %collective-permute-done.2.refs_2_), channel_id=1, source_target_pairs={{0,2},{1,3},{2,0},{3,1},{4,6},{5,7},{6,4},{7,5},{8,10},{9,11},{10,... | collective-permute-start | bytes 208904 | tf_op jit(solution)/shard_map/ppermute | solution.py:369
  16.2 0.0 collective-permute-done.12.refs_12_
  16.2 0.0 collective-permute-start.9
  16.2 0.0 collective-permute-done.10.refs_10_
  16.2 1.6 %collective-permute-start.5 = (bf16[272,128]{1,0:T(8,128)(2,1)S(1)}, bf16[272,128]{1,0:T(8,128)(2,1)S(1)}, u32[]{:S(2)}, u32[]{:S(2)}) collective-permute-start(bf16[272,128]{1,0:T(8,128)(2,1)S(1)} %collective-permute-done.1.refs_1_), channel_id=1, source_target_pairs={{0,2},{1,3},{2,0},{3,1},{4,6},{5,7},{6,4},{7,5},{8,10},{9,11},{10,... | collective-permute-start | bytes 208904 | tf_op jit(solution)/shard_map/ppermute | solution.py:369
  17.8 1.5 %collective-permute-done.3.refs_3_ = bf16[272,128]{1,0:T(8,128)(2,1)S(1)} collective-permute-done((bf16[272,128]{1,0:T(8,128)(2,1)S(1)}, bf16[272,128]{1,0:T(8,128)(2,1)S(1)}, u32[]{:S(2)}, u32[]{:S(2)}) %collective-permute-start.3) | collective-permute-done | bytes 69664 | tf_op jit(solution)/shard_map/ppermute | solution.py:369
  19.3 0.5 %collective-permute-start.7 = (bf16[272,128]{1,0:T(8,128)(2,1)S(1)}, bf16[272,128]{1,0:T(8,128)(2,1)S(1)}, u32[]{:S(2)}, u32[]{:S(2)}) collective-permute-start(bf16[272,128]{1,0:T(8,128)(2,1)S(1)} %collective-permute-done.3.refs_3_), channel_id=1, source_target_pairs={{0,2},{1,3},{2,0},{3,1},{4,6},{5,7},{6,4},{7,5},{8,10},{9,11},{10,... | collective-permute-start | bytes 208904 | tf_op jit(solution)/shard_map/ppermute | solution.py:369
  19.8 0.8 %collective-permute-done.6.refs_6_ = bf16[272,128]{1,0:T(8,128)(2,1)S(1)} collective-permute-done((bf16[272,128]{1,0:T(8,128)(2,1)S(1)}, bf16[272,128]{1,0:T(8,128)(2,1)S(1)}, u32[]{:S(2)}, u32[]{:S(2)}) %collective-permute-start.6) | collective-permute-done | bytes 69664 | tf_op jit(solution)/shard_map/ppermute | solution.py:369
  20.7 0.0 collective-permute-start.11
  20.7 0.5 %collective-permute-start.14 = (bf16[272,128]{1,0:T(8,128)(2,1)S(1)}, bf16[272,128]{1,0:T(8,128)(2,1)S(1)}, u32[]{:S(2)}, u32[]{:S(2)}) collective-permute-start(bf16[272,128]{1,0:T(8,128)(2,1)S(1)} %collective-permute-done.6.refs_6_), channel_id=1, source_target_pairs={{0,1},{1,0},{2,3},{3,2},{4,5},{5,4},{6,7},{7,6},{8,9},{9,8},{10,11... | collective-permute-start | bytes 208904 | tf_op jit(solution)/shard_map/ppermute | solution.py:369
  21.2 0.3 collective-permute-done.5.refs_5_
  21.5 0.0 collective-permute-start.13
  21.5 2.1 %collective-permute-done.7.refs_7_ = bf16[272,128]{1,0:T(8,128)(2,1)S(1)} collective-permute-done((bf16[272,128]{1,0:T(8,128)(2,1)S(1)}, bf16[272,128]{1,0:T(8,128)(2,1)S(1)}, u32[]{:S(2)}, u32[]{:S(2)}) %collective-permute-start.7) | collective-permute-done | bytes 69664 | tf_op jit(solution)/shard_map/ppermute | solution.py:369
  23.6 0.0 collective-permute-start.15
  23.6 0.0 collective-permute-done.14.refs_14_
  23.6 0.0 collective-permute-done.13.refs_13_
  23.6 1.2 %collective-permute-done.15.refs_15_ = bf16[272,128]{1,0:T(8,128)(2,1)S(1)} collective-permute-done((bf16[272,128]{1,0:T(8,128)(2,1)S(1)}, bf16[272,128]{1,0:T(8,128)(2,1)S(1)}, u32[]{:S(2)}, u32[]{:S(2)}) %collective-permute-start.15) | collective-permute-done | bytes 69664 | tf_op jit(solution)/shard_map/ppermute | solution.py:369
  24.9 0.7 %sort.1 = (bf16[16,256,128]{2,1,0:T(8,128)(2,1)S(1)}, s32[1]{0:T(128)}) custom-call(bf16[272,128]{1,0:T(8,128)(2,1)S(1)} %get-tuple-element.20.after.refs_0_, bf16[272,128]{1,0:T(8,128)(2,1)S(1)} %collective-permute-done.1.refs_1_, bf16[272,128]{1,0:T(8,128)(2,1)S(1)} %collective-permute-done.2.refs_2_, bf16[272,128]{1,0:T(8,128)(2,1)S(1)} %collective-permute-done.3.refs_3_, ...), custom_call_target="tpu_custom_call" | custom-call | tf_op jit(solution)/shard_map/sort/pallas_call | solution.py:384
  26.2 1.1 %collective-permute-done.16.refs_1_ = bf16[30,128,128]{2,1,0:T(8,128)(2,1)S(1)} collective-permute-done((bf16[30,128,128]{2,1,0:T(8,128)(2,1)S(1)}, bf16[30,128,128]{2,1,0:T(8,128)(2,1)S(1)}, u32[]{:S(2)}, u32[]{:S(2)}) %collective-permute-start.16) | collective-permute-done | bytes 983072 | tf_op jit(solution)/shard_map/ppermute | solution.py:357
  27.4 3.5 %finish.1 = bf16[768,2560]{1,0:T(8,128)(2,1)} custom-call(s32[250]{0:T(256)S(4)} %get-tuple-element.21.tab, bf16[16,256,128]{2,1,0:T(8,128)(2,1)S(1)} %get-tuple-element.24.amp, bf16[30,128,128]{2,1,0:T(8,128)(2,1)S(1)} %get-tuple-element.25.refs_0_, bf16[30,128,128]{2,1,0:T(8,128)(2,1)S(1)} %collective-permute-done.16.refs_1_, ...), custom_call_target="tpu_custom_call", output_to_operand_aliasing={{}: (6, {})} | custom-call | tf_op jit(solution)/shard_map/finish/pallas_call | solution.py:404
  (5 shorter events, 0.0 us)
Async XLA Ops:
  2.8 24.6 %collective-permute-start.16 = (bf16[30,128,128]{2,1,0:T(8,128)(2,1)S(1)}, bf16[30,128,128]{2,1,0:T(8,128)(2,1)S(1)}, u32[]{:S(2)}, u32[]{:S(2)}) collective-permute-start(bf16[30,128,128]{2,1,0:T(8,128)(2,1)S(1)} %get-tuple-element.25.refs_0_), channel_id=1, source_target_pairs={{0,16},{16,0},{1,17},{17,1},{2,18},{18,2},{3,19},{19,3},{4,20},{20... | collective-permute-start | bytes 2949128 | tf_op jit(solution)/shard_map/ppermute | solution.py:357
  5.6 8.5 %collective-permute-start.1 = (bf16[272,128]{1,0:T(8,128)(2,1)S(1)}, bf16[272,128]{1,0:T(8,128)(2,1)S(1)}, u32[]{:S(2)}, u32[]{:S(2)}) collective-permute-start(bf16[272,128]{1,0:T(8,128)(2,1)S(1)} %get-tuple-element.20.after.refs_0_), channel_id=1, source_target_pairs={{0,8},{1,9},{2,10},{3,11},{4,12},{5,13},{6,14},{7,15},{8,0},{9,1},... | collective-permute-start | bytes 208904 | tf_op jit(solution)/shard_map/ppermute | solution.py:369
  8.3 5.8 %collective-permute-start.4 = (bf16[272,128]{1,0:T(8,128)(2,1)S(1)}, bf16[272,128]{1,0:T(8,128)(2,1)S(1)}, u32[]{:S(2)}, u32[]{:S(2)}) collective-permute-start(bf16[272,128]{1,0:T(8,128)(2,1)S(1)} %get-tuple-element.20.after.refs_0_), channel_id=1, source_target_pairs={{0,2},{1,3},{2,0},{3,1},{4,6},{5,7},{6,4},{7,5},{8,10},{9,11},{10,... | collective-permute-start | bytes 208904 | tf_op jit(solution)/shard_map/ppermute | solution.py:369
  9.8 4.9 %collective-permute-start.2 = (bf16[272,128]{1,0:T(8,128)(2,1)S(1)}, bf16[272,128]{1,0:T(8,128)(2,1)S(1)}, u32[]{:S(2)}, u32[]{:S(2)}) collective-permute-start(bf16[272,128]{1,0:T(8,128)(2,1)S(1)} %get-tuple-element.20.after.refs_0_), channel_id=1, source_target_pairs={{0,4},{1,5},{2,6},{3,7},{4,0},{5,1},{6,2},{7,3},{8,12},{9,13},{10,... | collective-permute-start | bytes 208904 | tf_op jit(solution)/shard_map/ppermute | solution.py:369
  11.4 4.3 %collective-permute-start.8 = (bf16[272,128]{1,0:T(8,128)(2,1)S(1)}, bf16[272,128]{1,0:T(8,128)(2,1)S(1)}, u32[]{:S(2)}, u32[]{:S(2)}) collective-permute-start(bf16[272,128]{1,0:T(8,128)(2,1)S(1)} %get-tuple-element.20.after.refs_0_), channel_id=1, source_target_pairs={{0,1},{1,0},{2,3},{3,2},{4,5},{5,4},{6,7},{7,6},{8,9},{9,8},{10,11... | collective-permute-start | bytes 208904 | tf_op jit(solution)/shard_map/ppermute | solution.py:369
  14.1 2.1 %collective-permute-start.12 = (bf16[272,128]{1,0:T(8,128)(2,1)S(1)}, bf16[272,128]{1,0:T(8,128)(2,1)S(1)}, u32[]{:S(2)}, u32[]{:S(2)}) collective-permute-start(bf16[272,128]{1,0:T(8,128)(2,1)S(1)} %collective-permute-done.4.refs_4_), channel_id=1, source_target_pairs={{0,1},{1,0},{2,3},{3,2},{4,5},{5,4},{6,7},{7,6},{8,9},{9,8},{10,11... | collective-permute-start | bytes 208904 | tf_op jit(solution)/shard_map/ppermute | solution.py:369
  14.7 1.5 %collective-permute-start.10 = (bf16[272,128]{1,0:T(8,128)(2,1)S(1)}, bf16[272,128]{1,0:T(8,128)(2,1)S(1)}, u32[]{:S(2)}, u32[]{:S(2)}) collective-permute-start(bf16[272,128]{1,0:T(8,128)(2,1)S(1)} %collective-permute-done.2.refs_2_), channel_id=1, source_target_pairs={{0,1},{1,0},{2,3},{3,2},{4,5},{5,4},{6,7},{7,6},{8,9},{9,8},{10,11... | collective-permute-start | bytes 208904 | tf_op jit(solution)/shard_map/ppermute | solution.py:369
  14.8 4.5 %collective-permute-start.3 = (bf16[272,128]{1,0:T(8,128)(2,1)S(1)}, bf16[272,128]{1,0:T(8,128)(2,1)S(1)}, u32[]{:S(2)}, u32[]{:S(2)}) collective-permute-start(bf16[272,128]{1,0:T(8,128)(2,1)S(1)} %collective-permute-done.1.refs_1_), channel_id=1, source_target_pairs={{0,4},{1,5},{2,6},{3,7},{4,0},{5,1},{6,2},{7,3},{8,12},{9,13},{10,... | collective-permute-start | bytes 208904 | tf_op jit(solution)/shard_map/ppermute | solution.py:369
  15.7 5.0 %collective-permute-start.6 = (bf16[272,128]{1,0:T(8,128)(2,1)S(1)}, bf16[272,128]{1,0:T(8,128)(2,1)S(1)}, u32[]{:S(2)}, u32[]{:S(2)}) collective-permute-start(bf16[272,128]{1,0:T(8,128)(2,1)S(1)} %collective-permute-done.2.refs_2_), channel_id=1, source_target_pairs={{0,2},{1,3},{2,0},{3,1},{4,6},{5,7},{6,4},{7,5},{8,10},{9,11},{10,... | collective-permute-start | bytes 208904 | tf_op jit(solution)/shard_map/ppermute | solution.py:369
  16.2 4.5 %collective-permute-start.9 = (bf16[272,128]{1,0:T(8,128)(2,1)S(1)}, bf16[272,128]{1,0:T(8,128)(2,1)S(1)}, u32[]{:S(2)}, u32[]{:S(2)}) collective-permute-start(bf16[272,128]{1,0:T(8,128)(2,1)S(1)} %collective-permute-done.1.refs_1_), channel_id=1, source_target_pairs={{0,1},{1,0},{2,3},{3,2},{4,5},{5,4},{6,7},{7,6},{8,9},{9,8},{10,11... | collective-permute-start | bytes 208904 | tf_op jit(solution)/shard_map/ppermute | solution.py:369
  16.2 5.3 %collective-permute-start.5 = (bf16[272,128]{1,0:T(8,128)(2,1)S(1)}, bf16[272,128]{1,0:T(8,128)(2,1)S(1)}, u32[]{:S(2)}, u32[]{:S(2)}) collective-permute-start(bf16[272,128]{1,0:T(8,128)(2,1)S(1)} %collective-permute-done.1.refs_1_), channel_id=1, source_target_pairs={{0,2},{1,3},{2,0},{3,1},{4,6},{5,7},{6,4},{7,5},{8,10},{9,11},{10,... | collective-permute-start | bytes 208904 | tf_op jit(solution)/shard_map/ppermute | solution.py:369
  19.3 4.3 %collective-permute-start.7 = (bf16[272,128]{1,0:T(8,128)(2,1)S(1)}, bf16[272,128]{1,0:T(8,128)(2,1)S(1)}, u32[]{:S(2)}, u32[]{:S(2)}) collective-permute-start(bf16[272,128]{1,0:T(8,128)(2,1)S(1)} %collective-permute-done.3.refs_3_), channel_id=1, source_target_pairs={{0,2},{1,3},{2,0},{3,1},{4,6},{5,7},{6,4},{7,5},{8,10},{9,11},{10,... | collective-permute-start | bytes 208904 | tf_op jit(solution)/shard_map/ppermute | solution.py:369
  20.7 3.0 %collective-permute-start.11 = (bf16[272,128]{1,0:T(8,128)(2,1)S(1)}, bf16[272,128]{1,0:T(8,128)(2,1)S(1)}, u32[]{:S(2)}, u32[]{:S(2)}) collective-permute-start(bf16[272,128]{1,0:T(8,128)(2,1)S(1)} %collective-permute-done.3.refs_3_), channel_id=1, source_target_pairs={{0,1},{1,0},{2,3},{3,2},{4,5},{5,4},{6,7},{7,6},{8,9},{9,8},{10,11... | collective-permute-start | bytes 208904 | tf_op jit(solution)/shard_map/ppermute | solution.py:369
  20.7 3.0 %collective-permute-start.14 = (bf16[272,128]{1,0:T(8,128)(2,1)S(1)}, bf16[272,128]{1,0:T(8,128)(2,1)S(1)}, u32[]{:S(2)}, u32[]{:S(2)}) collective-permute-start(bf16[272,128]{1,0:T(8,128)(2,1)S(1)} %collective-permute-done.6.refs_6_), channel_id=1, source_target_pairs={{0,1},{1,0},{2,3},{3,2},{4,5},{5,4},{6,7},{7,6},{8,9},{9,8},{10,11... | collective-permute-start | bytes 208904 | tf_op jit(solution)/shard_map/ppermute | solution.py:369
  21.5 2.1 %collective-permute-start.13 = (bf16[272,128]{1,0:T(8,128)(2,1)S(1)}, bf16[272,128]{1,0:T(8,128)(2,1)S(1)}, u32[]{:S(2)}, u32[]{:S(2)}) collective-permute-start(bf16[272,128]{1,0:T(8,128)(2,1)S(1)} %collective-permute-done.5.refs_5_), channel_id=1, source_target_pairs={{0,1},{1,0},{2,3},{3,2},{4,5},{5,4},{6,7},{7,6},{8,9},{9,8},{10,11... | collective-permute-start | bytes 208904 | tf_op jit(solution)/shard_map/ppermute | solution.py:369
  23.6 1.3 %collective-permute-start.15 = (bf16[272,128]{1,0:T(8,128)(2,1)S(1)}, bf16[272,128]{1,0:T(8,128)(2,1)S(1)}, u32[]{:S(2)}, u32[]{:S(2)}) collective-permute-start(bf16[272,128]{1,0:T(8,128)(2,1)S(1)} %collective-permute-done.7.refs_7_), channel_id=1, source_target_pairs={{0,1},{1,0},{2,3},{3,2},{4,5},{5,4},{6,7},{7,6},{8,9},{9,8},{10,11... | collective-permute-start | bytes 208904 | tf_op jit(solution)/shard_map/ppermute | solution.py:369

commit v4 on v3

--- a/solution.py
+++ b/solution.py
@@ -52,9 +52,8 @@
             tab[t.nk + row] = rank + 1
 
 
-def pack_kernel(
-    t, first_cap, ksym, vsym, osym, v_ref, a_ref, head, rest, pay, tab, sems
-):
+def pack_kernel(t, chunks, ksym, vsym, osym, v_ref, a_ref, *refs):
+    packed, (pay, tab, sems) = refs[: len(chunks)], refs[len(chunks) :]
     own, vblocks, oblocks = t.own, t.vblocks, osym.shape[0]
     width = a_ref.shape[1]
     me = lax.axis_index("occ")
@@ -77,17 +76,25 @@
         def _(rank, vb=vb, row=row, place0=total):
             place = place0 + rank
 
-            @pl.when(place < first_cap)
+            def start(chunk, place0):
+                pltpu.make_async_copy(
+                    block(row, rank, vb), chunk.at[place - place0], sems.at[place]
+                ).start()
+
+            @pl.when(place < chunks[0])
             def _():
-                pltpu.make_async_copy(
-                    block(row, rank, vb), head.at[place], sems.at[place]
-                ).start()
-
-            @pl.when(place >= first_cap)
+                start(packed[0], 0)
+
+            @pl.when(place >= chunks[0])
             def _():
-                pltpu.make_async_copy(
-                    block(row, rank, vb), rest.at[place - first_cap], sems.at[place]
-                ).start()
+                place0 = chunks[0]
+                for size, chunk in zip(chunks[1:], packed[1:]):
+
+                    @pl.when((place >= place0) & (place < place0 + size))
+                    def _(chunk=chunk, place0=place0):
+                        start(chunk, place0)
+
+                    place0 += size
 
         total = total + n
 
@@ -125,7 +132,7 @@
     @pl.loop(0, total)
     def _(place):
         pltpu.make_async_copy(
-            v_ref.at[pl.ds(0, BLK), pl.ds(0, BLK)], head.at[0], sems.at[place]
+            v_ref.at[pl.ds(0, BLK), pl.ds(0, BLK)], packed[0].at[0], sems.at[place]
         ).wait()
 
 
@@ -244,10 +251,10 @@
     most[0] = jnp.max(peak).astype(jnp.int32)
 
 
-def finish_kernel(t, first_cap, tab, amp, *refs):
+def finish_kernel(t, chunks, tab, amp, *refs):
     n = t.n_occ
-    heads, rests = refs[:n], refs[n : 2 * n]
-    _, out, acc, stage, blocks, sent, sems = refs[2 * n :]
+    heads, rests = refs[:n], refs[n : n * len(chunks)]
+    _, out, acc, stage, blocks, sent, sems, load_sems = refs[n * len(chunks) :]
     me = lax.axis_index("occ")
     halves = [lax.rem(me - shift + n, n) for shift in range(n)]
 
@@ -290,16 +297,34 @@
     for half in range(1, n):
         most = jnp.maximum(most, tab[t.total + half])
 
-    @pl.when(most <= first_cap)
+    @pl.when(most <= chunks[0])
     def _():
         products(heads, usual)
 
-    @pl.when(most > first_cap)
+    @pl.when(most > chunks[0])
     def _():
+        def load(act):
+            place = chunks[0]
+            for c, size in enumerate(chunks[1:]):
+
+                @pl.when(most > place)
+                def _(c=c, size=size, place=place):
+                    for i in range(n):
+                        act(
+                            pltpu.make_async_copy(
+                                rests[c * n + i],
+                                blocks.at[i, pl.ds(place, size)],
+                                load_sems.at[c * n + i],
+                            )
+                        )
+
+                place += size
+
+        load(lambda copy: copy.start())
         for i in range(n):
-            blocks[i, :first_cap] = heads[i][...]
-            pltpu.sync_copy(rests[i], blocks.at[i, pl.ds(first_cap, blocks.shape[1] - first_cap)])
-        products([blocks.at[i] for i in range(n)], whole)
+            blocks[i, : chunks[0]] = heads[i][...]
+        load(lambda copy: copy.wait())
+        products([blocks.at[i] for i in range(n)], usual)
 
     @pl.loop(0, sent[0])
     def _(index):
@@ -317,19 +342,18 @@
     cols = vblocks * BLK
     t = Table(n_occ, kblocks, vblocks)
     cap = t.own * MAXB
-    first_cap = (cap * 3 + 3) // 4
+    first_cap = (cap * 27 + 39) // 40
+    more_cap = (cap - first_cap) // 3
+    chunks = tuple(c for c in (first_cap, more_cap, cap - first_cap - more_cap) if c)
     rows = MAXO * BLK + INFO
     bf16, f32, i32 = jnp.bfloat16, jnp.float32, jnp.int32
 
-    head, rest, pay = pl.pallas_call(
-        functools.partial(pack_kernel, t, first_cap),
-        out_shape=(
-            pltpu.VMEM((first_cap, BLK, BLK), bf16),
-            pltpu.VMEM((cap - first_cap, BLK, BLK), bf16),
-            pltpu.VMEM((rows, width), bf16),
-        ),
+    *packed, pay = pl.pallas_call(
+        functools.partial(pack_kernel, t, chunks),
+        out_shape=tuple(pltpu.VMEM((c, BLK, BLK), bf16) for c in chunks)
+        + (pltpu.VMEM((rows, width), bf16),),
         in_specs=[SMEM, SMEM, SMEM, HBM, VMEM],
-        out_specs=(VMEM, VMEM, VMEM),
+        out_specs=(VMEM,) * (len(chunks) + 1),
         scratch_shapes=[
             pltpu.SMEM((t.size,), i32),
             pltpu.SemaphoreType.DMA((cap,)),
@@ -340,9 +364,11 @@
     zero_out, tab, *spares = pl.pallas_call(
         functools.partial(plan_kernel, t),
         out_shape=(pltpu.HBM((occ_rows, cols), bf16), pltpu.SMEM((t.size,), i32))
-        + (pltpu.HBM((cap - first_cap, BLK, BLK), bf16),) * (n_occ - 1),
+        + tuple(
+            pltpu.HBM((c, BLK, BLK), bf16) for c in chunks[1:] for _ in range(n_occ - 1)
+        ),
         in_specs=[SMEM, SMEM, SMEM, ANY],
-        out_specs=(HBM, SMEM) + (HBM,) * (n_occ - 1),
+        out_specs=(HBM, SMEM) + (HBM,) * ((n_occ - 1) * (len(chunks) - 1)),
         scratch_shapes=[
             pltpu.VMEM((BLK, cols), bf16),
             pltpu.SemaphoreType.DMA((occ_rows // BLK,)),
@@ -356,7 +382,7 @@
     def across(x, shift):
         return lax.ppermute(x, "occ", [(i, (i + shift) % n_occ) for i in range(n_occ)])
 
-    heads = [across(head, shift) for shift in shifts]
+    heads = [across(packed[0], shift) for shift in shifts]
 
     bits = [1 << b for b in range(n_vir.bit_length() - 1)][::-1]
     masks = [0]
@@ -367,8 +393,8 @@
         for bit in bits:
             pairs = [(i, i ^ bit) for i in range(n_vir)]
             parts = parts + [lax.ppermute(p, "vir", pairs) for p in parts]
-            if len(parts) == 2:
-                parts[1], zero_out = lax.optimization_barrier((parts[1], zero_out))
+            if len(parts) == 8:
+                parts[5], zero_out = lax.optimization_barrier((parts[5], zero_out))
     else:
         whole = pay[None]
         for bit in bits:
@@ -393,18 +419,27 @@
         name="sort",
     )(*parts)
 
-    rests = lax.cond(
-        most[0] > first_cap,
-        lambda x, spares: [across(x, shift) for shift in shifts],
-        lambda x, spares: spares,
-        rest,
-        spares,
-    )
-    heads, rests = [head] + heads, [rest] + rests
+    n = len(shifts)
+    spares = [spares[c * n : (c + 1) * n] for c in range(len(chunks) - 1)]
+
+    def more(level, place, operands):
+        if level == len(chunks):
+            return []
+        return lax.cond(
+            most[0] > place,
+            lambda packed, spares: [[across(packed[0], shift) for shift in shifts]]
+            + more(level + 1, place + chunks[level], (packed[1:], spares[1:])),
+            lambda packed, spares: list(spares),
+            *operands,
+        )
+
+    rests = more(1, first_cap, (packed[1:], spares))
+    heads = [packed[0]] + heads
+    rests = [x for own, others in zip(packed[1:], rests) for x in [own, *others]]
     return pl.pallas_call(
-        functools.partial(finish_kernel, t, first_cap),
+        functools.partial(finish_kernel, t, chunks),
         out_shape=jax.ShapeDtypeStruct((occ_rows, cols), bf16),
-        in_specs=[SMEM] + [VMEM] * (1 + n_occ) + [ANY] * n_occ + [HBM],
+        in_specs=[SMEM] + [VMEM] * (1 + n_occ) + [ANY] * len(rests) + [HBM],
         out_specs=HBM,
         scratch_shapes=[
             pltpu.VMEM((MAXB, MAXO * BLK, BLK), f32),
@@ -412,8 +447,9 @@
             pltpu.VMEM((n_occ, cap, BLK, BLK), bf16),
             pltpu.SMEM((1,), i32),
             pltpu.SemaphoreType.DMA((vblocks * MAXO,)),
+            pltpu.SemaphoreType.DMA((max(len(rests), 1),)),
         ],
-        input_output_aliases={2 + 2 * n_occ: 0},
+        input_output_aliases={2 + n_occ + len(rests): 0},
         compiler_params=pltpu.CompilerParams(vmem_limit_bytes=24 * 2**20),
         name="finish",
     )(tab, *[here(x) for x in (amp, *heads)], *rests, zero_out)

time: 31 us -> 29 us (0.935)
  waiting for transfers between devices: 7.2 us -> 2.55 us
  starting transfers between devices: 13.3 us -> 15.9 us
    ppermute x15, waiting for transfers between devices: 6.06 us -> 2.34 us  [per_device(): parts = parts + [lax.ppermute(p, 'vir', pairs) for p in parts]]
    ppermute x15, starting transfers between devices: 10.4 us -> 13 us  [per_device(): parts = parts + [lax.ppermute(p, 'vir', pairs) for p in parts]]
    ppermute x1, waiting for transfers between devices: 1.13 us -> 0.21 us  [across(): lax.ppermute(x, 'occ', [(i, (i + shift) % n_occ) for i in range(n_occ)])]
  transfers between devices with their start and end apart: 16 -> 16, of which waited for: 6 -> 6; matrix products, arithmetic and copies ran while one was open for 0% -> 0% of each run, Pallas kernels for 11% -> 12%
where the time goes in v4:
time: 29 us; the launch traced here: 28.6 us
  starting transfers between devices  15.9 us (55%)
  Pallas kernels  9.47 us (33%)
  waiting for transfers between devices  2.55 us (9%)
  between operations  0.71 us (2%)
    ppermute x15, starting transfers between devices, per_device(): parts = parts + [lax.ppermute(p, 'vir', pairs) for p in parts]  13 us
    pallas_call x1, Pallas kernels, per_device(): pl.pallas_call(functools.partial(finish_kernel, t, chunks), out_shape=jax...  3.16 us
    ppermute x1, starting transfers between devices, across(): lax.ppermute(x, 'occ', [(i, (i + shift) % n_occ) for i in range(n_occ)])  2.88 us
    pallas_call x1, Pallas kernels, per_device(): pl.pallas_call(functools.partial(pack_kernel, t, chunks), out_shape=tuple...  2.87 us
    pallas_call x1, Pallas kernels, per_device(): pl.pallas_call(functools.partial(plan_kernel, t), out_shape=(pltpu.HBM((o...  2.73 us
    ppermute x15, waiting for transfers between devices, per_device(): parts = parts + [lax.ppermute(p, 'vir', pairs) for p in parts]  2.34 us
    pallas_call x1, Pallas kernels, per_device(): pl.pallas_call(functools.partial(sort_kernel, tuple(masks)), out_shape=(p...  0.71 us
  transfers between devices with their start and end apart: 16, of which 6 were waited for; matrix products, arithmetic and copies ran while one was open for 0% of the time, Pallas kernels for 12%

profile of v4, /device:TPU:0, one launch (start us, length us, event | category | flops | bytes accessed | tf_op | source)
XLA Modules:
  0.0 28.6 jit_solution(1211485493832506733)
XLA Ops:
  0.0 2.9 %pack.1 = (bf16[27,128,128]{2,1,0:T(8,128)(2,1)S(1)}, bf16[4,128,128]{2,1,0:T(8,128)(2,1)S(1)}, bf16[9,128,128]{2,1,0:T(8,128)(2,1)S(1)}, bf16[272,128]{1,0:T(8,128)(2,1)S(1)}) custom-call(s32[16]{0:T(128)} %ksym.3, s32[20]{0:T(128)} %vsym.3, s32[6]{0:T(128)} %osym.3, bf16[1024,2560]{1,0:T(8,128)(2,1)} %v_ref.1, bf16[768,128]{1,0:T(8,128)(2,1)} %a_ref.1), custom_call_target="tpu_custom_call" | custom-call | tf_op jit(solution)/shard_map/pack/pallas_call | solution.py:351
  2.9 2.9 %collective-permute-start.17 = (bf16[27,128,128]{2,1,0:T(8,128)(2,1)S(1)}, bf16[27,128,128]{2,1,0:T(8,128)(2,1)S(1)}, u32[]{:S(2)}, u32[]{:S(2)}) collective-permute-start(bf16[27,128,128]{2,1,0:T(8,128)(2,1)S(1)} %get-tuple-element.45.refs_0_), channel_id=1, source_target_pairs={{0,16},{16,0},{1,17},{17,1},{2,18},{18,2},{3,19},{19,3},{4,20},{20... | collective-permute-start | bytes 2654216 | tf_op jit(solution)/shard_map/ppermute | solution.py:383
  5.8 1.5 %collective-permute-start.5 = (bf16[272,128]{1,0:T(8,128)(2,1)S(1)}, bf16[272,128]{1,0:T(8,128)(2,1)S(1)}, u32[]{:S(2)}, u32[]{:S(2)}) collective-permute-start(bf16[272,128]{1,0:T(8,128)(2,1)S(1)} %get-tuple-element.40.after.refs_0_), channel_id=1, source_target_pairs={{0,2},{1,3},{2,0},{3,1},{4,6},{5,7},{6,4},{7,5},{8,10},{9,11},{10,... | collective-permute-start | bytes 208904 | tf_op jit(solution)/shard_map/ppermute | solution.py:395
  7.3 2.7 %collective-permute-start.2 = (bf16[272,128]{1,0:T(8,128)(2,1)S(1)}, bf16[272,128]{1,0:T(8,128)(2,1)S(1)}, u32[]{:S(2)}, u32[]{:S(2)}) collective-permute-start(bf16[272,128]{1,0:T(8,128)(2,1)S(1)} %get-tuple-element.40.after.refs_0_), channel_id=1, source_target_pairs={{0,8},{1,9},{2,10},{3,11},{4,12},{5,13},{6,14},{7,15},{8,0},{9,1},... | collective-permute-start | bytes 208904 | tf_op jit(solution)/shard_map/ppermute | solution.py:395
  9.9 0.0 collective-permute-start.9
  9.9 1.5 %collective-permute-start.3 = (bf16[272,128]{1,0:T(8,128)(2,1)S(1)}, bf16[272,128]{1,0:T(8,128)(2,1)S(1)}, u32[]{:S(2)}, u32[]{:S(2)}) collective-permute-start(bf16[272,128]{1,0:T(8,128)(2,1)S(1)} %get-tuple-element.40.after.refs_0_), channel_id=1, source_target_pairs={{0,4},{1,5},{2,6},{3,7},{4,0},{5,1},{6,2},{7,3},{8,12},{9,13},{10,... | collective-permute-start | bytes 208904 | tf_op jit(solution)/shard_map/ppermute | solution.py:395
  11.5 0.0 collective-permute-done.5.refs_4_
  11.5 0.2 collective-permute-start.13
  11.7 0.9 %collective-permute-done.2.refs_1_ = bf16[272,128]{1,0:T(8,128)(2,1)S(1)} collective-permute-done((bf16[272,128]{1,0:T(8,128)(2,1)S(1)}, bf16[272,128]{1,0:T(8,128)(2,1)S(1)}, u32[]{:S(2)}, u32[]{:S(2)}) %collective-permute-start.2) | collective-permute-done | bytes 69664 | tf_op jit(solution)/shard_map/ppermute | solution.py:395
  12.6 0.5 %collective-permute-start.6 = (bf16[272,128]{1,0:T(8,128)(2,1)S(1)}, bf16[272,128]{1,0:T(8,128)(2,1)S(1)}, u32[]{:S(2)}, u32[]{:S(2)}) collective-permute-start(bf16[272,128]{1,0:T(8,128)(2,1)S(1)} %collective-permute-done.2.refs_1_), channel_id=1, source_target_pairs={{0,2},{1,3},{2,0},{3,1},{4,6},{5,7},{6,4},{7,5},{8,10},{9,11},{10,... | collective-permute-start | bytes 208904 | tf_op jit(solution)/shard_map/ppermute | solution.py:395
  13.1 0.0 collective-permute-done.9.refs_8_
  13.1 2.2 %collective-permute-start.4 = (bf16[272,128]{1,0:T(8,128)(2,1)S(1)}, bf16[272,128]{1,0:T(8,128)(2,1)S(1)}, u32[]{:S(2)}, u32[]{:S(2)}) collective-permute-start(bf16[272,128]{1,0:T(8,128)(2,1)S(1)} %collective-permute-done.2.refs_1_), channel_id=1, source_target_pairs={{0,4},{1,5},{2,6},{3,7},{4,0},{5,1},{6,2},{7,3},{8,12},{9,13},{10,... | collective-permute-start | bytes 208904 | tf_op jit(solution)/shard_map/ppermute | solution.py:395
  15.3 0.0 collective-permute-done.3.refs_2_
  15.3 0.0 collective-permute-start.11
  15.3 0.0 collective-permute-done.13.refs_12_
  15.3 1.6 %collective-permute-start.7 = (bf16[272,128]{1,0:T(8,128)(2,1)S(1)}, bf16[272,128]{1,0:T(8,128)(2,1)S(1)}, u32[]{:S(2)}, u32[]{:S(2)}) collective-permute-start(bf16[272,128]{1,0:T(8,128)(2,1)S(1)} %collective-permute-done.3.refs_2_), channel_id=1, source_target_pairs={{0,2},{1,3},{2,0},{3,1},{4,6},{5,7},{6,4},{7,5},{8,10},{9,11},{10,... | collective-permute-start | bytes 208904 | tf_op jit(solution)/shard_map/ppermute | solution.py:395
  16.9 0.0 collective-permute-done.6.refs_5_
  16.9 0.2 collective-permute-start.10
  17.1 0.5 %collective-permute-done.4.refs_3_ = bf16[272,128]{1,0:T(8,128)(2,1)S(1)} collective-permute-done((bf16[272,128]{1,0:T(8,128)(2,1)S(1)}, bf16[272,128]{1,0:T(8,128)(2,1)S(1)}, u32[]{:S(2)}, u32[]{:S(2)}) %collective-permute-start.4) | collective-permute-done | bytes 69664 | tf_op jit(solution)/shard_map/ppermute | solution.py:395
  17.6 1.5 %collective-permute-start.8 = (bf16[272,128]{1,0:T(8,128)(2,1)S(1)}, bf16[272,128]{1,0:T(8,128)(2,1)S(1)}, u32[]{:S(2)}, u32[]{:S(2)}) collective-permute-start(bf16[272,128]{1,0:T(8,128)(2,1)S(1)} %collective-permute-done.4.refs_3_), channel_id=1, source_target_pairs={{0,2},{1,3},{2,0},{3,1},{4,6},{5,7},{6,4},{7,5},{8,10},{9,11},{10,... | collective-permute-start | bytes 208904 | tf_op jit(solution)/shard_map/ppermute | solution.py:395
  19.1 2.7 %plan.1 = (bf16[768,2560]{1,0:T(8,128)(2,1)}, s32[250]{0:T(256)S(4)}, bf16[4,128,128]{2,1,0:T(8,128)(2,1)}, bf16[9,128,128]{2,1,0:T(8,128)(2,1)}) custom-call(s32[16]{0:T(128)} %ksym.3, s32[20]{0:T(128)} %vsym.3, s32[6]{0:T(128)} %osym.3, bf16[272,128]{1,0:T(8,128)(2,1)S(1)} %get-tuple-element.40.after.refs_0_), custom_call_target="tpu_custom_call" | custom-call | tf_op jit(solution)/shard_map/plan/pallas_call | solution.py:364
  21.9 0.0 collective-permute-done.11.refs_10_
  21.9 0.1 collective-permute-start.14
  22.0 0.5 %collective-permute-start.15 = (bf16[272,128]{1,0:T(8,128)(2,1)S(1)}, bf16[272,128]{1,0:T(8,128)(2,1)S(1)}, u32[]{:S(2)}, u32[]{:S(2)}) collective-permute-start(bf16[272,128]{1,0:T(8,128)(2,1)S(1)} %collective-permute-done.7.refs_6_), channel_id=1, source_target_pairs={{0,1},{1,0},{2,3},{3,2},{4,5},{5,4},{6,7},{7,6},{8,9},{9,8},{10,11... | collective-permute-start | bytes 208904 | tf_op jit(solution)/shard_map/ppermute | solution.py:395
  22.5 0.1 collective-permute-start.12
  22.6 0.4 %collective-permute-start.16 = (bf16[272,128]{1,0:T(8,128)(2,1)S(1)}, bf16[272,128]{1,0:T(8,128)(2,1)S(1)}, u32[]{:S(2)}, u32[]{:S(2)}) collective-permute-start(bf16[272,128]{1,0:T(8,128)(2,1)S(1)} %collective-permute-done.8.refs_7_), channel_id=1, source_target_pairs={{0,1},{1,0},{2,3},{3,2},{4,5},{5,4},{6,7},{7,6},{8,9},{9,8},{10,11... | collective-permute-start | bytes 208904 | tf_op jit(solution)/shard_map/ppermute | solution.py:395
  23.0 0.4 %collective-permute-done.15.refs_14_ = bf16[272,128]{1,0:T(8,128)(2,1)S(1)} collective-permute-done((bf16[272,128]{1,0:T(8,128)(2,1)S(1)}, bf16[272,128]{1,0:T(8,128)(2,1)S(1)}, u32[]{:S(2)}, u32[]{:S(2)}) %collective-permute-start.15) | collective-permute-done | bytes 69664 | tf_op jit(solution)/shard_map/ppermute | solution.py:395
  23.4 0.4 %collective-permute-done.12.refs_11_ = bf16[272,128]{1,0:T(8,128)(2,1)S(1)} collective-permute-done((bf16[272,128]{1,0:T(8,128)(2,1)S(1)}, bf16[272,128]{1,0:T(8,128)(2,1)S(1)}, u32[]{:S(2)}, u32[]{:S(2)}) %collective-permute-start.12) | collective-permute-done | bytes 69664 | tf_op jit(solution)/shard_map/ppermute | solution.py:395
  23.7 0.2 collective-permute-done.16.refs_15_
  23.9 0.7 %sort.1 = (bf16[16,256,128]{2,1,0:T(8,128)(2,1)S(1)}, s32[1]{0:T(128)}) custom-call(bf16[272,128]{1,0:T(8,128)(2,1)S(1)} %get-tuple-element.40.after.refs_0_, bf16[272,128]{1,0:T(8,128)(2,1)S(1)} %collective-permute-done.2.refs_1_, bf16[272,128]{1,0:T(8,128)(2,1)S(1)} %collective-permute-done.3.refs_2_, bf16[272,128]{1,0:T(8,128)(2,1)S(1)} %collective-permute-done.4.refs_3_, ...), custom_call_target="tpu_custom_call" | custom-call | tf_op jit(solution)/shard_map/sort/pallas_call | solution.py:410
  25.3 0.2 collective-permute-done.17.refs_1_
  25.5 3.2 %finish.1 = bf16[768,2560]{1,0:T(8,128)(2,1)} custom-call(s32[250]{0:T(256)S(4)} %get-tuple-element.41.tab, bf16[16,256,128]{2,1,0:T(8,128)(2,1)S(1)} %get-tuple-element.44.amp, bf16[27,128,128]{2,1,0:T(8,128)(2,1)S(1)} %get-tuple-element.45.refs_0_, bf16[27,128,128]{2,1,0:T(8,128)(2,1)S(1)} %collective-permute-done.17.refs_1_, ...), custom_call_target="tpu_custom_call", output_to_operand_aliasing={{}: (8, {})} | custom-call | tf_op jit(solution)/shard_map/finish/pallas_call | solution.py:439
  (5 shorter events, 0.0 us)
Async XLA Ops:
  2.9 22.6 %collective-permute-start.17 = (bf16[27,128,128]{2,1,0:T(8,128)(2,1)S(1)}, bf16[27,128,128]{2,1,0:T(8,128)(2,1)S(1)}, u32[]{:S(2)}, u32[]{:S(2)}) collective-permute-start(bf16[27,128,128]{2,1,0:T(8,128)(2,1)S(1)} %get-tuple-element.45.refs_0_), channel_id=1, source_target_pairs={{0,16},{16,0},{1,17},{17,1},{2,18},{18,2},{3,19},{19,3},{4,20},{20... | collective-permute-start | bytes 2654216 | tf_op jit(solution)/shard_map/ppermute | solution.py:383
  5.8 5.7 %collective-permute-start.5 = (bf16[272,128]{1,0:T(8,128)(2,1)S(1)}, bf16[272,128]{1,0:T(8,128)(2,1)S(1)}, u32[]{:S(2)}, u32[]{:S(2)}) collective-permute-start(bf16[272,128]{1,0:T(8,128)(2,1)S(1)} %get-tuple-element.40.after.refs_0_), channel_id=1, source_target_pairs={{0,2},{1,3},{2,0},{3,1},{4,6},{5,7},{6,4},{7,5},{8,10},{9,11},{10,... | collective-permute-start | bytes 208904 | tf_op jit(solution)/shard_map/ppermute | solution.py:395
  7.3 5.3 %collective-permute-start.2 = (bf16[272,128]{1,0:T(8,128)(2,1)S(1)}, bf16[272,128]{1,0:T(8,128)(2,1)S(1)}, u32[]{:S(2)}, u32[]{:S(2)}) collective-permute-start(bf16[272,128]{1,0:T(8,128)(2,1)S(1)} %get-tuple-element.40.after.refs_0_), channel_id=1, source_target_pairs={{0,8},{1,9},{2,10},{3,11},{4,12},{5,13},{6,14},{7,15},{8,0},{9,1},... | collective-permute-start | bytes 208904 | tf_op jit(solution)/shard_map/ppermute | solution.py:395
  9.9 3.2 %collective-permute-start.9 = (bf16[272,128]{1,0:T(8,128)(2,1)S(1)}, bf16[272,128]{1,0:T(8,128)(2,1)S(1)}, u32[]{:S(2)}, u32[]{:S(2)}) collective-permute-start(bf16[272,128]{1,0:T(8,128)(2,1)S(1)} %get-tuple-element.40.after.refs_0_), channel_id=1, source_target_pairs={{0,1},{1,0},{2,3},{3,2},{4,5},{5,4},{6,7},{7,6},{8,9},{9,8},{10,11... | collective-permute-start | bytes 208904 | tf_op jit(solution)/shard_map/ppermute | solution.py:395
  9.9 5.4 %collective-permute-start.3 = (bf16[272,128]{1,0:T(8,128)(2,1)S(1)}, bf16[272,128]{1,0:T(8,128)(2,1)S(1)}, u32[]{:S(2)}, u32[]{:S(2)}) collective-permute-start(bf16[272,128]{1,0:T(8,128)(2,1)S(1)} %get-tuple-element.40.after.refs_0_), channel_id=1, source_target_pairs={{0,4},{1,5},{2,6},{3,7},{4,0},{5,1},{6,2},{7,3},{8,12},{9,13},{10,... | collective-permute-start | bytes 208904 | tf_op jit(solution)/shard_map/ppermute | solution.py:395
  11.5 3.9 %collective-permute-start.13 = (bf16[272,128]{1,0:T(8,128)(2,1)S(1)}, bf16[272,128]{1,0:T(8,128)(2,1)S(1)}, u32[]{:S(2)}, u32[]{:S(2)}) collective-permute-start(bf16[272,128]{1,0:T(8,128)(2,1)S(1)} %collective-permute-done.5.refs_4_), channel_id=1, source_target_pairs={{0,1},{1,0},{2,3},{3,2},{4,5},{5,4},{6,7},{7,6},{8,9},{9,8},{10,11... | collective-permute-start | bytes 208904 | tf_op jit(solution)/shard_map/ppermute | solution.py:395
  12.6 4.3 %collective-permute-start.6 = (bf16[272,128]{1,0:T(8,128)(2,1)S(1)}, bf16[272,128]{1,0:T(8,128)(2,1)S(1)}, u32[]{:S(2)}, u32[]{:S(2)}) collective-permute-start(bf16[272,128]{1,0:T(8,128)(2,1)S(1)} %collective-permute-done.2.refs_1_), channel_id=1, source_target_pairs={{0,2},{1,3},{2,0},{3,1},{4,6},{5,7},{6,4},{7,5},{8,10},{9,11},{10,... | collective-permute-start | bytes 208904 | tf_op jit(solution)/shard_map/ppermute | solution.py:395
  13.1 4.5 %collective-permute-start.4 = (bf16[272,128]{1,0:T(8,128)(2,1)S(1)}, bf16[272,128]{1,0:T(8,128)(2,1)S(1)}, u32[]{:S(2)}, u32[]{:S(2)}) collective-permute-start(bf16[272,128]{1,0:T(8,128)(2,1)S(1)} %collective-permute-done.2.refs_1_), channel_id=1, source_target_pairs={{0,4},{1,5},{2,6},{3,7},{4,0},{5,1},{6,2},{7,3},{8,12},{9,13},{10,... | collective-permute-start | bytes 208904 | tf_op jit(solution)/shard_map/ppermute | solution.py:395
  15.3 6.6 %collective-permute-start.11 = (bf16[272,128]{1,0:T(8,128)(2,1)S(1)}, bf16[272,128]{1,0:T(8,128)(2,1)S(1)}, u32[]{:S(2)}, u32[]{:S(2)}) collective-permute-start(bf16[272,128]{1,0:T(8,128)(2,1)S(1)} %collective-permute-done.3.refs_2_), channel_id=1, source_target_pairs={{0,1},{1,0},{2,3},{3,2},{4,5},{5,4},{6,7},{7,6},{8,9},{9,8},{10,11... | collective-permute-start | bytes 208904 | tf_op jit(solution)/shard_map/ppermute | solution.py:395
  15.3 6.6 %collective-permute-start.7 = (bf16[272,128]{1,0:T(8,128)(2,1)S(1)}, bf16[272,128]{1,0:T(8,128)(2,1)S(1)}, u32[]{:S(2)}, u32[]{:S(2)}) collective-permute-start(bf16[272,128]{1,0:T(8,128)(2,1)S(1)} %collective-permute-done.3.refs_2_), channel_id=1, source_target_pairs={{0,2},{1,3},{2,0},{3,1},{4,6},{5,7},{6,4},{7,5},{8,10},{9,11},{10,... | collective-permute-start | bytes 208904 | tf_op jit(solution)/shard_map/ppermute | solution.py:395
  16.9 5.5 %collective-permute-start.10 = (bf16[272,128]{1,0:T(8,128)(2,1)S(1)}, bf16[272,128]{1,0:T(8,128)(2,1)S(1)}, u32[]{:S(2)}, u32[]{:S(2)}) collective-permute-start(bf16[272,128]{1,0:T(8,128)(2,1)S(1)} %collective-permute-done.2.refs_1_), channel_id=1, source_target_pairs={{0,1},{1,0},{2,3},{3,2},{4,5},{5,4},{6,7},{7,6},{8,9},{9,8},{10,11... | collective-permute-start | bytes 208904 | tf_op jit(solution)/shard_map/ppermute | solution.py:395
  17.6 5.0 %collective-permute-start.8 = (bf16[272,128]{1,0:T(8,128)(2,1)S(1)}, bf16[272,128]{1,0:T(8,128)(2,1)S(1)}, u32[]{:S(2)}, u32[]{:S(2)}) collective-permute-start(bf16[272,128]{1,0:T(8,128)(2,1)S(1)} %collective-permute-done.4.refs_3_), channel_id=1, source_target_pairs={{0,2},{1,3},{2,0},{3,1},{4,6},{5,7},{6,4},{7,5},{8,10},{9,11},{10,... | collective-permute-start | bytes 208904 | tf_op jit(solution)/shard_map/ppermute | solution.py:395
  21.9 1.8 %collective-permute-start.14 = (bf16[272,128]{1,0:T(8,128)(2,1)S(1)}, bf16[272,128]{1,0:T(8,128)(2,1)S(1)}, u32[]{:S(2)}, u32[]{:S(2)}) collective-permute-start(bf16[272,128]{1,0:T(8,128)(2,1)S(1)} %collective-permute-done.6.refs_5_), channel_id=1, source_target_pairs={{0,1},{1,0},{2,3},{3,2},{4,5},{5,4},{6,7},{7,6},{8,9},{9,8},{10,11... | collective-permute-start | bytes 208904 | tf_op jit(solution)/shard_map/ppermute | solution.py:395
  22.0 1.4 %collective-permute-start.15 = (bf16[272,128]{1,0:T(8,128)(2,1)S(1)}, bf16[272,128]{1,0:T(8,128)(2,1)S(1)}, u32[]{:S(2)}, u32[]{:S(2)}) collective-permute-start(bf16[272,128]{1,0:T(8,128)(2,1)S(1)} %collective-permute-done.7.refs_6_), channel_id=1, source_target_pairs={{0,1},{1,0},{2,3},{3,2},{4,5},{5,4},{6,7},{7,6},{8,9},{9,8},{10,11... | collective-permute-start | bytes 208904 | tf_op jit(solution)/shard_map/ppermute | solution.py:395
  22.5 1.3 %collective-permute-start.12 = (bf16[272,128]{1,0:T(8,128)(2,1)S(1)}, bf16[272,128]{1,0:T(8,128)(2,1)S(1)}, u32[]{:S(2)}, u32[]{:S(2)}) collective-permute-start(bf16[272,128]{1,0:T(8,128)(2,1)S(1)} %collective-permute-done.4.refs_3_), channel_id=1, source_target_pairs={{0,1},{1,0},{2,3},{3,2},{4,5},{5,4},{6,7},{7,6},{8,9},{9,8},{10,11... | collective-permute-start | bytes 208904 | tf_op jit(solution)/shard_map/ppermute | solution.py:395
  22.6 1.3 %collective-permute-start.16 = (bf16[272,128]{1,0:T(8,128)(2,1)S(1)}, bf16[272,128]{1,0:T(8,128)(2,1)S(1)}, u32[]{:S(2)}, u32[]{:S(2)}) collective-permute-start(bf16[272,128]{1,0:T(8,128)(2,1)S(1)} %collective-permute-done.8.refs_7_), channel_id=1, source_target_pairs={{0,1},{1,0},{2,3},{3,2},{4,5},{5,4},{6,7},{7,6},{8,9},{9,8},{10,11... | collective-permute-start | bytes 208904 | tf_op jit(solution)/shard_map/ppermute | solution.py:395

commit v5 on v4

--- a/solution.py
+++ b/solution.py
@@ -37,7 +37,8 @@
         self.slot = self.vbl + IRREPS * MAXB
         self.off = self.slot + IRREPS * MAXO
         self.total = self.off + n_occ * vblocks
-        self.size = self.total + n_occ
+        self.active = self.total + n_occ
+        self.size = self.active + 1 + IRREPS
 
 
 def contraction_lists(t, ksym, tab, halves):
@@ -53,7 +54,7 @@
 
 
 def pack_kernel(t, chunks, ksym, vsym, osym, v_ref, a_ref, *refs):
-    packed, (pay, tab, sems) = refs[: len(chunks)], refs[len(chunks) :]
+    packed, (pay, tab, sems, pay_sems) = refs[: len(chunks)], refs[len(chunks) :]
     own, vblocks, oblocks = t.own, t.vblocks, osym.shape[0]
     width = a_ref.shape[1]
     me = lax.axis_index("occ")
@@ -98,16 +99,9 @@
 
         total = total + n
 
-    contraction_lists(t, ksym, tab, others)
-    most = total
-    for half in others:
-        other = jnp.int32(0)
-        for vb in range(vblocks):
-            other = other + tab[t.nk + half * IRREPS + vsym[vb]]
-        most = jnp.maximum(most, other)
-
     vir = lax.axis_index("vir")
     step = min(width, BLK)
+    copies = []
     for q in range(width // step):
         s = ksym[(vir * width + q * step) // BLK]
         cols = slice(q * step, (q + 1) * step)
@@ -120,14 +114,41 @@
             ]
             found = found + match.astype(jnp.int32)
         for i, ob in enumerate(slots):
-            rows = pl.ds(pl.multiple_of(jnp.maximum(ob, 0) * BLK, BLK), BLK)
-            part = a_ref[rows, cols]
-            pay[i * BLK : (i + 1) * BLK, cols] = jnp.where(
-                ob >= 0, part, jnp.zeros_like(part)
+            copy = pltpu.make_async_copy(
+                a_ref.at[
+                    pl.ds(pl.multiple_of(jnp.maximum(ob, 0) * BLK, BLK), BLK),
+                    pl.ds(q * step, step),
+                ],
+                pay.at[pl.ds(i * BLK, BLK), pl.ds(q * step, step)],
+                pay_sems.at[q * MAXO + i],
             )
+            copies.append((ob, copy))
+
+            @pl.when(ob >= 0)
+            def _(copy=copy):
+                copy.start()
+
+            @pl.when(ob < 0)
+            def _(i=i, cols=cols):
+                pay[i * BLK : (i + 1) * BLK, cols] = jnp.zeros((BLK, step), jnp.bfloat16)
+
+    contraction_lists(t, ksym, tab, others)
+    most = total
+    for half in others:
+        other = jnp.int32(0)
+        for vb in range(vblocks):
+            other = other + tab[t.nk + half * IRREPS + vsym[vb]]
+        most = jnp.maximum(most, other)
+
     pay[MAXO * BLK :, :] = jnp.full(
         (INFO, width), most.astype(jnp.float32), jnp.float32
     ).astype(jnp.bfloat16)
+
+    for ob, copy in copies:
+
+        @pl.when(ob >= 0)
+        def _(copy=copy):
+            copy.wait()
 
     @pl.loop(0, total)
     def _(place):
@@ -171,19 +192,28 @@
     totals = lax.fori_loop(0, t.vblocks, count, (jnp.int32(0),) * t.n_occ)
     for half, total in enumerate(totals):
         tab[t.total + half] = total
+    tab[t.active] = 0
+    for s in range(IRREPS):
+
+        @pl.when((tab[t.cnt + s] > 0) & (tab[t.slot + s * MAXO] >= 0))
+        def _(s=s):
+            used = tab[t.active]
+            tab[t.active + 1 + used] = s
+            tab[t.active] = used + 1
     for fill in fills:
         fill.wait()
 
 
 def each_irrep(t, tab, act, variants):
-    @pl.loop(0, IRREPS)
-    def _(s):
+    @pl.loop(0, tab[t.active])
+    def _(i):
+        s = tab[t.active + 1 + i]
         count = tab[t.cnt + s]
-        rows = jnp.where(tab[t.slot + s * MAXO] >= 0, BLK, 0)
+        rows = jnp.int32(BLK)
         for slot in range(1, MAXO):
             more = tab[t.slot + s * MAXO + slot] >= 0
             rows = jnp.where(more, (slot + 1) * BLK, rows)
-        todo = (count > 0) & (rows > 0)
+        todo = count > 0
         for have, width in variants:
             fits = todo & (rows <= have) & (count <= width)
 
@@ -213,21 +243,25 @@
         steps = jnp.maximum(steps, count)
 
     def terms(rank):
-        sums = [None] * len(vbs)
+        lefts, rights = [], [[] for _ in vbs]
         for row, count, places, source in zip(bases, counts, offs, sources):
             there = rank < count
             here = jnp.where(there, rank, 0)
             kb = jnp.where(there, tab[t.kbl + row * t.own + here], 0)
             left = amp[kb, :rows, :]
-            for j, place in enumerate(places):
-                part = jnp.dot(
-                    left,
-                    source[jnp.where(there, place + here, 0)],
-                    preferred_element_type=jnp.float32,
-                )
-                part = jnp.where(there, part, 0.0)
-                sums[j] = part if sums[j] is None else sums[j] + part
-        return sums
+            lefts.append(jnp.where(there, left, jnp.zeros_like(left)))
+            for place, column in zip(places, rights):
+                right = source[jnp.where(there, place + here, 0)]
+                column.append(jnp.where(there, right, jnp.zeros_like(right)))
+        left = jnp.concatenate(lefts, axis=1)
+        return [
+            jnp.dot(
+                left,
+                jnp.concatenate(column, axis=0),
+                preferred_element_type=jnp.float32,
+            )
+            for column in rights
+        ]
 
     for j, part in enumerate(terms(jnp.int32(0))):
         acc[j, :rows, :] = part
@@ -352,11 +386,12 @@
         functools.partial(pack_kernel, t, chunks),
         out_shape=tuple(pltpu.VMEM((c, BLK, BLK), bf16) for c in chunks)
         + (pltpu.VMEM((rows, width), bf16),),
-        in_specs=[SMEM, SMEM, SMEM, HBM, VMEM],
+        in_specs=[SMEM, SMEM, SMEM, HBM, HBM],
         out_specs=(VMEM,) * (len(chunks) + 1),
         scratch_shapes=[
             pltpu.SMEM((t.size,), i32),
             pltpu.SemaphoreType.DMA((cap,)),
+            pltpu.SemaphoreType.DMA((MAXO * max(width // BLK, 1),)),
         ],
         compiler_params=pltpu.CompilerParams(vmem_limit_bytes=8 * 2**20),
         name="pack",

time: 29 us -> 28.9 us (level)
    pallas_call x1, Pallas kernels: 2.87 us -> 2.52 us  [per_device(): pl.pallas_call(functools.partial(pack_kernel, t, chunks), out_shape=tuple...]
    ppermute x15, starting transfers between devices: 13 us -> 12.7 us  [per_device(): parts = parts + [lax.ppermute(p, 'vir', pairs) for p in parts]]
    ppermute x15, waiting for transfers between devices: 2.34 us -> 2.65 us  [per_device(): parts = parts + [lax.ppermute(p, 'vir', pairs) for p in parts]]
  transfers between devices with their start and end apart: 16 -> 16, of which waited for: 6 -> 7; matrix products, arithmetic and copies ran while one was open for 0% -> 0% of each run, Pallas kernels for 12% -> 12%
where the time goes in v5:
time: 28.9 us; the launch traced here: 28.6 us
  starting transfers between devices  15.8 us (55%)
  Pallas kernels  9.31 us (32%)
  waiting for transfers between devices  2.73 us (9%)
  between operations  0.71 us (2%)
    ppermute x15, starting transfers between devices, per_device(): parts = parts + [lax.ppermute(p, 'vir', pairs) for p in parts]  12.7 us
    pallas_call x1, Pallas kernels, per_device(): pl.pallas_call(functools.partial(finish_kernel, t, chunks), out_shape=jax...  3.36 us
    ppermute x1, starting transfers between devices, across(): lax.ppermute(x, 'occ', [(i, (i + shift) % n_occ) for i in range(n_occ)])  3.09 us
    pallas_call x1, Pallas kernels, per_device(): pl.pallas_call(functools.partial(plan_kernel, t), out_shape=(pltpu.HBM((o...  2.73 us
    ppermute x15, waiting for transfers between devices, per_device(): parts = parts + [lax.ppermute(p, 'vir', pairs) for p in parts]  2.65 us
    pallas_call x1, Pallas kernels, per_device(): pl.pallas_call(functools.partial(pack_kernel, t, chunks), out_shape=tuple...  2.52 us
    pallas_call x1, Pallas kernels, per_device(): pl.pallas_call(functools.partial(sort_kernel, tuple(masks)), out_shape=(p...  0.71 us
  transfers between devices with their start and end apart: 16, of which 7 were waited for; matrix products, arithmetic and copies ran while one was open for 0% of the time, Pallas kernels for 12%

profile of v5, /device:TPU:0, one launch (start us, length us, event | category | flops | bytes accessed | tf_op | source)
XLA Modules:
  0.0 28.6 jit_solution(17648500295101948906)
XLA Ops:
  0.0 2.5 %pack.1 = (bf16[27,128,128]{2,1,0:T(8,128)(2,1)S(1)}, bf16[4,128,128]{2,1,0:T(8,128)(2,1)S(1)}, bf16[9,128,128]{2,1,0:T(8,128)(2,1)S(1)}, bf16[272,128]{1,0:T(8,128)(2,1)S(1)}) custom-call(s32[16]{0:T(128)} %ksym.3, s32[20]{0:T(128)} %vsym.3, s32[6]{0:T(128)} %osym.3, bf16[1024,2560]{1,0:T(8,128)(2,1)} %v_ref.1, bf16[768,128]{1,0:T(8,128)(2,1)} %a_ref.1), custom_call_target="tpu_custom_call" | custom-call | tf_op jit(solution)/shard_map/pack/pallas_call | solution.py:385
  2.5 3.1 %collective-permute-start.17 = (bf16[27,128,128]{2,1,0:T(8,128)(2,1)S(1)}, bf16[27,128,128]{2,1,0:T(8,128)(2,1)S(1)}, u32[]{:S(2)}, u32[]{:S(2)}) collective-permute-start(bf16[27,128,128]{2,1,0:T(8,128)(2,1)S(1)} %get-tuple-element.45.refs_0_), channel_id=1, source_target_pairs={{0,16},{16,0},{1,17},{17,1},{2,18},{18,2},{3,19},{19,3},{4,20},{20... | collective-permute-start | bytes 2654216 | tf_op jit(solution)/shard_map/ppermute | solution.py:418
  5.6 1.5 %collective-permute-start.5 = (bf16[272,128]{1,0:T(8,128)(2,1)S(1)}, bf16[272,128]{1,0:T(8,128)(2,1)S(1)}, u32[]{:S(2)}, u32[]{:S(2)}) collective-permute-start(bf16[272,128]{1,0:T(8,128)(2,1)S(1)} %get-tuple-element.40.after.refs_0_), channel_id=1, source_target_pairs={{0,2},{1,3},{2,0},{3,1},{4,6},{5,7},{6,4},{7,5},{8,10},{9,11},{10,... | collective-permute-start | bytes 208904 | tf_op jit(solution)/shard_map/ppermute | solution.py:430
  7.2 2.7 %collective-permute-start.2 = (bf16[272,128]{1,0:T(8,128)(2,1)S(1)}, bf16[272,128]{1,0:T(8,128)(2,1)S(1)}, u32[]{:S(2)}, u32[]{:S(2)}) collective-permute-start(bf16[272,128]{1,0:T(8,128)(2,1)S(1)} %get-tuple-element.40.after.refs_0_), channel_id=1, source_target_pairs={{0,8},{1,9},{2,10},{3,11},{4,12},{5,13},{6,14},{7,15},{8,0},{9,1},... | collective-permute-start | bytes 208904 | tf_op jit(solution)/shard_map/ppermute | solution.py:430
  9.8 0.0 collective-permute-start.9
  9.8 1.5 %collective-permute-start.3 = (bf16[272,128]{1,0:T(8,128)(2,1)S(1)}, bf16[272,128]{1,0:T(8,128)(2,1)S(1)}, u32[]{:S(2)}, u32[]{:S(2)}) collective-permute-start(bf16[272,128]{1,0:T(8,128)(2,1)S(1)} %get-tuple-element.40.after.refs_0_), channel_id=1, source_target_pairs={{0,4},{1,5},{2,6},{3,7},{4,0},{5,1},{6,2},{7,3},{8,12},{9,13},{10,... | collective-permute-start | bytes 208904 | tf_op jit(solution)/shard_map/ppermute | solution.py:430
  11.3 0.0 collective-permute-done.5.refs_4_
  11.3 0.2 collective-permute-start.13
  11.6 1.0 %collective-permute-done.2.refs_1_ = bf16[272,128]{1,0:T(8,128)(2,1)S(1)} collective-permute-done((bf16[272,128]{1,0:T(8,128)(2,1)S(1)}, bf16[272,128]{1,0:T(8,128)(2,1)S(1)}, u32[]{:S(2)}, u32[]{:S(2)}) %collective-permute-start.2) | collective-permute-done | bytes 69664 | tf_op jit(solution)/shard_map/ppermute | solution.py:430
  12.5 0.4 %collective-permute-start.6 = (bf16[272,128]{1,0:T(8,128)(2,1)S(1)}, bf16[272,128]{1,0:T(8,128)(2,1)S(1)}, u32[]{:S(2)}, u32[]{:S(2)}) collective-permute-start(bf16[272,128]{1,0:T(8,128)(2,1)S(1)} %collective-permute-done.2.refs_1_), channel_id=1, source_target_pairs={{0,2},{1,3},{2,0},{3,1},{4,6},{5,7},{6,4},{7,5},{8,10},{9,11},{10,... | collective-permute-start | bytes 208904 | tf_op jit(solution)/shard_map/ppermute | solution.py:430
  12.9 0.0 collective-permute-done.9.refs_8_
  12.9 2.4 %collective-permute-start.4 = (bf16[272,128]{1,0:T(8,128)(2,1)S(1)}, bf16[272,128]{1,0:T(8,128)(2,1)S(1)}, u32[]{:S(2)}, u32[]{:S(2)}) collective-permute-start(bf16[272,128]{1,0:T(8,128)(2,1)S(1)} %collective-permute-done.2.refs_1_), channel_id=1, source_target_pairs={{0,4},{1,5},{2,6},{3,7},{4,0},{5,1},{6,2},{7,3},{8,12},{9,13},{10,... | collective-permute-start | bytes 208904 | tf_op jit(solution)/shard_map/ppermute | solution.py:430
  15.3 0.0 collective-permute-done.3.refs_2_
  15.3 0.0 collective-permute-done.13.refs_12_
  15.3 1.4 %collective-permute-start.7 = (bf16[272,128]{1,0:T(8,128)(2,1)S(1)}, bf16[272,128]{1,0:T(8,128)(2,1)S(1)}, u32[]{:S(2)}, u32[]{:S(2)}) collective-permute-start(bf16[272,128]{1,0:T(8,128)(2,1)S(1)} %collective-permute-done.3.refs_2_), channel_id=1, source_target_pairs={{0,2},{1,3},{2,0},{3,1},{4,6},{5,7},{6,4},{7,5},{8,10},{9,11},{10,... | collective-permute-start | bytes 208904 | tf_op jit(solution)/shard_map/ppermute | solution.py:430
  16.8 0.1 collective-permute-done.6.refs_5_
  16.9 0.1 collective-permute-start.10
  16.9 0.7 %collective-permute-done.4.refs_3_ = bf16[272,128]{1,0:T(8,128)(2,1)S(1)} collective-permute-done((bf16[272,128]{1,0:T(8,128)(2,1)S(1)}, bf16[272,128]{1,0:T(8,128)(2,1)S(1)}, u32[]{:S(2)}, u32[]{:S(2)}) %collective-permute-start.4) | collective-permute-done | bytes 69664 | tf_op jit(solution)/shard_map/ppermute | solution.py:430
  17.6 1.4 %collective-permute-start.8 = (bf16[272,128]{1,0:T(8,128)(2,1)S(1)}, bf16[272,128]{1,0:T(8,128)(2,1)S(1)}, u32[]{:S(2)}, u32[]{:S(2)}) collective-permute-start(bf16[272,128]{1,0:T(8,128)(2,1)S(1)} %collective-permute-done.4.refs_3_), channel_id=1, source_target_pairs={{0,2},{1,3},{2,0},{3,1},{4,6},{5,7},{6,4},{7,5},{8,10},{9,11},{10,... | collective-permute-start | bytes 208904 | tf_op jit(solution)/shard_map/ppermute | solution.py:430
  19.0 2.7 %plan.1 = (bf16[768,2560]{1,0:T(8,128)(2,1)}, s32[259]{0:T(512)S(4)}, bf16[4,128,128]{2,1,0:T(8,128)(2,1)}, bf16[9,128,128]{2,1,0:T(8,128)(2,1)}) custom-call(s32[16]{0:T(128)} %ksym.3, s32[20]{0:T(128)} %vsym.3, s32[6]{0:T(128)} %osym.3, bf16[272,128]{1,0:T(8,128)(2,1)S(1)} %get-tuple-element.40.after.refs_0_), custom_call_target="tpu_custom_call" | custom-call | tf_op jit(solution)/shard_map/plan/pallas_call | solution.py:399
  21.7 0.1 collective-permute-start.14
  21.8 0.5 %collective-permute-start.15 = (bf16[272,128]{1,0:T(8,128)(2,1)S(1)}, bf16[272,128]{1,0:T(8,128)(2,1)S(1)}, u32[]{:S(2)}, u32[]{:S(2)}) collective-permute-start(bf16[272,128]{1,0:T(8,128)(2,1)S(1)} %collective-permute-done.7.refs_6_), channel_id=1, source_target_pairs={{0,1},{1,0},{2,3},{3,2},{4,5},{5,4},{6,7},{7,6},{8,9},{9,8},{10,11... | collective-permute-start | bytes 208904 | tf_op jit(solution)/shard_map/ppermute | solution.py:430
  22.3 0.0 collective-permute-done.10.refs_9_
  22.3 0.1 collective-permute-start.12
  22.4 0.4 %collective-permute-start.16 = (bf16[272,128]{1,0:T(8,128)(2,1)S(1)}, bf16[272,128]{1,0:T(8,128)(2,1)S(1)}, u32[]{:S(2)}, u32[]{:S(2)}) collective-permute-start(bf16[272,128]{1,0:T(8,128)(2,1)S(1)} %collective-permute-done.8.refs_7_), channel_id=1, source_target_pairs={{0,1},{1,0},{2,3},{3,2},{4,5},{5,4},{6,7},{7,6},{8,9},{9,8},{10,11... | collective-permute-start | bytes 208904 | tf_op jit(solution)/shard_map/ppermute | solution.py:430
  22.8 0.4 %collective-permute-done.15.refs_14_ = bf16[272,128]{1,0:T(8,128)(2,1)S(1)} collective-permute-done((bf16[272,128]{1,0:T(8,128)(2,1)S(1)}, bf16[272,128]{1,0:T(8,128)(2,1)S(1)}, u32[]{:S(2)}, u32[]{:S(2)}) %collective-permute-start.15) | collective-permute-done | bytes 69664 | tf_op jit(solution)/shard_map/ppermute | solution.py:430
  23.2 0.4 %collective-permute-done.12.refs_11_ = bf16[272,128]{1,0:T(8,128)(2,1)S(1)} collective-permute-done((bf16[272,128]{1,0:T(8,128)(2,1)S(1)}, bf16[272,128]{1,0:T(8,128)(2,1)S(1)}, u32[]{:S(2)}, u32[]{:S(2)}) %collective-permute-start.12) | collective-permute-done | bytes 69664 | tf_op jit(solution)/shard_map/ppermute | solution.py:430
  23.6 0.0 collective-permute-done.14.refs_13_
  23.6 0.2 collective-permute-done.16.refs_15_
  23.7 0.7 %sort.1 = (bf16[16,256,128]{2,1,0:T(8,128)(2,1)S(1)}, s32[1]{0:T(128)}) custom-call(bf16[272,128]{1,0:T(8,128)(2,1)S(1)} %get-tuple-element.40.after.refs_0_, bf16[272,128]{1,0:T(8,128)(2,1)S(1)} %collective-permute-done.2.refs_1_, bf16[272,128]{1,0:T(8,128)(2,1)S(1)} %collective-permute-done.3.refs_2_, bf16[272,128]{1,0:T(8,128)(2,1)S(1)} %collective-permute-done.4.refs_3_, ...), custom_call_target="tpu_custom_call" | custom-call | tf_op jit(solution)/shard_map/sort/pallas_call | solution.py:445
  25.1 0.1 collective-permute-done.17.refs_1_
  25.2 3.4 %finish.1 = bf16[768,2560]{1,0:T(8,128)(2,1)} custom-call(s32[259]{0:T(512)S(4)} %get-tuple-element.41.tab, bf16[16,256,128]{2,1,0:T(8,128)(2,1)S(1)} %get-tuple-element.44.amp, bf16[27,128,128]{2,1,0:T(8,128)(2,1)S(1)} %get-tuple-element.45.refs_0_, bf16[27,128,128]{2,1,0:T(8,128)(2,1)S(1)} %collective-permute-done.17.refs_1_, ...), custom_call_target="tpu_custom_call", output_to_operand_aliasing={{}: (8, {})} | custom-call | tf_op jit(solution)/shard_map/finish/pallas_call | solution.py:474
  (5 shorter events, 0.0 us)
Async XLA Ops:
  2.5 22.7 %collective-permute-start.17 = (bf16[27,128,128]{2,1,0:T(8,128)(2,1)S(1)}, bf16[27,128,128]{2,1,0:T(8,128)(2,1)S(1)}, u32[]{:S(2)}, u32[]{:S(2)}) collective-permute-start(bf16[27,128,128]{2,1,0:T(8,128)(2,1)S(1)} %get-tuple-element.45.refs_0_), channel_id=1, source_target_pairs={{0,16},{16,0},{1,17},{17,1},{2,18},{18,2},{3,19},{19,3},{4,20},{20... | collective-permute-start | bytes 2654216 | tf_op jit(solution)/shard_map/ppermute | solution.py:418
  5.6 5.7 %collective-permute-start.5 = (bf16[272,128]{1,0:T(8,128)(2,1)S(1)}, bf16[272,128]{1,0:T(8,128)(2,1)S(1)}, u32[]{:S(2)}, u32[]{:S(2)}) collective-permute-start(bf16[272,128]{1,0:T(8,128)(2,1)S(1)} %get-tuple-element.40.after.refs_0_), channel_id=1, source_target_pairs={{0,2},{1,3},{2,0},{3,1},{4,6},{5,7},{6,4},{7,5},{8,10},{9,11},{10,... | collective-permute-start | bytes 208904 | tf_op jit(solution)/shard_map/ppermute | solution.py:430
  7.2 5.4 %collective-permute-start.2 = (bf16[272,128]{1,0:T(8,128)(2,1)S(1)}, bf16[272,128]{1,0:T(8,128)(2,1)S(1)}, u32[]{:S(2)}, u32[]{:S(2)}) collective-permute-start(bf16[272,128]{1,0:T(8,128)(2,1)S(1)} %get-tuple-element.40.after.refs_0_), channel_id=1, source_target_pairs={{0,8},{1,9},{2,10},{3,11},{4,12},{5,13},{6,14},{7,15},{8,0},{9,1},... | collective-permute-start | bytes 208904 | tf_op jit(solution)/shard_map/ppermute | solution.py:430
  9.8 3.1 %collective-permute-start.9 = (bf16[272,128]{1,0:T(8,128)(2,1)S(1)}, bf16[272,128]{1,0:T(8,128)(2,1)S(1)}, u32[]{:S(2)}, u32[]{:S(2)}) collective-permute-start(bf16[272,128]{1,0:T(8,128)(2,1)S(1)} %get-tuple-element.40.after.refs_0_), channel_id=1, source_target_pairs={{0,1},{1,0},{2,3},{3,2},{4,5},{5,4},{6,7},{7,6},{8,9},{9,8},{10,11... | collective-permute-start | bytes 208904 | tf_op jit(solution)/shard_map/ppermute | solution.py:430
  9.8 5.5 %collective-permute-start.3 = (bf16[272,128]{1,0:T(8,128)(2,1)S(1)}, bf16[272,128]{1,0:T(8,128)(2,1)S(1)}, u32[]{:S(2)}, u32[]{:S(2)}) collective-permute-start(bf16[272,128]{1,0:T(8,128)(2,1)S(1)} %get-tuple-element.40.after.refs_0_), channel_id=1, source_target_pairs={{0,4},{1,5},{2,6},{3,7},{4,0},{5,1},{6,2},{7,3},{8,12},{9,13},{10,... | collective-permute-start | bytes 208904 | tf_op jit(solution)/shard_map/ppermute | solution.py:430
  11.3 4.0 %collective-permute-start.13 = (bf16[272,128]{1,0:T(8,128)(2,1)S(1)}, bf16[272,128]{1,0:T(8,128)(2,1)S(1)}, u32[]{:S(2)}, u32[]{:S(2)}) collective-permute-start(bf16[272,128]{1,0:T(8,128)(2,1)S(1)} %collective-permute-done.5.refs_4_), channel_id=1, source_target_pairs={{0,1},{1,0},{2,3},{3,2},{4,5},{5,4},{6,7},{7,6},{8,9},{9,8},{10,11... | collective-permute-start | bytes 208904 | tf_op jit(solution)/shard_map/ppermute | solution.py:430
  12.5 4.3 %collective-permute-start.6 = (bf16[272,128]{1,0:T(8,128)(2,1)S(1)}, bf16[272,128]{1,0:T(8,128)(2,1)S(1)}, u32[]{:S(2)}, u32[]{:S(2)}) collective-permute-start(bf16[272,128]{1,0:T(8,128)(2,1)S(1)} %collective-permute-done.2.refs_1_), channel_id=1, source_target_pairs={{0,2},{1,3},{2,0},{3,1},{4,6},{5,7},{6,4},{7,5},{8,10},{9,11},{10,... | collective-permute-start | bytes 208904 | tf_op jit(solution)/shard_map/ppermute | solution.py:430
  12.9 4.7 %collective-permute-start.4 = (bf16[272,128]{1,0:T(8,128)(2,1)S(1)}, bf16[272,128]{1,0:T(8,128)(2,1)S(1)}, u32[]{:S(2)}, u32[]{:S(2)}) collective-permute-start(bf16[272,128]{1,0:T(8,128)(2,1)S(1)} %collective-permute-done.2.refs_1_), channel_id=1, source_target_pairs={{0,4},{1,5},{2,6},{3,7},{4,0},{5,1},{6,2},{7,3},{8,12},{9,13},{10,... | collective-permute-start | bytes 208904 | tf_op jit(solution)/shard_map/ppermute | solution.py:430
  15.3 6.4 %collective-permute-start.11 = (bf16[272,128]{1,0:T(8,128)(2,1)S(1)}, bf16[272,128]{1,0:T(8,128)(2,1)S(1)}, u32[]{:S(2)}, u32[]{:S(2)}) collective-permute-start(bf16[272,128]{1,0:T(8,128)(2,1)S(1)} %collective-permute-done.3.refs_2_), channel_id=1, source_target_pairs={{0,1},{1,0},{2,3},{3,2},{4,5},{5,4},{6,7},{7,6},{8,9},{9,8},{10,11... | collective-permute-start | bytes 208904 | tf_op jit(solution)/shard_map/ppermute | solution.py:430
  15.3 6.5 %collective-permute-start.7 = (bf16[272,128]{1,0:T(8,128)(2,1)S(1)}, bf16[272,128]{1,0:T(8,128)(2,1)S(1)}, u32[]{:S(2)}, u32[]{:S(2)}) collective-permute-start(bf16[272,128]{1,0:T(8,128)(2,1)S(1)} %collective-permute-done.3.refs_2_), channel_id=1, source_target_pairs={{0,2},{1,3},{2,0},{3,1},{4,6},{5,7},{6,4},{7,5},{8,10},{9,11},{10,... | collective-permute-start | bytes 208904 | tf_op jit(solution)/shard_map/ppermute | solution.py:430
  16.9 5.5 %collective-permute-start.10 = (bf16[272,128]{1,0:T(8,128)(2,1)S(1)}, bf16[272,128]{1,0:T(8,128)(2,1)S(1)}, u32[]{:S(2)}, u32[]{:S(2)}) collective-permute-start(bf16[272,128]{1,0:T(8,128)(2,1)S(1)} %collective-permute-done.2.refs_1_), channel_id=1, source_target_pairs={{0,1},{1,0},{2,3},{3,2},{4,5},{5,4},{6,7},{7,6},{8,9},{9,8},{10,11... | collective-permute-start | bytes 208904 | tf_op jit(solution)/shard_map/ppermute | solution.py:430
  17.6 4.8 %collective-permute-start.8 = (bf16[272,128]{1,0:T(8,128)(2,1)S(1)}, bf16[272,128]{1,0:T(8,128)(2,1)S(1)}, u32[]{:S(2)}, u32[]{:S(2)}) collective-permute-start(bf16[272,128]{1,0:T(8,128)(2,1)S(1)} %collective-permute-done.4.refs_3_), channel_id=1, source_target_pairs={{0,2},{1,3},{2,0},{3,1},{4,6},{5,7},{6,4},{7,5},{8,10},{9,11},{10,... | collective-permute-start | bytes 208904 | tf_op jit(solution)/shard_map/ppermute | solution.py:430
  21.7 1.8 %collective-permute-start.14 = (bf16[272,128]{1,0:T(8,128)(2,1)S(1)}, bf16[272,128]{1,0:T(8,128)(2,1)S(1)}, u32[]{:S(2)}, u32[]{:S(2)}) collective-permute-start(bf16[272,128]{1,0:T(8,128)(2,1)S(1)} %collective-permute-done.6.refs_5_), channel_id=1, source_target_pairs={{0,1},{1,0},{2,3},{3,2},{4,5},{5,4},{6,7},{7,6},{8,9},{9,8},{10,11... | collective-permute-start | bytes 208904 | tf_op jit(solution)/shard_map/ppermute | solution.py:430
  21.8 1.4 %collective-permute-start.15 = (bf16[272,128]{1,0:T(8,128)(2,1)S(1)}, bf16[272,128]{1,0:T(8,128)(2,1)S(1)}, u32[]{:S(2)}, u32[]{:S(2)}) collective-permute-start(bf16[272,128]{1,0:T(8,128)(2,1)S(1)} %collective-permute-done.7.refs_6_), channel_id=1, source_target_pairs={{0,1},{1,0},{2,3},{3,2},{4,5},{5,4},{6,7},{7,6},{8,9},{9,8},{10,11... | collective-permute-start | bytes 208904 | tf_op jit(solution)/shard_map/ppermute | solution.py:430
  22.3 1.3 %collective-permute-start.12 = (bf16[272,128]{1,0:T(8,128)(2,1)S(1)}, bf16[272,128]{1,0:T(8,128)(2,1)S(1)}, u32[]{:S(2)}, u32[]{:S(2)}) collective-permute-start(bf16[272,128]{1,0:T(8,128)(2,1)S(1)} %collective-permute-done.4.refs_3_), channel_id=1, source_target_pairs={{0,1},{1,0},{2,3},{3,2},{4,5},{5,4},{6,7},{7,6},{8,9},{9,8},{10,11... | collective-permute-start | bytes 208904 | tf_op jit(solution)/shard_map/ppermute | solution.py:430
  22.4 1.3 %collective-permute-start.16 = (bf16[272,128]{1,0:T(8,128)(2,1)S(1)}, bf16[272,128]{1,0:T(8,128)(2,1)S(1)}, u32[]{:S(2)}, u32[]{:S(2)}) collective-permute-start(bf16[272,128]{1,0:T(8,128)(2,1)S(1)} %collective-permute-done.8.refs_7_), channel_id=1, source_target_pairs={{0,1},{1,0},{2,3},{3,2},{4,5},{5,4},{6,7},{7,6},{8,9},{9,8},{10,11... | collective-permute-start | bytes 208904 | tf_op jit(solution)/shard_map/ppermute | solution.py:430

commit v6 on v5

--- a/solution.py
+++ b/solution.py
@@ -193,13 +193,17 @@
     for half, total in enumerate(totals):
         tab[t.total + half] = total
     tab[t.active] = 0
-    for s in range(IRREPS):
-
-        @pl.when((tab[t.cnt + s] > 0) & (tab[t.slot + s * MAXO] >= 0))
-        def _(s=s):
-            used = tab[t.active]
-            tab[t.active + 1 + used] = s
-            tab[t.active] = used + 1
+    for slots in range(MAXO, 0, -1):
+        for s in range(IRREPS):
+            fit = tab[t.slot + s * MAXO + slots - 1] >= 0
+            if slots < MAXO:
+                fit = fit & (tab[t.slot + s * MAXO + slots] < 0)
+
+            @pl.when((tab[t.cnt + s] > 0) & fit)
+            def _(s=s):
+                used = tab[t.active]
+                tab[t.active + 1 + used] = s
+                tab[t.active] = used + 1
     for fill in fills:
         fill.wait()
 

time: 28.9 us -> 28.6 us (0.990)
  transfers between devices with their start and end apart: 16 -> 16, of which waited for: 7 -> 6; matrix products, arithmetic and copies ran while one was open for 0% -> 0% of each run, Pallas kernels for 12% -> 12%
where the time goes in v6:
time: 28.6 us; the launch traced here: 28.4 us
  starting transfers between devices  15.9 us (56%)
  Pallas kernels  9.21 us (32%)
  waiting for transfers between devices  2.64 us (9%)
  between operations  0.71 us (2%)
    ppermute x15, starting transfers between devices, per_device(): parts = parts + [lax.ppermute(p, 'vir', pairs) for p in parts]  12.7 us
    ppermute x1, starting transfers between devices, across(): lax.ppermute(x, 'occ', [(i, (i + shift) % n_occ) for i in range(n_occ)])  3.2 us
    pallas_call x1, Pallas kernels, per_device(): pl.pallas_call(functools.partial(finish_kernel, t, chunks), out_shape=jax...  3.12 us
    pallas_call x1, Pallas kernels, per_device(): pl.pallas_call(functools.partial(plan_kernel, t), out_shape=(pltpu.HBM((o...  2.73 us
    pallas_call x1, Pallas kernels, per_device(): pl.pallas_call(functools.partial(pack_kernel, t, chunks), out_shape=tuple...  2.64 us
    ppermute x15, waiting for transfers between devices, per_device(): parts = parts + [lax.ppermute(p, 'vir', pairs) for p in parts]  2.6 us
    pallas_call x1, Pallas kernels, per_device(): pl.pallas_call(functools.partial(sort_kernel, tuple(masks)), out_shape=(p...  0.71 us
  transfers between devices with their start and end apart: 16, of which 6 were waited for; matrix products, arithmetic and copies ran while one was open for 0% of the time, Pallas kernels for 12%

profile of v6, /device:TPU:0, one launch (start us, length us, event | category | flops | bytes accessed | tf_op | source)
XLA Modules:
  0.0 28.4 jit_solution(2983760471193052351)
XLA Ops:
  0.0 2.6 %pack.1 = (bf16[27,128,128]{2,1,0:T(8,128)(2,1)S(1)}, bf16[4,128,128]{2,1,0:T(8,128)(2,1)S(1)}, bf16[9,128,128]{2,1,0:T(8,128)(2,1)S(1)}, bf16[272,128]{1,0:T(8,128)(2,1)S(1)}) custom-call(s32[16]{0:T(128)} %ksym.3, s32[20]{0:T(128)} %vsym.3, s32[6]{0:T(128)} %osym.3, bf16[1024,2560]{1,0:T(8,128)(2,1)} %v_ref.1, bf16[768,128]{1,0:T(8,128)(2,1)} %a_ref.1), custom_call_target="tpu_custom_call" | custom-call | tf_op jit(solution)/shard_map/pack/pallas_call | solution.py:389
  2.6 3.2 %collective-permute-start.17 = (bf16[27,128,128]{2,1,0:T(8,128)(2,1)S(1)}, bf16[27,128,128]{2,1,0:T(8,128)(2,1)S(1)}, u32[]{:S(2)}, u32[]{:S(2)}) collective-permute-start(bf16[27,128,128]{2,1,0:T(8,128)(2,1)S(1)} %get-tuple-element.45.refs_0_), channel_id=1, source_target_pairs={{0,16},{16,0},{1,17},{17,1},{2,18},{18,2},{3,19},{19,3},{4,20},{20... | collective-permute-start | bytes 2654216 | tf_op jit(solution)/shard_map/ppermute | solution.py:422
  5.8 1.3 %collective-permute-start.5 = (bf16[272,128]{1,0:T(8,128)(2,1)S(1)}, bf16[272,128]{1,0:T(8,128)(2,1)S(1)}, u32[]{:S(2)}, u32[]{:S(2)}) collective-permute-start(bf16[272,128]{1,0:T(8,128)(2,1)S(1)} %get-tuple-element.40.after.refs_0_), channel_id=1, source_target_pairs={{0,2},{1,3},{2,0},{3,1},{4,6},{5,7},{6,4},{7,5},{8,10},{9,11},{10,... | collective-permute-start | bytes 208904 | tf_op jit(solution)/shard_map/ppermute | solution.py:434
  7.1 2.5 %collective-permute-start.2 = (bf16[272,128]{1,0:T(8,128)(2,1)S(1)}, bf16[272,128]{1,0:T(8,128)(2,1)S(1)}, u32[]{:S(2)}, u32[]{:S(2)}) collective-permute-start(bf16[272,128]{1,0:T(8,128)(2,1)S(1)} %get-tuple-element.40.after.refs_0_), channel_id=1, source_target_pairs={{0,8},{1,9},{2,10},{3,11},{4,12},{5,13},{6,14},{7,15},{8,0},{9,1},... | collective-permute-start | bytes 208904 | tf_op jit(solution)/shard_map/ppermute | solution.py:434
  9.6 0.0 collective-permute-start.9
  9.6 1.7 %collective-permute-start.3 = (bf16[272,128]{1,0:T(8,128)(2,1)S(1)}, bf16[272,128]{1,0:T(8,128)(2,1)S(1)}, u32[]{:S(2)}, u32[]{:S(2)}) collective-permute-start(bf16[272,128]{1,0:T(8,128)(2,1)S(1)} %get-tuple-element.40.after.refs_0_), channel_id=1, source_target_pairs={{0,4},{1,5},{2,6},{3,7},{4,0},{5,1},{6,2},{7,3},{8,12},{9,13},{10,... | collective-permute-start | bytes 208904 | tf_op jit(solution)/shard_map/ppermute | solution.py:434
  11.4 0.0 collective-permute-done.5.refs_4_
  11.4 0.2 collective-permute-start.13
  11.6 1.2 %collective-permute-done.2.refs_1_ = bf16[272,128]{1,0:T(8,128)(2,1)S(1)} collective-permute-done((bf16[272,128]{1,0:T(8,128)(2,1)S(1)}, bf16[272,128]{1,0:T(8,128)(2,1)S(1)}, u32[]{:S(2)}, u32[]{:S(2)}) %collective-permute-start.2) | collective-permute-done | bytes 69664 | tf_op jit(solution)/shard_map/ppermute | solution.py:434
  12.8 0.3 %collective-permute-start.6 = (bf16[272,128]{1,0:T(8,128)(2,1)S(1)}, bf16[272,128]{1,0:T(8,128)(2,1)S(1)}, u32[]{:S(2)}, u32[]{:S(2)}) collective-permute-start(bf16[272,128]{1,0:T(8,128)(2,1)S(1)} %collective-permute-done.2.refs_1_), channel_id=1, source_target_pairs={{0,2},{1,3},{2,0},{3,1},{4,6},{5,7},{6,4},{7,5},{8,10},{9,11},{10,... | collective-permute-start | bytes 208904 | tf_op jit(solution)/shard_map/ppermute | solution.py:434
  13.1 0.0 collective-permute-done.9.refs_8_
  13.1 1.7 %collective-permute-start.4 = (bf16[272,128]{1,0:T(8,128)(2,1)S(1)}, bf16[272,128]{1,0:T(8,128)(2,1)S(1)}, u32[]{:S(2)}, u32[]{:S(2)}) collective-permute-start(bf16[272,128]{1,0:T(8,128)(2,1)S(1)} %collective-permute-done.2.refs_1_), channel_id=1, source_target_pairs={{0,4},{1,5},{2,6},{3,7},{4,0},{5,1},{6,2},{7,3},{8,12},{9,13},{10,... | collective-permute-start | bytes 208904 | tf_op jit(solution)/shard_map/ppermute | solution.py:434
  14.8 0.0 collective-permute-done.3.refs_2_
  14.8 0.0 collective-permute-start.11
  14.8 2.1 %collective-permute-start.7 = (bf16[272,128]{1,0:T(8,128)(2,1)S(1)}, bf16[272,128]{1,0:T(8,128)(2,1)S(1)}, u32[]{:S(2)}, u32[]{:S(2)}) collective-permute-start(bf16[272,128]{1,0:T(8,128)(2,1)S(1)} %collective-permute-done.3.refs_2_), channel_id=1, source_target_pairs={{0,2},{1,3},{2,0},{3,1},{4,6},{5,7},{6,4},{7,5},{8,10},{9,11},{10,... | collective-permute-start | bytes 208904 | tf_op jit(solution)/shard_map/ppermute | solution.py:434
  16.9 0.2 collective-permute-done.6.refs_5_
  17.1 0.3 %collective-permute-done.4.refs_3_ = bf16[272,128]{1,0:T(8,128)(2,1)S(1)} collective-permute-done((bf16[272,128]{1,0:T(8,128)(2,1)S(1)}, bf16[272,128]{1,0:T(8,128)(2,1)S(1)}, u32[]{:S(2)}, u32[]{:S(2)}) %collective-permute-start.4) | collective-permute-done | bytes 69664 | tf_op jit(solution)/shard_map/ppermute | solution.py:434
  17.4 1.7 %collective-permute-start.8 = (bf16[272,128]{1,0:T(8,128)(2,1)S(1)}, bf16[272,128]{1,0:T(8,128)(2,1)S(1)}, u32[]{:S(2)}, u32[]{:S(2)}) collective-permute-start(bf16[272,128]{1,0:T(8,128)(2,1)S(1)} %collective-permute-done.4.refs_3_), channel_id=1, source_target_pairs={{0,2},{1,3},{2,0},{3,1},{4,6},{5,7},{6,4},{7,5},{8,10},{9,11},{10,... | collective-permute-start | bytes 208904 | tf_op jit(solution)/shard_map/ppermute | solution.py:434
  19.1 2.7 %plan.1 = (bf16[768,2560]{1,0:T(8,128)(2,1)}, s32[259]{0:T(512)S(4)}, bf16[4,128,128]{2,1,0:T(8,128)(2,1)}, bf16[9,128,128]{2,1,0:T(8,128)(2,1)}) custom-call(s32[16]{0:T(128)} %ksym.3, s32[20]{0:T(128)} %vsym.3, s32[6]{0:T(128)} %osym.3, bf16[272,128]{1,0:T(8,128)(2,1)S(1)} %get-tuple-element.40.after.refs_0_), custom_call_target="tpu_custom_call" | custom-call | tf_op jit(solution)/shard_map/plan/pallas_call | solution.py:403
  21.9 0.0 collective-permute-done.11.refs_10_
  21.9 0.1 collective-permute-start.14
  22.0 0.0 collective-permute-done.7.refs_6_
  22.0 0.5 %collective-permute-start.15 = (bf16[272,128]{1,0:T(8,128)(2,1)S(1)}, bf16[272,128]{1,0:T(8,128)(2,1)S(1)}, u32[]{:S(2)}, u32[]{:S(2)}) collective-permute-start(bf16[272,128]{1,0:T(8,128)(2,1)S(1)} %collective-permute-done.7.refs_6_), channel_id=1, source_target_pairs={{0,1},{1,0},{2,3},{3,2},{4,5},{5,4},{6,7},{7,6},{8,9},{9,8},{10,11... | collective-permute-start | bytes 208904 | tf_op jit(solution)/shard_map/ppermute | solution.py:434
  22.5 0.1 collective-permute-start.12
  22.6 0.0 collective-permute-done.8.refs_7_
  22.6 0.4 %collective-permute-start.16 = (bf16[272,128]{1,0:T(8,128)(2,1)S(1)}, bf16[272,128]{1,0:T(8,128)(2,1)S(1)}, u32[]{:S(2)}, u32[]{:S(2)}) collective-permute-start(bf16[272,128]{1,0:T(8,128)(2,1)S(1)} %collective-permute-done.8.refs_7_), channel_id=1, source_target_pairs={{0,1},{1,0},{2,3},{3,2},{4,5},{5,4},{6,7},{7,6},{8,9},{9,8},{10,11... | collective-permute-start | bytes 208904 | tf_op jit(solution)/shard_map/ppermute | solution.py:434
  23.0 0.4 %collective-permute-done.15.refs_14_ = bf16[272,128]{1,0:T(8,128)(2,1)S(1)} collective-permute-done((bf16[272,128]{1,0:T(8,128)(2,1)S(1)}, bf16[272,128]{1,0:T(8,128)(2,1)S(1)}, u32[]{:S(2)}, u32[]{:S(2)}) %collective-permute-start.15) | collective-permute-done | bytes 69664 | tf_op jit(solution)/shard_map/ppermute | solution.py:434
  23.4 0.4 %collective-permute-done.12.refs_11_ = bf16[272,128]{1,0:T(8,128)(2,1)S(1)} collective-permute-done((bf16[272,128]{1,0:T(8,128)(2,1)S(1)}, bf16[272,128]{1,0:T(8,128)(2,1)S(1)}, u32[]{:S(2)}, u32[]{:S(2)}) %collective-permute-start.12) | collective-permute-done | bytes 69664 | tf_op jit(solution)/shard_map/ppermute | solution.py:434
  23.7 0.2 collective-permute-done.16.refs_15_
  23.9 0.7 %sort.1 = (bf16[16,256,128]{2,1,0:T(8,128)(2,1)S(1)}, s32[1]{0:T(128)}) custom-call(bf16[272,128]{1,0:T(8,128)(2,1)S(1)} %get-tuple-element.40.after.refs_0_, bf16[272,128]{1,0:T(8,128)(2,1)S(1)} %collective-permute-done.2.refs_1_, bf16[272,128]{1,0:T(8,128)(2,1)S(1)} %collective-permute-done.3.refs_2_, bf16[272,128]{1,0:T(8,128)(2,1)S(1)} %collective-permute-done.4.refs_3_, ...), custom_call_target="tpu_custom_call" | custom-call | tf_op jit(solution)/shard_map/sort/pallas_call | solution.py:449
  25.3 0.0 collective-permute-done.17.refs_1_
  25.3 3.1 %finish.1 = bf16[768,2560]{1,0:T(8,128)(2,1)} custom-call(s32[259]{0:T(512)S(4)} %get-tuple-element.41.tab, bf16[16,256,128]{2,1,0:T(8,128)(2,1)S(1)} %get-tuple-element.44.amp, bf16[27,128,128]{2,1,0:T(8,128)(2,1)S(1)} %get-tuple-element.45.refs_0_, bf16[27,128,128]{2,1,0:T(8,128)(2,1)S(1)} %collective-permute-done.17.refs_1_, ...), custom_call_target="tpu_custom_call", output_to_operand_aliasing={{}: (8, {})} | custom-call | tf_op jit(solution)/shard_map/finish/pallas_call | solution.py:478
  (5 shorter events, 0.0 us)
Async XLA Ops:
  2.6 22.7 %collective-permute-start.17 = (bf16[27,128,128]{2,1,0:T(8,128)(2,1)S(1)}, bf16[27,128,128]{2,1,0:T(8,128)(2,1)S(1)}, u32[]{:S(2)}, u32[]{:S(2)}) collective-permute-start(bf16[27,128,128]{2,1,0:T(8,128)(2,1)S(1)} %get-tuple-element.45.refs_0_), channel_id=1, source_target_pairs={{0,16},{16,0},{1,17},{17,1},{2,18},{18,2},{3,19},{19,3},{4,20},{20... | collective-permute-start | bytes 2654216 | tf_op jit(solution)/shard_map/ppermute | solution.py:422
  5.8 5.5 %collective-permute-start.5 = (bf16[272,128]{1,0:T(8,128)(2,1)S(1)}, bf16[272,128]{1,0:T(8,128)(2,1)S(1)}, u32[]{:S(2)}, u32[]{:S(2)}) collective-permute-start(bf16[272,128]{1,0:T(8,128)(2,1)S(1)} %get-tuple-element.40.after.refs_0_), channel_id=1, source_target_pairs={{0,2},{1,3},{2,0},{3,1},{4,6},{5,7},{6,4},{7,5},{8,10},{9,11},{10,... | collective-permute-start | bytes 208904 | tf_op jit(solution)/shard_map/ppermute | solution.py:434
  7.1 5.6 %collective-permute-start.2 = (bf16[272,128]{1,0:T(8,128)(2,1)S(1)}, bf16[272,128]{1,0:T(8,128)(2,1)S(1)}, u32[]{:S(2)}, u32[]{:S(2)}) collective-permute-start(bf16[272,128]{1,0:T(8,128)(2,1)S(1)} %get-tuple-element.40.after.refs_0_), channel_id=1, source_target_pairs={{0,8},{1,9},{2,10},{3,11},{4,12},{5,13},{6,14},{7,15},{8,0},{9,1},... | collective-permute-start | bytes 208904 | tf_op jit(solution)/shard_map/ppermute | solution.py:434
  9.6 3.5 %collective-permute-start.9 = (bf16[272,128]{1,0:T(8,128)(2,1)S(1)}, bf16[272,128]{1,0:T(8,128)(2,1)S(1)}, u32[]{:S(2)}, u32[]{:S(2)}) collective-permute-start(bf16[272,128]{1,0:T(8,128)(2,1)S(1)} %get-tuple-element.40.after.refs_0_), channel_id=1, source_target_pairs={{0,1},{1,0},{2,3},{3,2},{4,5},{5,4},{6,7},{7,6},{8,9},{9,8},{10,11... | collective-permute-start | bytes 208904 | tf_op jit(solution)/shard_map/ppermute | solution.py:434
  9.6 5.2 %collective-permute-start.3 = (bf16[272,128]{1,0:T(8,128)(2,1)S(1)}, bf16[272,128]{1,0:T(8,128)(2,1)S(1)}, u32[]{:S(2)}, u32[]{:S(2)}) collective-permute-start(bf16[272,128]{1,0:T(8,128)(2,1)S(1)} %get-tuple-element.40.after.refs_0_), channel_id=1, source_target_pairs={{0,4},{1,5},{2,6},{3,7},{4,0},{5,1},{6,2},{7,3},{8,12},{9,13},{10,... | collective-permute-start | bytes 208904 | tf_op jit(solution)/shard_map/ppermute | solution.py:434
  11.4 3.5 %collective-permute-start.13 = (bf16[272,128]{1,0:T(8,128)(2,1)S(1)}, bf16[272,128]{1,0:T(8,128)(2,1)S(1)}, u32[]{:S(2)}, u32[]{:S(2)}) collective-permute-start(bf16[272,128]{1,0:T(8,128)(2,1)S(1)} %collective-permute-done.5.refs_4_), channel_id=1, source_target_pairs={{0,1},{1,0},{2,3},{3,2},{4,5},{5,4},{6,7},{7,6},{8,9},{9,8},{10,11... | collective-permute-start | bytes 208904 | tf_op jit(solution)/shard_map/ppermute | solution.py:434
  12.8 4.3 %collective-permute-start.6 = (bf16[272,128]{1,0:T(8,128)(2,1)S(1)}, bf16[272,128]{1,0:T(8,128)(2,1)S(1)}, u32[]{:S(2)}, u32[]{:S(2)}) collective-permute-start(bf16[272,128]{1,0:T(8,128)(2,1)S(1)} %collective-permute-done.2.refs_1_), channel_id=1, source_target_pairs={{0,2},{1,3},{2,0},{3,1},{4,6},{5,7},{6,4},{7,5},{8,10},{9,11},{10,... | collective-permute-start | bytes 208904 | tf_op jit(solution)/shard_map/ppermute | solution.py:434
  13.1 4.3 %collective-permute-start.4 = (bf16[272,128]{1,0:T(8,128)(2,1)S(1)}, bf16[272,128]{1,0:T(8,128)(2,1)S(1)}, u32[]{:S(2)}, u32[]{:S(2)}) collective-permute-start(bf16[272,128]{1,0:T(8,128)(2,1)S(1)} %collective-permute-done.2.refs_1_), channel_id=1, source_target_pairs={{0,4},{1,5},{2,6},{3,7},{4,0},{5,1},{6,2},{7,3},{8,12},{9,13},{10,... | collective-permute-start | bytes 208904 | tf_op jit(solution)/shard_map/ppermute | solution.py:434
  14.8 7.0 %collective-permute-start.11 = (bf16[272,128]{1,0:T(8,128)(2,1)S(1)}, bf16[272,128]{1,0:T(8,128)(2,1)S(1)}, u32[]{:S(2)}, u32[]{:S(2)}) collective-permute-start(bf16[272,128]{1,0:T(8,128)(2,1)S(1)} %collective-permute-done.3.refs_2_), channel_id=1, source_target_pairs={{0,1},{1,0},{2,3},{3,2},{4,5},{5,4},{6,7},{7,6},{8,9},{9,8},{10,11... | collective-permute-start | bytes 208904 | tf_op jit(solution)/shard_map/ppermute | solution.py:434
  14.8 7.1 %collective-permute-start.7 = (bf16[272,128]{1,0:T(8,128)(2,1)S(1)}, bf16[272,128]{1,0:T(8,128)(2,1)S(1)}, u32[]{:S(2)}, u32[]{:S(2)}) collective-permute-start(bf16[272,128]{1,0:T(8,128)(2,1)S(1)} %collective-permute-done.3.refs_2_), channel_id=1, source_target_pairs={{0,2},{1,3},{2,0},{3,1},{4,6},{5,7},{6,4},{7,5},{8,10},{9,11},{10,... | collective-permute-start | bytes 208904 | tf_op jit(solution)/shard_map/ppermute | solution.py:434
  17.1 5.4 %collective-permute-start.10 = (bf16[272,128]{1,0:T(8,128)(2,1)S(1)}, bf16[272,128]{1,0:T(8,128)(2,1)S(1)}, u32[]{:S(2)}, u32[]{:S(2)}) collective-permute-start(bf16[272,128]{1,0:T(8,128)(2,1)S(1)} %collective-permute-done.2.refs_1_), channel_id=1, source_target_pairs={{0,1},{1,0},{2,3},{3,2},{4,5},{5,4},{6,7},{7,6},{8,9},{9,8},{10,11... | collective-permute-start | bytes 208904 | tf_op jit(solution)/shard_map/ppermute | solution.py:434
  17.4 5.1 %collective-permute-start.8 = (bf16[272,128]{1,0:T(8,128)(2,1)S(1)}, bf16[272,128]{1,0:T(8,128)(2,1)S(1)}, u32[]{:S(2)}, u32[]{:S(2)}) collective-permute-start(bf16[272,128]{1,0:T(8,128)(2,1)S(1)} %collective-permute-done.4.refs_3_), channel_id=1, source_target_pairs={{0,2},{1,3},{2,0},{3,1},{4,6},{5,7},{6,4},{7,5},{8,10},{9,11},{10,... | collective-permute-start | bytes 208904 | tf_op jit(solution)/shard_map/ppermute | solution.py:434
  21.9 1.8 %collective-permute-start.14 = (bf16[272,128]{1,0:T(8,128)(2,1)S(1)}, bf16[272,128]{1,0:T(8,128)(2,1)S(1)}, u32[]{:S(2)}, u32[]{:S(2)}) collective-permute-start(bf16[272,128]{1,0:T(8,128)(2,1)S(1)} %collective-permute-done.6.refs_5_), channel_id=1, source_target_pairs={{0,1},{1,0},{2,3},{3,2},{4,5},{5,4},{6,7},{7,6},{8,9},{9,8},{10,11... | collective-permute-start | bytes 208904 | tf_op jit(solution)/shard_map/ppermute | solution.py:434
  22.0 1.4 %collective-permute-start.15 = (bf16[272,128]{1,0:T(8,128)(2,1)S(1)}, bf16[272,128]{1,0:T(8,128)(2,1)S(1)}, u32[]{:S(2)}, u32[]{:S(2)}) collective-permute-start(bf16[272,128]{1,0:T(8,128)(2,1)S(1)} %collective-permute-done.7.refs_6_), channel_id=1, source_target_pairs={{0,1},{1,0},{2,3},{3,2},{4,5},{5,4},{6,7},{7,6},{8,9},{9,8},{10,11... | collective-permute-start | bytes 208904 | tf_op jit(solution)/shard_map/ppermute | solution.py:434
  22.5 1.3 %collective-permute-start.12 = (bf16[272,128]{1,0:T(8,128)(2,1)S(1)}, bf16[272,128]{1,0:T(8,128)(2,1)S(1)}, u32[]{:S(2)}, u32[]{:S(2)}) collective-permute-start(bf16[272,128]{1,0:T(8,128)(2,1)S(1)} %collective-permute-done.4.refs_3_), channel_id=1, source_target_pairs={{0,1},{1,0},{2,3},{3,2},{4,5},{5,4},{6,7},{7,6},{8,9},{9,8},{10,11... | collective-permute-start | bytes 208904 | tf_op jit(solution)/shard_map/ppermute | solution.py:434
  22.6 1.3 %collective-permute-start.16 = (bf16[272,128]{1,0:T(8,128)(2,1)S(1)}, bf16[272,128]{1,0:T(8,128)(2,1)S(1)}, u32[]{:S(2)}, u32[]{:S(2)}) collective-permute-start(bf16[272,128]{1,0:T(8,128)(2,1)S(1)} %collective-permute-done.8.refs_7_), channel_id=1, source_target_pairs={{0,1},{1,0},{2,3},{3,2},{4,5},{5,4},{6,7},{7,6},{8,9},{9,8},{10,11... | collective-permute-start | bytes 208904 | tf_op jit(solution)/shard_map/ppermute | solution.py:434

commit v7 on v6

--- a/solution.py
+++ b/solution.py
@@ -380,7 +380,7 @@
     cols = vblocks * BLK
     t = Table(n_occ, kblocks, vblocks)
     cap = t.own * MAXB
-    first_cap = (cap * 27 + 39) // 40
+    first_cap = (cap * 28 + 39) // 40
     more_cap = (cap - first_cap) // 3
     chunks = tuple(c for c in (first_cap, more_cap, cap - first_cap - more_cap) if c)
     rows = MAXO * BLK + INFO

time: 28.6 us -> 29.7 us (1.038); the launches traced: 28.4 us -> 29.2 us
  waiting for transfers between devices: 2.64 us -> 3.14 us
    ppermute x1, waiting for transfers between devices: 0.05 us -> 0.79 us  [across(): lax.ppermute(x, 'occ', [(i, (i + shift) % n_occ) for i in range(n_occ)])]
  transfers between devices with their start and end apart: 16 -> 16, of which waited for: 6 -> 7; matrix products, arithmetic and copies ran while one was open for 0% -> 0% of each run, Pallas kernels for 12% -> 12%
where the time goes in v7:
time: 29.7 us; the launch traced here: 29.2 us
  starting transfers between devices  15.9 us (54%)
  Pallas kernels  9.49 us (32%)
  waiting for transfers between devices  3.14 us (11%)
  between operations  0.71 us (2%)
    ppermute x15, starting transfers between devices, per_device(): parts = parts + [lax.ppermute(p, 'vir', pairs) for p in parts]  12.8 us
    pallas_call x1, Pallas kernels, per_device(): pl.pallas_call(functools.partial(finish_kernel, t, chunks), out_shape=jax...  3.28 us
    ppermute x1, starting transfers between devices, across(): lax.ppermute(x, 'occ', [(i, (i + shift) % n_occ) for i in range(n_occ)])  3.09 us
    pallas_call x1, Pallas kernels, per_device(): pl.pallas_call(functools.partial(pack_kernel, t, chunks), out_shape=tuple...  2.76 us
    pallas_call x1, Pallas kernels, per_device(): pl.pallas_call(functools.partial(plan_kernel, t), out_shape=(pltpu.HBM((o...  2.73 us
    ppermute x15, waiting for transfers between devices, per_device(): parts = parts + [lax.ppermute(p, 'vir', pairs) for p in parts]  2.35 us
    ppermute x1, waiting for transfers between devices, across(): lax.ppermute(x, 'occ', [(i, (i + shift) % n_occ) for i in range(n_occ)])  0.79 us
    pallas_call x1, Pallas kernels, per_device(): pl.pallas_call(functools.partial(sort_kernel, tuple(masks)), out_shape=(p...  0.71 us
  transfers between devices with their start and end apart: 16, of which 7 were waited for; matrix products, arithmetic and copies ran while one was open for 0% of the time, Pallas kernels for 12%

profile of v7, /device:TPU:0, one launch (start us, length us, event | category | flops | bytes accessed | tf_op | source)
XLA Modules:
  0.0 29.2 jit_solution(1532921510360021040)
XLA Ops:
  0.0 2.8 %pack.1 = (bf16[28,128,128]{2,1,0:T(8,128)(2,1)S(1)}, bf16[4,128,128]{2,1,0:T(8,128)(2,1)S(1)}, bf16[8,128,128]{2,1,0:T(8,128)(2,1)S(1)}, bf16[272,128]{1,0:T(8,128)(2,1)S(1)}) custom-call(s32[16]{0:T(128)} %ksym.3, s32[20]{0:T(128)} %vsym.3, s32[6]{0:T(128)} %osym.3, bf16[1024,2560]{1,0:T(8,128)(2,1)} %v_ref.1, bf16[768,128]{1,0:T(8,128)(2,1)} %a_ref.1), custom_call_target="tpu_custom_call" | custom-call | tf_op jit(solution)/shard_map/pack/pallas_call | solution.py:389
  2.8 3.1 %collective-permute-start.17 = (bf16[28,128,128]{2,1,0:T(8,128)(2,1)S(1)}, bf16[28,128,128]{2,1,0:T(8,128)(2,1)S(1)}, u32[]{:S(2)}, u32[]{:S(2)}) collective-permute-start(bf16[28,128,128]{2,1,0:T(8,128)(2,1)S(1)} %get-tuple-element.45.refs_0_), channel_id=1, source_target_pairs={{0,16},{16,0},{1,17},{17,1},{2,18},{18,2},{3,19},{19,3},{4,20},{20... | collective-permute-start | bytes 2752520 | tf_op jit(solution)/shard_map/ppermute | solution.py:422
  5.9 1.4 %collective-permute-start.5 = (bf16[272,128]{1,0:T(8,128)(2,1)S(1)}, bf16[272,128]{1,0:T(8,128)(2,1)S(1)}, u32[]{:S(2)}, u32[]{:S(2)}) collective-permute-start(bf16[272,128]{1,0:T(8,128)(2,1)S(1)} %get-tuple-element.40.after.refs_0_), channel_id=1, source_target_pairs={{0,2},{1,3},{2,0},{3,1},{4,6},{5,7},{6,4},{7,5},{8,10},{9,11},{10,... | collective-permute-start | bytes 208904 | tf_op jit(solution)/shard_map/ppermute | solution.py:434
  7.3 2.6 %collective-permute-start.2 = (bf16[272,128]{1,0:T(8,128)(2,1)S(1)}, bf16[272,128]{1,0:T(8,128)(2,1)S(1)}, u32[]{:S(2)}, u32[]{:S(2)}) collective-permute-start(bf16[272,128]{1,0:T(8,128)(2,1)S(1)} %get-tuple-element.40.after.refs_0_), channel_id=1, source_target_pairs={{0,8},{1,9},{2,10},{3,11},{4,12},{5,13},{6,14},{7,15},{8,0},{9,1},... | collective-permute-start | bytes 208904 | tf_op jit(solution)/shard_map/ppermute | solution.py:434
  9.9 1.6 %collective-permute-start.3 = (bf16[272,128]{1,0:T(8,128)(2,1)S(1)}, bf16[272,128]{1,0:T(8,128)(2,1)S(1)}, u32[]{:S(2)}, u32[]{:S(2)}) collective-permute-start(bf16[272,128]{1,0:T(8,128)(2,1)S(1)} %get-tuple-element.40.after.refs_0_), channel_id=1, source_target_pairs={{0,4},{1,5},{2,6},{3,7},{4,0},{5,1},{6,2},{7,3},{8,12},{9,13},{10,... | collective-permute-start | bytes 208904 | tf_op jit(solution)/shard_map/ppermute | solution.py:434
  11.5 0.0 collective-permute-done.5.refs_4_
  11.5 0.2 collective-permute-start.13
  11.7 0.9 %collective-permute-done.2.refs_1_ = bf16[272,128]{1,0:T(8,128)(2,1)S(1)} collective-permute-done((bf16[272,128]{1,0:T(8,128)(2,1)S(1)}, bf16[272,128]{1,0:T(8,128)(2,1)S(1)}, u32[]{:S(2)}, u32[]{:S(2)}) %collective-permute-start.2) | collective-permute-done | bytes 69664 | tf_op jit(solution)/shard_map/ppermute | solution.py:434
  12.6 0.5 %collective-permute-start.6 = (bf16[272,128]{1,0:T(8,128)(2,1)S(1)}, bf16[272,128]{1,0:T(8,128)(2,1)S(1)}, u32[]{:S(2)}, u32[]{:S(2)}) collective-permute-start(bf16[272,128]{1,0:T(8,128)(2,1)S(1)} %collective-permute-done.2.refs_1_), channel_id=1, source_target_pairs={{0,2},{1,3},{2,0},{3,1},{4,6},{5,7},{6,4},{7,5},{8,10},{9,11},{10,... | collective-permute-start | bytes 208904 | tf_op jit(solution)/shard_map/ppermute | solution.py:434
  13.1 1.9 %collective-permute-start.4 = (bf16[272,128]{1,0:T(8,128)(2,1)S(1)}, bf16[272,128]{1,0:T(8,128)(2,1)S(1)}, u32[]{:S(2)}, u32[]{:S(2)}) collective-permute-start(bf16[272,128]{1,0:T(8,128)(2,1)S(1)} %collective-permute-done.2.refs_1_), channel_id=1, source_target_pairs={{0,4},{1,5},{2,6},{3,7},{4,0},{5,1},{6,2},{7,3},{8,12},{9,13},{10,... | collective-permute-start | bytes 208904 | tf_op jit(solution)/shard_map/ppermute | solution.py:434
  15.0 0.0 collective-permute-done.3.refs_2_
  15.0 0.0 collective-permute-start.11
  15.0 0.0 collective-permute-done.13.refs_12_
  15.0 1.8 %collective-permute-start.7 = (bf16[272,128]{1,0:T(8,128)(2,1)S(1)}, bf16[272,128]{1,0:T(8,128)(2,1)S(1)}, u32[]{:S(2)}, u32[]{:S(2)}) collective-permute-start(bf16[272,128]{1,0:T(8,128)(2,1)S(1)} %collective-permute-done.3.refs_2_), channel_id=1, source_target_pairs={{0,2},{1,3},{2,0},{3,1},{4,6},{5,7},{6,4},{7,5},{8,10},{9,11},{10,... | collective-permute-start | bytes 208904 | tf_op jit(solution)/shard_map/ppermute | solution.py:434
  16.8 0.1 collective-permute-done.6.refs_5_
  16.9 0.1 collective-permute-start.10
  17.0 0.5 %collective-permute-done.4.refs_3_ = bf16[272,128]{1,0:T(8,128)(2,1)S(1)} collective-permute-done((bf16[272,128]{1,0:T(8,128)(2,1)S(1)}, bf16[272,128]{1,0:T(8,128)(2,1)S(1)}, u32[]{:S(2)}, u32[]{:S(2)}) %collective-permute-start.4) | collective-permute-done | bytes 69664 | tf_op jit(solution)/shard_map/ppermute | solution.py:434
  17.4 1.6 %collective-permute-start.8 = (bf16[272,128]{1,0:T(8,128)(2,1)S(1)}, bf16[272,128]{1,0:T(8,128)(2,1)S(1)}, u32[]{:S(2)}, u32[]{:S(2)}) collective-permute-start(bf16[272,128]{1,0:T(8,128)(2,1)S(1)} %collective-permute-done.4.refs_3_), channel_id=1, source_target_pairs={{0,2},{1,3},{2,0},{3,1},{4,6},{5,7},{6,4},{7,5},{8,10},{9,11},{10,... | collective-permute-start | bytes 208904 | tf_op jit(solution)/shard_map/ppermute | solution.py:434
  19.0 2.7 %plan.1 = (bf16[768,2560]{1,0:T(8,128)(2,1)}, s32[259]{0:T(512)S(4)}, bf16[4,128,128]{2,1,0:T(8,128)(2,1)}, bf16[8,128,128]{2,1,0:T(8,128)(2,1)}) custom-call(s32[16]{0:T(128)} %ksym.3, s32[20]{0:T(128)} %vsym.3, s32[6]{0:T(128)} %osym.3, bf16[272,128]{1,0:T(8,128)(2,1)S(1)} %get-tuple-element.40.after.refs_0_), custom_call_target="tpu_custom_call" | custom-call | tf_op jit(solution)/shard_map/plan/pallas_call | solution.py:403
  21.7 0.0 collective-permute-done.11.refs_10_
  21.8 0.1 collective-permute-start.14
  21.8 0.0 collective-permute-done.7.refs_6_
  21.8 0.5 %collective-permute-start.15 = (bf16[272,128]{1,0:T(8,128)(2,1)S(1)}, bf16[272,128]{1,0:T(8,128)(2,1)S(1)}, u32[]{:S(2)}, u32[]{:S(2)}) collective-permute-start(bf16[272,128]{1,0:T(8,128)(2,1)S(1)} %collective-permute-done.7.refs_6_), channel_id=1, source_target_pairs={{0,1},{1,0},{2,3},{3,2},{4,5},{5,4},{6,7},{7,6},{8,9},{9,8},{10,11... | collective-permute-start | bytes 208904 | tf_op jit(solution)/shard_map/ppermute | solution.py:434
  22.3 0.1 collective-permute-start.12
  22.4 0.0 collective-permute-done.8.refs_7_
  22.4 0.4 %collective-permute-start.16 = (bf16[272,128]{1,0:T(8,128)(2,1)S(1)}, bf16[272,128]{1,0:T(8,128)(2,1)S(1)}, u32[]{:S(2)}, u32[]{:S(2)}) collective-permute-start(bf16[272,128]{1,0:T(8,128)(2,1)S(1)} %collective-permute-done.8.refs_7_), channel_id=1, source_target_pairs={{0,1},{1,0},{2,3},{3,2},{4,5},{5,4},{6,7},{7,6},{8,9},{9,8},{10,11... | collective-permute-start | bytes 208904 | tf_op jit(solution)/shard_map/ppermute | solution.py:434
  22.9 0.4 %collective-permute-done.15.refs_14_ = bf16[272,128]{1,0:T(8,128)(2,1)S(1)} collective-permute-done((bf16[272,128]{1,0:T(8,128)(2,1)S(1)}, bf16[272,128]{1,0:T(8,128)(2,1)S(1)}, u32[]{:S(2)}, u32[]{:S(2)}) %collective-permute-start.15) | collective-permute-done | bytes 69664 | tf_op jit(solution)/shard_map/ppermute | solution.py:434
  23.2 0.4 %collective-permute-done.12.refs_11_ = bf16[272,128]{1,0:T(8,128)(2,1)S(1)} collective-permute-done((bf16[272,128]{1,0:T(8,128)(2,1)S(1)}, bf16[272,128]{1,0:T(8,128)(2,1)S(1)}, u32[]{:S(2)}, u32[]{:S(2)}) %collective-permute-start.12) | collective-permute-done | bytes 69664 | tf_op jit(solution)/shard_map/ppermute | solution.py:434
  23.6 0.2 collective-permute-done.16.refs_15_
  23.8 0.7 %sort.1 = (bf16[16,256,128]{2,1,0:T(8,128)(2,1)S(1)}, s32[1]{0:T(128)}) custom-call(bf16[272,128]{1,0:T(8,128)(2,1)S(1)} %get-tuple-element.40.after.refs_0_, bf16[272,128]{1,0:T(8,128)(2,1)S(1)} %collective-permute-done.2.refs_1_, bf16[272,128]{1,0:T(8,128)(2,1)S(1)} %collective-permute-done.3.refs_2_, bf16[272,128]{1,0:T(8,128)(2,1)S(1)} %collective-permute-done.4.refs_3_, ...), custom_call_target="tpu_custom_call" | custom-call | tf_op jit(solution)/shard_map/sort/pallas_call | solution.py:449
  25.1 0.8 %collective-permute-done.17.refs_1_ = bf16[28,128,128]{2,1,0:T(8,128)(2,1)S(1)} collective-permute-done((bf16[28,128,128]{2,1,0:T(8,128)(2,1)S(1)}, bf16[28,128,128]{2,1,0:T(8,128)(2,1)S(1)}, u32[]{:S(2)}, u32[]{:S(2)}) %collective-permute-start.17) | collective-permute-done | bytes 917536 | tf_op jit(solution)/shard_map/ppermute | solution.py:422
  25.9 3.3 %finish.1 = bf16[768,2560]{1,0:T(8,128)(2,1)} custom-call(s32[259]{0:T(512)S(4)} %get-tuple-element.41.tab, bf16[16,256,128]{2,1,0:T(8,128)(2,1)S(1)} %get-tuple-element.44.amp, bf16[28,128,128]{2,1,0:T(8,128)(2,1)S(1)} %get-tuple-element.45.refs_0_, bf16[28,128,128]{2,1,0:T(8,128)(2,1)S(1)} %collective-permute-done.17.refs_1_, ...), custom_call_target="tpu_custom_call", output_to_operand_aliasing={{}: (8, {})} | custom-call | tf_op jit(solution)/shard_map/finish/pallas_call | solution.py:478
  (5 shorter events, 0.0 us)
Async XLA Ops:
  2.8 23.1 %collective-permute-start.17 = (bf16[28,128,128]{2,1,0:T(8,128)(2,1)S(1)}, bf16[28,128,128]{2,1,0:T(8,128)(2,1)S(1)}, u32[]{:S(2)}, u32[]{:S(2)}) collective-permute-start(bf16[28,128,128]{2,1,0:T(8,128)(2,1)S(1)} %get-tuple-element.45.refs_0_), channel_id=1, source_target_pairs={{0,16},{16,0},{1,17},{17,1},{2,18},{18,2},{3,19},{19,3},{4,20},{20... | collective-permute-start | bytes 2752520 | tf_op jit(solution)/shard_map/ppermute | solution.py:422
  5.9 5.6 %collective-permute-start.5 = (bf16[272,128]{1,0:T(8,128)(2,1)S(1)}, bf16[272,128]{1,0:T(8,128)(2,1)S(1)}, u32[]{:S(2)}, u32[]{:S(2)}) collective-permute-start(bf16[272,128]{1,0:T(8,128)(2,1)S(1)} %get-tuple-element.40.after.refs_0_), channel_id=1, source_target_pairs={{0,2},{1,3},{2,0},{3,1},{4,6},{5,7},{6,4},{7,5},{8,10},{9,11},{10,... | collective-permute-start | bytes 208904 | tf_op jit(solution)/shard_map/ppermute | solution.py:434
  7.3 5.3 %collective-permute-start.2 = (bf16[272,128]{1,0:T(8,128)(2,1)S(1)}, bf16[272,128]{1,0:T(8,128)(2,1)S(1)}, u32[]{:S(2)}, u32[]{:S(2)}) collective-permute-start(bf16[272,128]{1,0:T(8,128)(2,1)S(1)} %get-tuple-element.40.after.refs_0_), channel_id=1, source_target_pairs={{0,8},{1,9},{2,10},{3,11},{4,12},{5,13},{6,14},{7,15},{8,0},{9,1},... | collective-permute-start | bytes 208904 | tf_op jit(solution)/shard_map/ppermute | solution.py:434
  9.9 3.2 %collective-permute-start.9 = (bf16[272,128]{1,0:T(8,128)(2,1)S(1)}, bf16[272,128]{1,0:T(8,128)(2,1)S(1)}, u32[]{:S(2)}, u32[]{:S(2)}) collective-permute-start(bf16[272,128]{1,0:T(8,128)(2,1)S(1)} %get-tuple-element.40.after.refs_0_), channel_id=1, source_target_pairs={{0,1},{1,0},{2,3},{3,2},{4,5},{5,4},{6,7},{7,6},{8,9},{9,8},{10,11... | collective-permute-start | bytes 208904 | tf_op jit(solution)/shard_map/ppermute | solution.py:434
  9.9 5.1 %collective-permute-start.3 = (bf16[272,128]{1,0:T(8,128)(2,1)S(1)}, bf16[272,128]{1,0:T(8,128)(2,1)S(1)}, u32[]{:S(2)}, u32[]{:S(2)}) collective-permute-start(bf16[272,128]{1,0:T(8,128)(2,1)S(1)} %get-tuple-element.40.after.refs_0_), channel_id=1, source_target_pairs={{0,4},{1,5},{2,6},{3,7},{4,0},{5,1},{6,2},{7,3},{8,12},{9,13},{10,... | collective-permute-start | bytes 208904 | tf_op jit(solution)/shard_map/ppermute | solution.py:434
  11.5 3.5 %collective-permute-start.13 = (bf16[272,128]{1,0:T(8,128)(2,1)S(1)}, bf16[272,128]{1,0:T(8,128)(2,1)S(1)}, u32[]{:S(2)}, u32[]{:S(2)}) collective-permute-start(bf16[272,128]{1,0:T(8,128)(2,1)S(1)} %collective-permute-done.5.refs_4_), channel_id=1, source_target_pairs={{0,1},{1,0},{2,3},{3,2},{4,5},{5,4},{6,7},{7,6},{8,9},{9,8},{10,11... | collective-permute-start | bytes 208904 | tf_op jit(solution)/shard_map/ppermute | solution.py:434
  12.6 4.3 %collective-permute-start.6 = (bf16[272,128]{1,0:T(8,128)(2,1)S(1)}, bf16[272,128]{1,0:T(8,128)(2,1)S(1)}, u32[]{:S(2)}, u32[]{:S(2)}) collective-permute-start(bf16[272,128]{1,0:T(8,128)(2,1)S(1)} %collective-permute-done.2.refs_1_), channel_id=1, source_target_pairs={{0,2},{1,3},{2,0},{3,1},{4,6},{5,7},{6,4},{7,5},{8,10},{9,11},{10,... | collective-permute-start | bytes 208904 | tf_op jit(solution)/shard_map/ppermute | solution.py:434
  13.1 4.3 %collective-permute-start.4 = (bf16[272,128]{1,0:T(8,128)(2,1)S(1)}, bf16[272,128]{1,0:T(8,128)(2,1)S(1)}, u32[]{:S(2)}, u32[]{:S(2)}) collective-permute-start(bf16[272,128]{1,0:T(8,128)(2,1)S(1)} %collective-permute-done.2.refs_1_), channel_id=1, source_target_pairs={{0,4},{1,5},{2,6},{3,7},{4,0},{5,1},{6,2},{7,3},{8,12},{9,13},{10,... | collective-permute-start | bytes 208904 | tf_op jit(solution)/shard_map/ppermute | solution.py:434
  15.0 6.8 %collective-permute-start.11 = (bf16[272,128]{1,0:T(8,128)(2,1)S(1)}, bf16[272,128]{1,0:T(8,128)(2,1)S(1)}, u32[]{:S(2)}, u32[]{:S(2)}) collective-permute-start(bf16[272,128]{1,0:T(8,128)(2,1)S(1)} %collective-permute-done.3.refs_2_), channel_id=1, source_target_pairs={{0,1},{1,0},{2,3},{3,2},{4,5},{5,4},{6,7},{7,6},{8,9},{9,8},{10,11... | collective-permute-start | bytes 208904 | tf_op jit(solution)/shard_map/ppermute | solution.py:434
  15.0 6.8 %collective-permute-start.7 = (bf16[272,128]{1,0:T(8,128)(2,1)S(1)}, bf16[272,128]{1,0:T(8,128)(2,1)S(1)}, u32[]{:S(2)}, u32[]{:S(2)}) collective-permute-start(bf16[272,128]{1,0:T(8,128)(2,1)S(1)} %collective-permute-done.3.refs_2_), channel_id=1, source_target_pairs={{0,2},{1,3},{2,0},{3,1},{4,6},{5,7},{6,4},{7,5},{8,10},{9,11},{10,... | collective-permute-start | bytes 208904 | tf_op jit(solution)/shard_map/ppermute | solution.py:434
  16.9 5.5 %collective-permute-start.10 = (bf16[272,128]{1,0:T(8,128)(2,1)S(1)}, bf16[272,128]{1,0:T(8,128)(2,1)S(1)}, u32[]{:S(2)}, u32[]{:S(2)}) collective-permute-start(bf16[272,128]{1,0:T(8,128)(2,1)S(1)} %collective-permute-done.2.refs_1_), channel_id=1, source_target_pairs={{0,1},{1,0},{2,3},{3,2},{4,5},{5,4},{6,7},{7,6},{8,9},{9,8},{10,11... | collective-permute-start | bytes 208904 | tf_op jit(solution)/shard_map/ppermute | solution.py:434
  17.4 5.0 %collective-permute-start.8 = (bf16[272,128]{1,0:T(8,128)(2,1)S(1)}, bf16[272,128]{1,0:T(8,128)(2,1)S(1)}, u32[]{:S(2)}, u32[]{:S(2)}) collective-permute-start(bf16[272,128]{1,0:T(8,128)(2,1)S(1)} %collective-permute-done.4.refs_3_), channel_id=1, source_target_pairs={{0,2},{1,3},{2,0},{3,1},{4,6},{5,7},{6,4},{7,5},{8,10},{9,11},{10,... | collective-permute-start | bytes 208904 | tf_op jit(solution)/shard_map/ppermute | solution.py:434
  21.8 1.8 %collective-permute-start.14 = (bf16[272,128]{1,0:T(8,128)(2,1)S(1)}, bf16[272,128]{1,0:T(8,128)(2,1)S(1)}, u32[]{:S(2)}, u32[]{:S(2)}) collective-permute-start(bf16[272,128]{1,0:T(8,128)(2,1)S(1)} %collective-permute-done.6.refs_5_), channel_id=1, source_target_pairs={{0,1},{1,0},{2,3},{3,2},{4,5},{5,4},{6,7},{7,6},{8,9},{9,8},{10,11... | collective-permute-start | bytes 208904 | tf_op jit(solution)/shard_map/ppermute | solution.py:434
  21.8 1.4 %collective-permute-start.15 = (bf16[272,128]{1,0:T(8,128)(2,1)S(1)}, bf16[272,128]{1,0:T(8,128)(2,1)S(1)}, u32[]{:S(2)}, u32[]{:S(2)}) collective-permute-start(bf16[272,128]{1,0:T(8,128)(2,1)S(1)} %collective-permute-done.7.refs_6_), channel_id=1, source_target_pairs={{0,1},{1,0},{2,3},{3,2},{4,5},{5,4},{6,7},{7,6},{8,9},{9,8},{10,11... | collective-permute-start | bytes 208904 | tf_op jit(solution)/shard_map/ppermute | solution.py:434
  22.3 1.3 %collective-permute-start.12 = (bf16[272,128]{1,0:T(8,128)(2,1)S(1)}, bf16[272,128]{1,0:T(8,128)(2,1)S(1)}, u32[]{:S(2)}, u32[]{:S(2)}) collective-permute-start(bf16[272,128]{1,0:T(8,128)(2,1)S(1)} %collective-permute-done.4.refs_3_), channel_id=1, source_target_pairs={{0,1},{1,0},{2,3},{3,2},{4,5},{5,4},{6,7},{7,6},{8,9},{9,8},{10,11... | collective-permute-start | bytes 208904 | tf_op jit(solution)/shard_map/ppermute | solution.py:434
  22.4 1.3 %collective-permute-start.16 = (bf16[272,128]{1,0:T(8,128)(2,1)S(1)}, bf16[272,128]{1,0:T(8,128)(2,1)S(1)}, u32[]{:S(2)}, u32[]{:S(2)}) collective-permute-start(bf16[272,128]{1,0:T(8,128)(2,1)S(1)} %collective-permute-done.8.refs_7_), channel_id=1, source_target_pairs={{0,1},{1,0},{2,3},{3,2},{4,5},{5,4},{6,7},{7,6},{8,9},{9,8},{10,11... | collective-permute-start | bytes 208904 | tf_op jit(solution)/shard_map/ppermute | solution.py:434
